TPU v7x, 128 devices: a whole 4x4x4 slice. The times are simulated.
128 devices in a mesh: gx: 16 (over y, z_lo, core), gy: 8 (over x, z_hi).
Axes of the slice: x: 4, y: 4, z: 4 (z_hi: 2, z_lo: 2; z = z_hi * 2 + z_lo), core: 2. Of those that a mesh axis runs over, the one named last changes fastest.
Arguments:
- populations: float32 [19, 128, 32768], P(None, 'gx', 'gy'), may hold values from 0.016 to 0.467, as said below
- h_axial: float32 [128, 32768], P('gx', 'gy'), may hold values from 1 to 3
- h_transverse: float32 [2, 128, 32768], P(None, 'gx', 'gy'), may hold values from -4 to 4
Outputs:
- populations_next: float32 [19, 128, 32768], P(None, 'gx', 'gy')
- demag_field: float32 [3, 128, 32768], P(None, 'gx', 'gy')
Inputs may be any that keep to these rules, and one draw needn't show every extreme that they name: `populations`: each population lies between 0.6 and 1.4 times its lattice weight.
All inputs are finite; a program needn't handle non-finite values.
Results may differ from a plain program's by a relative error of at most 0.000078.
Values sent between devices are 32-bit elements; how exact they have to be, the bound alone decides.
No kernel may reach another device: no remote copies, remote signals or barrier semaphores. Data moves between devices by JAX's collectives and lax.ppermute only.
A program may use at most 128 MiB of HBM per device.

v0:
```python
import jax
import jax.numpy as jnp
from jax import lax
from jax.sharding import PartitionSpec as P

NZ = 64


VELOCITIES = (
    (0, 0, 0),
    (1, 0, 0),
    (-1, 0, 0),
    (0, 1, 0),
    (0, -1, 0),
    (0, 0, 1),
    (0, 0, -1),
    (1, 1, 0),
    (-1, -1, 0),
    (1, -1, 0),
    (-1, 1, 0),
    (1, 0, 1),
    (-1, 0, -1),
    (1, 0, -1),
    (-1, 0, 1),
    (0, 1, 1),
    (0, -1, -1),
    (0, 1, -1),
    (0, -1, 1),
)
WEIGHTS = (1.0 / 3.0,) + (1.0 / 18.0,) * 6 + (1.0 / 36.0,) * 12
LANGEVIN_SCALE = 1.5
SATURATION = 1.0
KELVIN_COEF = 0.05
RELAX_TIME = 0.6
HIGHEST = lax.Precision.HIGHEST


def with_halo(shard, sides, width):
    for axis, dim in sides:
        size, length = (lax.axis_size(axis), shard.shape[dim])
        up = [(i, (i + 1) % size) for i in range(size)]
        down = [(j, i) for i, j in up]
        last = lax.slice_in_dim(shard, length - width, length, axis=dim)
        leading = lax.slice_in_dim(shard, 0, width, axis=dim)
        before = lax.ppermute(last, axis, up)
        after = lax.ppermute(leading, axis, down)
        shard = jnp.concatenate([before, shard, after], axis=dim)
    return shard


def langevin(applied):
    magnitude = jnp.sqrt(jnp.sum(applied * applied, axis=0))
    argument = LANGEVIN_SCALE * magnitude
    return SATURATION * (1.0 / jnp.tanh(argument) - 1.0 / argument) * applied / magnitude


def wavenumber(indices, count, dtype):
    return 2.0 * jnp.sin(jnp.pi * indices.astype(dtype) / count)


def demag_kernel(comp_x, comp_y, comp_z, wave_x, wave_y, wave_z, anchor):
    squared = wave_x * wave_x + wave_y * wave_y + wave_z * wave_z
    factor = jnp.where(anchor, 0.0, -1.0 / jnp.where(anchor, 1.0, squared))
    along = (wave_x * comp_x + wave_y * comp_y + wave_z * comp_z) * factor
    return (wave_x * along, wave_y * along, wave_z * along)


def kelvin(magnet, wide):
    centre = wide[:, 1:-1, 1:-1]
    grad_x = 0.5 * (wide[:, 2:, 1:-1] - wide[:, :-2, 1:-1])
    grad_y = 0.5 * (wide[:, 1:-1, 2:] - wide[:, 1:-1, :-2])
    grad_z = 0.5 * (jnp.roll(centre, -1, axis=3) - jnp.roll(centre, 1, axis=3))
    return KELVIN_COEF * (magnet[0:1] * grad_x + magnet[1:2] * grad_y + magnet[2:3] * grad_z)


def moments(popul, body_force):
    density = jnp.sum(popul, axis=0)
    momentum = [0.5 * body_force[0], 0.5 * body_force[1], 0.5 * body_force[2]]
    for number in range(19):
        for column in range(3):
            if VELOCITIES[number][column] == 1:
                momentum[column] = momentum[column] + popul[number]
            elif VELOCITIES[number][column] == -1:
                momentum[column] = momentum[column] - popul[number]
    return (density, (momentum[0] / density, momentum[1] / density, momentum[2] / density))


def relax(popul_one, density, velocity, body_force, lattice, weight):
    vel_x, vel_y, vel_z = velocity
    along_u = lattice[0] * vel_x + lattice[1] * vel_y + lattice[2] * vel_z
    along_f = lattice[0] * body_force[0] + lattice[1] * body_force[1] + lattice[2] * body_force[2]
    u_dot_f = vel_x * body_force[0] + vel_y * body_force[1] + vel_z * body_force[2]
    u_square = vel_x * vel_x + vel_y * vel_y + vel_z * vel_z
    equilib = weight * density * (1.0 + 3.0 * along_u + 4.5 * along_u * along_u - 1.5 * u_square)
    source = (
        (1.0 - 0.5 / RELAX_TIME) * weight * (3.0 * (along_f - u_dot_f) + 9.0 * along_u * along_f)
    )
    return popul_one - (popul_one - equilib) / RELAX_TIME + source


def roll_depth(flat, step, depth):
    if step == 0:
        return flat
    column = lax.broadcasted_iota(jnp.int32, flat.shape, flat.ndim - 1) % depth
    if step == 1:
        return jnp.where(
            column == 0, jnp.roll(flat, 1 - depth, axis=-1), jnp.roll(flat, 1, axis=-1)
        )
    return jnp.where(
        column == depth - 1, jnp.roll(flat, depth - 1, axis=-1), jnp.roll(flat, -1, axis=-1)
    )


def collide_flat(popul, body_force):
    density, velocity = moments(popul, body_force)
    return [
        roll_depth(
            relax(
                popul[number], density, velocity, body_force, VELOCITIES[number], WEIGHTS[number]
            ),
            VELOCITIES[number][2],
            NZ,
        )
        for number in range(19)
    ]


def shifted(source, lattice, rows_x, rows_y):
    return source[
        1 - lattice[0] : 1 - lattice[0] + rows_x, 1 - lattice[1] : 1 - lattice[1] + rows_y
    ]


def dft_table(count, sign):
    counter = jnp.arange(count, dtype=jnp.int32)
    angle = (counter[:, None] * counter[None, :] % count).astype(jnp.float32) * (
        2.0 * jnp.pi / count
    )
    return (jnp.cos(angle), sign * jnp.sin(angle))


def complex_pass(spectrum, cosine, sine, form):
    with_cos = jnp.einsum(form, spectrum, cosine, precision=HIGHEST)
    with_sin = jnp.einsum(form, spectrum, sine, precision=HIGHEST)
    return jnp.stack([with_cos[0] - with_sin[1], with_sin[0] + with_cos[1]])


def apply_kernel(spectrum, wave_x, wave_y, wave_z, anchor):
    halves = []
    for which_part in range(2):
        comps = demag_kernel(
            spectrum[which_part, 0],
            spectrum[which_part, 1],
            spectrum[which_part, 2],
            wave_x,
            wave_y,
            wave_z,
            anchor,
        )
        halves.append(jnp.stack(comps))
    return jnp.stack(halves)


def kernel_waves(start_x, count_x, full_x, count_y, full_y, index_z, depth):
    index_x = start_x + jnp.arange(count_x, dtype=jnp.int32)
    index_y = jnp.arange(count_y, dtype=jnp.int32)
    wave_x = wavenumber(index_x, full_x, jnp.float32)[None, :, None]
    wave_y = wavenumber(index_y, full_y, jnp.float32)[None, None, :]
    wave_z = wavenumber(index_z, depth, jnp.float32)[:, None, None]
    anchor = (
        (index_z == 0)[:, None, None]
        & (index_x == 0)[None, :, None]
        & (index_y == 0)[None, None, :]
    )
    return (wave_x, wave_y, wave_z, anchor)


def demag_field(magnet):
    rows_x, rows_y, depth = (magnet.shape[1], magnet.shape[2], magnet.shape[3])
    full_x = rows_x * lax.axis_size("gx")
    full_y = rows_y * lax.axis_size("gy")
    fwd_cos, fwd_sin = dft_table(depth, -1.0)
    back_cos, back_sin = (fwd_cos, fwd_sin)
    cos_x, fwd_sin_x = dft_table(full_x, -1.0)
    cos_y, fwd_sin_y = dft_table(full_y, -1.0)
    form_x = "pckxy,xm->pckmy"
    form_y = "pckxy,ym->pckxm"
    spectrum = jnp.stack(
        [
            jnp.einsum("cxyz,zk->ckxy", magnet, fwd_cos, precision=HIGHEST),
            jnp.einsum("cxyz,zk->ckxy", magnet, fwd_sin, precision=HIGHEST),
        ]
    )
    spectrum = lax.all_to_all(spectrum, "gx", split_axis=2, concat_axis=3, tiled=True)
    depth_local = spectrum.shape[2]
    index_z = lax.axis_index("gx") * depth_local + jnp.arange(depth_local, dtype=jnp.int32)
    spectrum = complex_pass(spectrum, cos_x, fwd_sin_x, form_x)
    spectrum = lax.all_to_all(spectrum, "gy", split_axis=3, concat_axis=4, tiled=True)
    spectrum = complex_pass(spectrum, cos_y, fwd_sin_y, form_y)
    slab_x = spectrum.shape[3]
    waves = kernel_waves(
        lax.axis_index("gy") * slab_x, slab_x, full_x, full_y, full_y, index_z, depth
    )
    spectrum = apply_kernel(spectrum, *waves)
    spectrum = complex_pass(spectrum, cos_y, -fwd_sin_y, form_y)
    spectrum = lax.all_to_all(spectrum, "gy", split_axis=4, concat_axis=3, tiled=True)
    spectrum = complex_pass(spectrum, cos_x, -fwd_sin_x, form_x)
    spectrum = lax.all_to_all(spectrum, "gx", split_axis=3, concat_axis=2, tiled=True)
    real_field = jnp.einsum("ckxy,kz->cxyz", spectrum[0], back_cos, precision=HIGHEST) + jnp.einsum(
        "ckxy,kz->cxyz", spectrum[1], back_sin, precision=HIGHEST
    )
    return real_field * (1.0 / (full_x * full_y * depth))


def on_device(populations, h_axial, h_transverse):
    rows_x = populations.shape[1]
    rows_y = populations.shape[2] // NZ
    grid = (rows_x, rows_y, NZ)
    applied = jnp.concatenate([h_transverse, h_axial[None]], axis=0).reshape((3,) + grid)
    magnet = langevin(applied)
    demag = demag_field(magnet)
    total_field = applied + demag
    wide = with_halo(total_field, (("gx", 1), ("gy", 2)), 1)
    body_force = kelvin(magnet, wide).reshape(3, rows_x, rows_y * NZ)
    post = collide_flat(populations, body_force)
    moving = jnp.stack([post[number] for number in range(19) if number not in (0, 5, 6)])
    moving_rim = with_halo(moving.reshape((16,) + grid), (("gx", 1), ("gy", 2)), 1)
    outgoing = []
    for number in range(19):
        if number in (0, 5, 6):
            outgoing.append(post[number])
        else:
            slot = number - 1 if number < 5 else number - 3
            moved = shifted(moving_rim[slot], VELOCITIES[number], rows_x, rows_y)
            outgoing.append(moved.reshape(rows_x, rows_y * NZ))
    result = jnp.stack(outgoing)
    return (result, demag.reshape(3, rows_x, rows_y * NZ))


def solution(mesh):
    placed = (P(None, "gx", "gy"), P("gx", "gy"), P(None, "gx", "gy"))
    return jax.shard_map(
        on_device,
        mesh=mesh,
        in_specs=placed,
        out_specs=(P(None, "gx", "gy"), P(None, "gx", "gy")),
        check_vma=False,
    )
```

profile of v0, /device:TPU:1, one launch (start us, length us, event | category | flops | bytes accessed | tf_op | source)
XLA Modules:
  0.0 343.9 jit_solution(4829794229292998479)
XLA Ops:
  8.4 8.0 %all-to-all-start = ((f32[16,1,12288]{2,1,0:T(1,128)}), f32[16,1,12288]{2,1,0:T(1,128)S(1)}, u32[]{:S(2)}, u32[]{:S(2)}) async-start(f32[16,1,12288]{2,1,0:T(1,128)} %reshape.1378), calls=%async_computation | async-start | bytes 1572864 | tf_op jit(solution)/shard_map/all_to_all | solution.py:194
  16.5 12.4 %all-to-all-done = f32[16,1,12288]{2,1,0:T(1,128)S(1)} async-done(((f32[16,1,12288]{2,1,0:T(1,128)}), f32[16,1,12288]{2,1,0:T(1,128)S(1)}, u32[]{:S(2)}, u32[]{:S(2)}) %all-to-all-start) | async-done | bytes 786464 | tf_op jit(solution)/shard_map/all_to_all | solution.py:194
  32.7 2.7 fusion.9
  41.4 7.2 %all-to-all-start.1 = ((f32[8,1,24576]{2,1,0:T(1,128)}), f32[8,1,24576]{2,1,0:T(1,128)S(1)}, u32[]{:S(2)}, u32[]{:S(2)}) async-start(f32[8,1,24576]{2,1,0:T(1,128)} %reshape.1380), calls=%async_computation.1 | async-start | bytes 1572864 | tf_op jit(solution)/shard_map/all_to_all | solution.py:198
  48.9 12.5 %all-to-all-done.1 = f32[8,1,24576]{2,1,0:T(1,128)S(1)} async-done(((f32[8,1,24576]{2,1,0:T(1,128)}), f32[8,1,24576]{2,1,0:T(1,128)S(1)}, u32[]{:S(2)}, u32[]{:S(2)}) %all-to-all-start.1) | async-done | bytes 786464 | tf_op jit(solution)/shard_map/all_to_all | solution.py:198
  66.2 5.9 %fusion.18 = f32[2,3,4,16,512]{4,3,2,1,0:T(8,128)S(1)} fusion(f32[2,3,4,16,512]{4,3,2,1,0:T(8,128)S(1)} %all_to_all.57), kind=kOutput, calls=%fused_computation.25 | convolution fusion | flops 1211891712 | bytes 1572864 | tf_op jit(solution)/shard_map/pckxy,ym->pckxm/dot_general | solution.py:144
  72.1 6.0 %fusion.22 = f32[2,3,4,16,512]{4,3,2,1,0:T(8,128)S(1)} fusion(f32[2,3,4,16,512]{4,3,2,1,0:T(8,128)S(1)} %all_to_all.57), kind=kOutput, calls=%fused_computation.29 | convolution fusion | flops 1211629568 | bytes 1572864 | tf_op jit(solution)/shard_map/pckxy,ym->pckxm/dot_general | solution.py:143
  78.7 5.3 %fusion.16 = f32[2,3,4,16,512]{4,3,2,1,0:T(8,128)S(1)} fusion(f32[1,3,4,16,512]{4,3,2,1,0:T(8,128)S(1)} %maximum_bitcast_fusion.1, f32[1,3,4,16,512]{4,3,2,1,0:T(8,128)S(1)} %maximum_bitcast_fusion), kind=kOutput, calls=%fused_computation.23 | convolution fusion | flops 1212350464 | bytes 1572864 | tf_op jit(solution)/shard_map/pckxy,ym->pckxm/dot_general | solution.py:144
  84.0 5.3 %fusion.20 = f32[2,3,4,16,512]{4,3,2,1,0:T(8,128)S(1)} fusion(f32[1,3,4,16,512]{4,3,2,1,0:T(8,128)S(1)} %maximum_bitcast_fusion.1, f32[1,3,4,16,512]{4,3,2,1,0:T(8,128)S(1)} %maximum_bitcast_fusion), kind=kOutput, calls=%fused_computation.27 | convolution fusion | flops 1211826176 | bytes 1572864 | tf_op jit(solution)/shard_map/pckxy,ym->pckxm/dot_general | solution.py:143
  89.5 4.6 %copy.71 = f32[2,3,4,16,512]{3,2,1,0,4:T(4,128)} copy(f32[2,3,4,16,512]{4,3,2,1,0:T(8,128)S(1)} %pad_maximum_fusion.14) | data formatting | bytes 1572864 | tf_op jit(solution)/shard_map/stack | solution.py:145
  94.1 6.9 %reshape.1382 = f32[8,1,24576]{2,1,0:T(1,128)S(1)} reshape(f32[512,2,3,4,16]{4,3,2,1,0:T(4,128)} %bitcast.474) | data formatting | bytes 1572864
  101.0 16.0 %all_to_all.69 = f32[8,1,24576]{2,1,0:T(1,128)S(1)} all-to-all(f32[8,1,24576]{2,1,0:T(1,128)S(1)} %reshape.1382), channel_id=1, replica_groups=mesh['gx'=16,'gy'=8] {'gy'}, dimensions={0} | all-to-all | bytes 1572864 | tf_op jit(solution)/shard_map/all_to_all | solution.py:206
  119.6 7.1 %reshape.1383 = f32[512,2,3,4,16]{4,3,2,1,0:T(4,128)} reshape(f32[8,24576]{1,0:T(8,128)S(1)} %reduce.2) | data formatting | bytes 1572864
  126.6 5.1 %copy.72 = f32[2,3,4,16,8,64]{5,3,4,2,1,0:T(8,128)S(1)} copy(f32[2,3,4,16,8,64]{3,2,1,0,5,4:T(4,128)} %bitcast.475) | data formatting | bytes 1572864 | tf_op jit(solution)/shard_map/all_to_all | solution.py:206
  131.8 2.7 convolution_bitcast_fusion
  138.8 3.8 %reshape.1384 = f32[16,1,12288]{2,1,0:T(1,128)} reshape(f32[128,2,3,4,64]{4,3,2,1,0:T(4,128)} %bitcast.485) | data formatting | bytes 1572864
  142.6 6.7 %all-to-all-start.3 = ((f32[16,1,12288]{2,1,0:T(1,128)}), f32[16,1,12288]{2,1,0:T(1,128)}, u32[]{:S(2)}, u32[]{:S(2)}) async-start(f32[16,1,12288]{2,1,0:T(1,128)} %reshape.1384), calls=%async_computation.3 | async-start | bytes 1572864 | tf_op jit(solution)/shard_map/all_to_all | solution.py:208
  156.0 6.3 %all-to-all-done.3 = f32[16,1,12288]{2,1,0:T(1,128)} async-done(((f32[16,1,12288]{2,1,0:T(1,128)}), f32[16,1,12288]{2,1,0:T(1,128)}, u32[]{:S(2)}, u32[]{:S(2)}) %all-to-all-start.3) | async-done | bytes 786464 | tf_op jit(solution)/shard_map/all_to_all | solution.py:208
  162.2 3.7 %reduce.3 = f32[16,12288]{1,0:T(8,128)S(1)} reduce(f32[16,1,12288]{2,1,0:T(1,128)} %all-to-all-done.3, f32[]{:T(128)} %broadcast.1830), dimensions={1}, to_apply=%all_to_all.62.reduce_sub_computation | reduce | bytes 1572868 | tf_op jit(solution)/shard_map/all_to_all | solution.py:208
  185.3 4.3 %collective-permute-start.2 = (f32[3,10,1,64]{3,2,1,0:T(1,128)}, f32[3,10,1,64]{3,2,1,0:T(1,128)}, u32[]{:S(2)}, u32[]{:S(2)}) collective-permute-start(f32[3,10,1,64]{3,2,1,0:T(1,128)} %copy.79), channel_id=1, source_target_pairs={{1,0},{2,1},{3,2},{4,3},{5,4},{6,5},{7,6},{0,7},{9,8},{10,9},{11,1... | collective-permute-start | bytes 23048 | tf_op jit(solution)/shard_map/ppermute | solution.py:46
  198.8 2.8 fusion.32
  274.2 3.6 %collective-permute-start.5 = (f32[16,1,64,64]{3,2,1,0:T(8,128)S(1)}, f32[16,1,64,64]{3,2,1,0:T(8,128)S(1)}, u32[]{:S(2)}, u32[]{:S(2)}) collective-permute-start(f32[16,1,64,64]{3,2,1,0:T(8,128)S(1)} %get-tuple-element.35), channel_id=1, source_target_pairs={{8,0},{16,8},{24,16},{32,24},{40,32},{48,40},{56,48},{64,56},{72,6... | collective-permute-start | bytes 786440 | tf_op jit(solution)/shard_map/ppermute | solution.py:46
  278.0 12.7 %collective-permute-done.5 = f32[16,1,64,64]{3,2,1,0:T(8,128)S(1)} collective-permute-done((f32[16,1,64,64]{3,2,1,0:T(8,128)S(1)}, f32[16,1,64,64]{3,2,1,0:T(8,128)S(1)}, u32[]{:S(2)}, u32[]{:S(2)}) %collective-permute-start.5) | collective-permute-done | bytes 262176 | tf_op jit(solution)/shard_map/ppermute | solution.py:46
  292.1 3.2 collective-permute-start.6
  (360 shorter events, 187.3 us)
Async XLA Ops:
  8.4 20.5 %all-to-all-start = ((f32[16,1,12288]{2,1,0:T(1,128)}), f32[16,1,12288]{2,1,0:T(1,128)S(1)}, u32[]{:S(2)}, u32[]{:S(2)}) async-start(f32[16,1,12288]{2,1,0:T(1,128)} %reshape.1378), calls=%async_computation | async-start | bytes 1572864 | tf_op jit(solution)/shard_map/all_to_all | solution.py:194
  41.4 19.9 %all-to-all-start.1 = ((f32[8,1,24576]{2,1,0:T(1,128)}), f32[8,1,24576]{2,1,0:T(1,128)S(1)}, u32[]{:S(2)}, u32[]{:S(2)}) async-start(f32[8,1,24576]{2,1,0:T(1,128)} %reshape.1380), calls=%async_computation.1 | async-start | bytes 1572864 | tf_op jit(solution)/shard_map/all_to_all | solution.py:198
  138.8 14.8 %copy-start = (f32[19,8,4096]{2,1,0:T(8,128)S(1)}, f32[19,8,4096]{2,1,0:T(8,128)}, u32[]{:S(2)}) copy-start(f32[19,8,4096]{2,1,0:T(8,128)} %param.3) | copy-start | bytes 7471108
  142.6 19.6 %all-to-all-start.3 = ((f32[16,1,12288]{2,1,0:T(1,128)}), f32[16,1,12288]{2,1,0:T(1,128)}, u32[]{:S(2)}, u32[]{:S(2)}) async-start(f32[16,1,12288]{2,1,0:T(1,128)} %reshape.1384), calls=%async_computation.3 | async-start | bytes 1572864 | tf_op jit(solution)/shard_map/all_to_all | solution.py:208
  173.9 4.1 %collective-permute-start = (f32[3,1,64,64]{2,3,1,0:T(8,128)S(1)}, f32[3,1,64,64]{2,3,1,0:T(8,128)S(1)}, u32[]{:S(2)}, u32[]{:S(2)}) collective-permute-start(f32[3,1,64,64]{2,3,1,0:T(8,128)S(1)} %get-tuple-element.76), channel_id=1, source_target_pairs={{8,0},{16,8},{24,16},{32,24},{40,32},{48,40},{56,48},{64,56},{72,6... | collective-permute-start | bytes 147464 | tf_op jit(solution)/shard_map/ppermute | solution.py:46
  175.1 3.3 collective-permute-start.1
  182.2 12.5 %collective-permute-start.3 = (f32[3,10,1,64]{3,2,1,0:T(1,128)}, f32[3,10,1,64]{3,2,1,0:T(1,128)}, u32[]{:S(2)}, u32[]{:S(2)}) collective-permute-start(f32[3,10,1,64]{3,2,1,0:T(1,128)} %copy.81), channel_id=1, source_target_pairs={{0,1},{1,2},{2,3},{3,4},{4,5},{5,6},{6,7},{7,0},{8,9},{9,10},{10,1... | collective-permute-start | bytes 23048 | tf_op jit(solution)/shard_map/ppermute | solution.py:45
  185.3 13.6 %copy-start.8 = (f32[8,64,64]{1,2,0:T(8,128)S(1)}, f32[8,64,64]{1,2,0:T(8,128)}, u32[]{:S(2)}) copy-start(f32[8,64,64]{1,2,0:T(8,128)} %get-tuple-element.68) | copy-start | bytes 393220
  185.3 11.5 %collective-permute-start.2 = (f32[3,10,1,64]{3,2,1,0:T(1,128)}, f32[3,10,1,64]{3,2,1,0:T(1,128)}, u32[]{:S(2)}, u32[]{:S(2)}) collective-permute-start(f32[3,10,1,64]{3,2,1,0:T(1,128)} %copy.79), channel_id=1, source_target_pairs={{1,0},{2,1},{3,2},{4,3},{5,4},{6,5},{7,6},{0,7},{9,8},{10,9},{11,1... | collective-permute-start | bytes 23048 | tf_op jit(solution)/shard_map/ppermute | solution.py:46
  240.4 9.6 %copy-start.45 = (f32[1,8,1]{2,1,0:T(8,128)S(1)}, f32[1,8,1]{2,1,0:T(8,128)}, u32[]{:S(2)}) copy-start(f32[1,8,1]{2,1,0:T(8,128)} %slice_bitcast_fusion.52) | copy-start | bytes 100
  240.6 11.2 %copy-start.44 = (f32[1,8,63]{2,1,0:T(8,128)S(1)}, f32[1,8,63]{2,1,0:T(8,128)}, u32[]{:S(2)}) copy-start(f32[1,8,63]{2,1,0:T(8,128)} %slice_bitcast_fusion.51) | copy-start | bytes 6052
  240.8 12.8 %copy-start.43 = (f32[1,8,1]{2,1,0:T(8,128)S(1)}, f32[1,8,1]{2,1,0:T(8,128)}, u32[]{:S(2)}) copy-start(f32[1,8,1]{2,1,0:T(8,128)} %slice_bitcast_fusion.50) | copy-start | bytes 100
  241.9 13.5 %copy-start.42 = (f32[1,8,63]{2,1,0:T(8,128)S(1)}, f32[1,8,63]{2,1,0:T(8,128)}, u32[]{:S(2)}) copy-start(f32[1,8,63]{2,1,0:T(8,128)} %slice_bitcast_fusion.49) | copy-start | bytes 6052
  243.7 13.5 %copy-start.41 = (f32[1,8,1]{2,1,0:T(8,128)S(1)}, f32[1,8,1]{2,1,0:T(8,128)}, u32[]{:S(2)}) copy-start(f32[1,8,1]{2,1,0:T(8,128)} %slice_bitcast_fusion.48) | copy-start | bytes 100
  245.5 13.5 %copy-start.40 = (f32[1,8,63]{2,1,0:T(8,128)S(1)}, f32[1,8,63]{2,1,0:T(8,128)}, u32[]{:S(2)}) copy-start(f32[1,8,63]{2,1,0:T(8,128)} %slice_bitcast_fusion.47) | copy-start | bytes 6052
  247.4 13.5 %copy-start.30 = (f32[1,8,4095]{2,1,0:T(8,128)S(1)}, f32[1,8,4095]{2,1,0:T(8,128)}, u32[]{:S(2)}) copy-start(f32[1,8,4095]{2,1,0:T(8,128)} %slice_bitcast_fusion.20) | copy-start | bytes 393124
  247.4 13.5 %copy-start.39 = (f32[1,8,1]{2,1,0:T(8,128)S(1)}, f32[1,8,1]{2,1,0:T(8,128)}, u32[]{:S(2)}) copy-start(f32[1,8,1]{2,1,0:T(8,128)} %slice_bitcast_fusion.46) | copy-start | bytes 100
  274.2 16.5 %collective-permute-start.5 = (f32[16,1,64,64]{3,2,1,0:T(8,128)S(1)}, f32[16,1,64,64]{3,2,1,0:T(8,128)S(1)}, u32[]{:S(2)}, u32[]{:S(2)}) collective-permute-start(f32[16,1,64,64]{3,2,1,0:T(8,128)S(1)} %get-tuple-element.35), channel_id=1, source_target_pairs={{8,0},{16,8},{24,16},{32,24},{40,32},{48,40},{56,48},{64,56},{72,6... | collective-permute-start | bytes 786440 | tf_op jit(solution)/shard_map/ppermute | solution.py:46
  277.8 12.9 %collective-permute-start.4 = (f32[16,1,64,64]{3,2,1,0:T(8,128)S(1)}, f32[16,1,64,64]{3,2,1,0:T(8,128)S(1)}, u32[]{:S(2)}, u32[]{:S(2)}) collective-permute-start(f32[16,1,64,64]{3,2,1,0:T(8,128)S(1)} %get-tuple-element.34), channel_id=1, source_target_pairs={{0,8},{8,16},{16,24},{24,32},{32,40},{40,48},{48,56},{56,64},{64,7... | collective-permute-start | bytes 786440 | tf_op jit(solution)/shard_map/ppermute | solution.py:45
  278.0 21.4 %copy-start.1 = (f32[16,8,64,64]{3,2,1,0:T(8,128)S(1)}, f32[16,8,64,64]{3,2,1,0:T(8,128)}, u32[]{:S(2)}) copy-start(f32[16,8,64,64]{3,2,1,0:T(8,128)} %fusion.59) | copy-start | bytes 6291460
  292.1 4.9 %collective-permute-start.7 = (f32[16,10,1,64]{3,2,1,0:T(1,128)S(1)}, f32[16,10,1,64]{3,2,1,0:T(1,128)S(1)}, u32[]{:S(2)}, u32[]{:S(2)}) collective-permute-start(f32[16,10,1,64]{3,2,1,0:T(1,128)S(1)} %get-tuple-element.33), channel_id=1, source_target_pairs={{1,0},{2,1},{3,2},{4,3},{5,4},{6,5},{7,6},{0,7},{9,8},{10,9},{11,1... | collective-permute-start | bytes 122888 | tf_op jit(solution)/shard_map/ppermute | solution.py:46
  292.1 7.2 %collective-permute-start.6 = (f32[16,10,1,64]{3,2,1,0:T(1,128)S(1)}, f32[16,10,1,64]{3,2,1,0:T(1,128)S(1)}, u32[]{:S(2)}, u32[]{:S(2)}) collective-permute-start(f32[16,10,1,64]{3,2,1,0:T(1,128)S(1)} %get-tuple-element.32), channel_id=1, source_target_pairs={{0,1},{1,2},{2,3},{3,4},{4,5},{5,6},{6,7},{7,0},{8,9},{9,10},{10,1... | collective-permute-start | bytes 122888 | tf_op jit(solution)/shard_map/ppermute | solution.py:45
  328.2 9.5 %copy-start.25 = (f32[1,8,4096]{2,1,0:T(8,128)S(1)}, f32[1,8,4096]{2,1,0:T(8,128)}, u32[]{:S(2)}) copy-start(f32[1,8,4096]{2,1,0:T(8,128)} %stack_reshape.55) | copy-start | bytes 393220
  328.3 10.0 %copy-start.26 = (f32[1,8,4096]{2,1,0:T(8,128)S(1)}, f32[1,8,4096]{2,1,0:T(8,128)}, u32[]{:S(2)}) copy-start(f32[1,8,4096]{2,1,0:T(8,128)} %stack_reshape.56) | copy-start | bytes 393220
  (42 other events, 208.5 us)
where the time goes:
time: 350 us; the launch traced here: 344 us
  local copies, waits for them, and re-layouts  156 us (45%)
  waiting for transfers between devices  49.3 us (14%)
  other arithmetic  47.3 us (14%)
  matrix products  37.9 us (11%)
  starting transfers between devices  35.8 us (10%)
  blocking collectives  16 us (5%)
    unnamed x141, local copies, waits for them, and re-layouts  42.7 us
    dot_general x4, matrix products, complex_pass(): with_cos = jnp.einsum(form, spectrum, cosine, precision=HIGHEST)  16.6 us
    dot_general x4, matrix products, complex_pass(): with_sin = jnp.einsum(form, spectrum, sine, precision=HIGHEST)  16.5 us
    all_to_all x1, blocking collectives, demag_field(): lax.all_to_all(spectrum, 'gy', split_axis=4, concat_axis=3, tiled=True)  16 us
    ppermute x4, waiting for transfers between devices, with_halo(): after = lax.ppermute(leading, axis, down)  15.4 us
    another operation x17, local copies, waits for them, and re-layouts, on_device(): result = jnp.stack(outgoing)  15.3 us
    all_to_all x1, waiting for transfers between devices, demag_field(): lax.all_to_all(spectrum, 'gy', split_axis=3, concat_axis=4, tiled=True)  12.5 us
    all_to_all x1, waiting for transfers between devices, demag_field(): lax.all_to_all(spectrum, 'gx', split_axis=2, concat_axis=3, tiled=True)  12.4 us
  transfers between devices with their start and end apart: 11, of which 8 were waited for; matrix products, arithmetic and copies ran while one was open for 5% of the time, Pallas kernels for 0%

commit v1 on v0

v1 whole, which is shorter than its diff:
```python
import functools

import jax
import jax.numpy as jnp
import numpy as np
from jax import lax
from jax.experimental import pallas as pl
from jax.experimental.pallas import tpu as pltpu
from jax.sharding import PartitionSpec as P

NX, NY, NZ = 128, 512, 64
GX, GY = 16, 8
VELOCITIES = (
    (0, 0, 0),
    (1, 0, 0),
    (-1, 0, 0),
    (0, 1, 0),
    (0, -1, 0),
    (0, 0, 1),
    (0, 0, -1),
    (1, 1, 0),
    (-1, -1, 0),
    (1, -1, 0),
    (-1, 1, 0),
    (1, 0, 1),
    (-1, 0, -1),
    (1, 0, -1),
    (-1, 0, 1),
    (0, 1, 1),
    (0, -1, -1),
    (0, 1, -1),
    (0, -1, 1),
)
WEIGHTS = (1.0 / 3.0,) + (1.0 / 18.0,) * 6 + (1.0 / 36.0,) * 12
OMEGA = 1.0 / 0.6
HIGHEST = lax.Precision.HIGHEST
F32 = jnp.float32
VMEM_BYTES = 48 * 1024 * 1024

X_FACE = ((0, 0, 1, 2), (1, 0, 7, 10), (-1, 0, 9, 8), (0, 1, 11, 14), (0, -1, 13, 12))
Y_FACE = ((0, 0, 3, 4), (1, 0, 7, 9), (-1, 0, 10, 8), (0, 1, 15, 18), (0, -1, 17, 16))
X_SLOT = {n: s for s, row in enumerate(X_FACE) for n in row[2:]}

ROWS_FWD = 12
ROWS_BACK = 20
PITCH = 80


def cas(rows, cols, count):
    angle = 2.0 * np.pi * ((rows[:, None] * cols[None, :]) % count) / count
    return np.cos(angle) + np.sin(angle)


def wave(index, count):
    return 2.0 * np.sin(np.pi * index / count)


@functools.lru_cache(maxsize=None)
def tables():
    every_x, every_z = np.arange(NX), np.arange(NZ)
    half = np.arange(NY // 2)
    out = {}
    fwd_z = np.zeros((NZ, 128))
    fwd_z[:, :NZ] = cas(every_z, every_z, NZ)
    out["fwd_z"] = fwd_z
    out["back_z"] = np.tile(cas(every_z, every_z, NZ), (1, 2))
    fwd_x, back_x = [], []
    m = np.arange(8)
    for parity in range(2):
        order = []
        for side in (parity, 1 - parity):
            for x2 in range(2):
                for x4 in range(4):
                    order += list(8 * (2 * m + side) + 2 * x4 + x2)
        fwd_x.append(cas(every_x, np.array(order), NX))
        order = []
        for x2 in range(2):
            for x6 in range(6):
                order += list((8 * (2 * m + parity) - 2 + 2 * x6 + x2) % NX)
        back_x.append(cas(np.array(order), every_x, NX))
    out["fwd_x"] = np.stack(fwd_x)
    out["back_x"] = np.stack(back_x)
    even, odd = 2 * half, 2 * half + 1
    halo = np.array(
        [
            (64 * g + (-2, -1, 64, 65)[k]) % NY
            for g in range(GY)
            for c in range(4)
            for k in range(4)
        ]
    )
    out["even"] = cas(half, even, NY)
    out["odd"] = cas(half, odd, NY)
    out["back_even"] = np.concatenate([cas(even, half, NY), cas(even, halo, NY)], axis=1)
    out["back_odd"] = np.concatenate([cas(odd, half, NY), cas(odd, halo, NY)], axis=1)
    out["wave_x"] = np.repeat(wave(every_x, NX)[:, None], 128, axis=1)
    out["wave_y"] = np.stack([wave(even, NY), wave(odd, NY)])
    out["wave_z"] = np.repeat(wave(every_z, NZ)[:, None], 128, axis=1)
    return {name: np.asarray(value, np.float32) for name, value in out.items()}


def dot(a, b, dims=(1, 0)):
    return lax.dot_general(
        a, b, (((dims[0],), (dims[1],)), ((), ())), precision=HIGHEST, preferred_element_type=F32
    )


def langevin(hx, hy, hz):
    magnitude = jnp.sqrt(hx * hx + hy * hy + hz * hz)
    argument = 1.5 * magnitude
    decay = jnp.exp(-2.0 * argument)
    scale = ((1.0 + decay) / (1.0 - decay) - 1.0 / argument) / magnitude
    return hx * scale, hy * scale, hz * scale


def lanes(shape=(8, 128)):
    return lax.broadcasted_iota(jnp.int32, shape, len(shape) - 1)


def first_kernel(ht_ref, ha_ref, table_ref, magnet_ref, send_ref, rows_ref):
    magnet = langevin(ht_ref[0], ht_ref[1], ha_ref[...])
    for c in range(3):
        magnet_ref[c] = magnet[c]
        for pair in range(32):
            tile = magnet[c][:, pair * 128 : pair * 128 + 128]
            rows_ref[pl.ds(c * 512 + 2 * pair, 8, stride=64), :] = tile
            rows_ref[pl.ds(c * 512 + 2 * pair + 1, 8, stride=64), :] = pltpu.roll(tile, 64, 1)
    spectrum = dot(table_ref[...], rows_ref[...], (1, 1))
    for row in range(ROWS_FWD):
        send_ref[pl.ds(row, NZ, stride=ROWS_FWD), :] = spectrum[:, row * 128 : row * 128 + 128]


def transpose_blocks(tiles):
    block = lanes() // 16
    for bit in (1, 2, 4):
        low = (block & bit) == 0
        out = list(tiles)
        for i in range(8):
            if i & bit == 0:
                a, b = tiles[i], tiles[i | bit]
                out[i] = jnp.where(low, a, pltpu.roll(b, 16 * bit, 1))
                out[i | bit] = jnp.where(low, pltpu.roll(a, 128 - 16 * bit, 1), b)
        tiles = out
    return tiles


def plane_kernel(
    own_ref,
    other_ref,
    fwd_x_ref,
    back_x_ref,
    even_ref,
    odd_ref,
    back_even_ref,
    back_odd_ref,
    wave_x_ref,
    wave_y_ref,
    wave_z_ref,
    send_ref,
    cells_ref,
):
    row = lax.axis_index("gx")
    parity = lax.rem(row, 2)
    index_z = (row // 2) * GY + lax.axis_index("gy")
    left = lanes() < 64
    for side, ref in enumerate((own_ref, other_ref)):
        for c in range(3):
            for pair in range(4):
                for x4 in range(4):
                    start = 2 * pair * ROWS_FWD + c * 4 + x4
                    a = ref[pl.ds(start, 8, stride=GY * ROWS_FWD), :]
                    b = ref[pl.ds(start + ROWS_FWD, 8, stride=GY * ROWS_FWD), :]
                    at = side * 64 + x4 * 8
                    col = c * 512 + pair * 128
                    cells_ref[at : at + 8, col : col + 128] = jnp.where(
                        left, a, pltpu.roll(b, 64, 1)
                    )
                    cells_ref[at + 32 : at + 40, col : col + 128] = jnp.where(
                        left, pltpu.roll(a, 64, 1), b
                    )
    wave_x = wave_x_ref[:, 0:1]
    wave_z = wave_z_ref[pl.ds(index_z, 1), 0:1]
    spectrum = dot(fwd_x_ref[parity], cells_ref[...])
    along = wave_x * spectrum[:, :512] + wave_z * spectrum[:, 1024:]
    both = jnp.concatenate([along, spectrum[:, 512:1024]], axis=0)
    parts = (
        dot(both[:, :256] + both[:, 256:], even_ref[...]),
        dot(both[:, :256] - both[:, 256:], odd_ref[...]),
    )
    back = []
    for which in range(2):
        wave_y = wave_y_ref[which : which + 1, :]
        squared = wave_x * wave_x + wave_y * wave_y + wave_z * wave_z
        anchor = squared == 0.0
        factor = jnp.where(
            anchor, 0.0, (-1.0 / (NX * NY * NZ)) / jnp.where(anchor, 1.0, squared)
        )
        potential = (parts[which][:128] + wave_y * parts[which][128:]) * factor
        stacked = jnp.concatenate([potential, wave_y * potential], axis=0)
        back.append(dot(stacked, (back_even_ref, back_odd_ref)[which][...]))
    low, high = back[0] + back[1], back[0] - back[1]
    column = lanes((128, 128)) % 16
    halo_p, halo_q = low[:128, 256:], low[128:, 256:]
    halo = jnp.where(
        column < 4,
        wave_x * halo_p,
        jnp.where(column < 8, halo_q, jnp.where(column < 12, wave_z * halo_p, 0.0)),
    )
    potential = jnp.concatenate([low[:128, :256], high[:128, :256]], axis=1)
    fields = jnp.concatenate(
        [wave_x * potential, low[128:, :256], high[128:, :256], wave_z * potential, halo], axis=1
    )
    cells = dot(back_x_ref[parity], fields)
    step = GY * ROWS_BACK
    for x6 in range(6):
        for c in range(3):
            for pair in range(4):
                col = c * 512 + pair * 128
                a = cells[x6 * 8 : x6 * 8 + 8, col : col + 128]
                b = cells[48 + x6 * 8 : 56 + x6 * 8, col : col + 128]
                at = 2 * pair * ROWS_BACK + c * 6 + x6
                send_ref[pl.ds(at, 8, stride=step), :] = jnp.where(left, a, pltpu.roll(b, 64, 1))
                send_ref[pl.ds(at + ROWS_BACK, 8, stride=step), :] = jnp.where(
                    left, pltpu.roll(a, 64, 1), b
                )
    for part in range(2):
        tiles = []
        for x in range(part * 8, part * 8 + 8):
            if x < 12:
                at = (x % 2) * 48 + (x // 2) * 8
                tiles.append(cells[at : at + 8, 1536:])
            else:
                tiles.append(jnp.zeros((8, 128), F32))
        for g, tile in enumerate(transpose_blocks(tiles)):
            send_ref[pl.ds(g * ROWS_BACK + 18 + part, 8, stride=step), :] = tile


def macroscopic(density, momentum, force):
    inverse = 1.0 / density
    vel = [(momentum[k] + 0.5 * force[k]) * inverse for k in range(3)]
    u_square = vel[0] * vel[0] + vel[1] * vel[1] + vel[2] * vel[2]
    u_dot_f = vel[0] * force[0] + vel[1] * force[1] + vel[2] * force[2]
    scaled = OMEGA * density
    base = scaled * (1.0 - 1.5 * u_square) - 0.5 * u_dot_f
    return vel, scaled, base


def along(lattice, vector):
    total = None
    for sign, value in zip(lattice, vector):
        if isinstance(sign, int):
            if sign == 0:
                continue
            term = value if sign == 1 else -value
        else:
            term = sign * value
        total = term if total is None else total + term
    return total


def relax_terms(lattice, vel, force, scaled, base):
    along_u = along(lattice, vel)
    along_f = along(lattice, force)
    even = base + along_u * (4.5 * scaled * along_u + 1.5 * along_f)
    odd = 3.0 * scaled * along_u + 0.5 * along_f
    return even, odd


def shift_z(tile, step, lane):
    if step == 0:
        return tile
    if step == 1:
        return jnp.where(lane % 64 == 0, pltpu.roll(tile, 65, 1), pltpu.roll(tile, 1, 1))
    return jnp.where(lane % 64 == 63, pltpu.roll(tile, 63, 1), pltpu.roll(tile, 127, 1))


def cell_kernel(
    recv_ref,
    table_ref,
    applied_ref,
    magnet_ref,
    pop_ref,
    x_ref,
    y_ref,
    out_ref,
    demag_ref,
    field_ref,
    total_ref,
    post_ref,
    low_ref,
    high_ref,
):
    lane = lanes()
    left = lane < 64
    for row in range(ROWS_BACK):
        spectrum = recv_ref[pl.ds(row, NZ, stride=ROWS_BACK), :]
        field_ref[row * 128 : row * 128 + 128, :] = dot(spectrum, table_ref[...], (0, 0))
    for c in range(3):
        for x in range(12):
            at = (c * 12 + x) * PITCH
            src = (c * 12 + x) * 64
            total_ref[at + 8 : at + 72, :] = (
                field_ref[src : src + 64, :] + applied_ref[at + 8 : at + 72, :]
            )
            src = 2304 + x * 16 + c * 4
            total_ref[at + 6 : at + 8, :] = (
                field_ref[src : src + 2, :] + applied_ref[at + 6 : at + 8, :]
            )
            total_ref[at + 72 : at + 74, :] = (
                field_ref[src + 2 : src + 4, :] + applied_ref[at + 72 : at + 74, :]
            )

    def cells(c, x, y):
        return total_ref[pl.ds((c * 12 + 2 + x) * PITCH + 8 + y, 8, stride=PITCH), :]

    def force_at(magnet, ya, yb):
        force = []
        for c in range(3):
            d_x = jnp.where(left, cells(c, 1, ya), cells(c, 1, yb)) - jnp.where(
                left, cells(c, -1, ya), cells(c, -1, yb)
            )
            d_y = jnp.where(left, cells(c, 0, ya + 1), cells(c, 0, yb + 1)) - jnp.where(
                left, cells(c, 0, ya - 1), cells(c, 0, yb - 1)
            )
            a, b = cells(c, 0, ya), cells(c, 0, yb)
            d_z = jnp.where(left, pltpu.roll(a, 127, 1), pltpu.roll(b, 127, 1)) - jnp.where(
                left, pltpu.roll(a, 1, 1), pltpu.roll(b, 1, 1)
            )
            force.append(0.025 * (magnet[0] * d_x + magnet[1] * d_y + magnet[2] * d_z))
        return force

    applied = []
    for c in range(3):
        at = (c * 12 + 2) * PITCH + 8
        applied.append(
            jnp.where(
                left,
                applied_ref[pl.ds(at + 64, 8, stride=PITCH), :],
                applied_ref[pl.ds(at - 1, 8, stride=PITCH), :],
            )
        )
    sign = jnp.where(left, -1.0, 1.0)
    force = force_at(langevin(*applied), 64, -1)
    vel, scaled, base = macroscopic(y_ref[5], [y_ref[6], y_ref[7], y_ref[8]], force)
    for slot, (cx, cz, up, down) in enumerate(Y_FACE):
        even, odd = relax_terms((cx, sign, cz), vel, force, scaled, base)
        post = shift_z((1.0 - OMEGA) * y_ref[slot] + WEIGHTS[up] * (even + odd), cz, lane)
        post_ref[up, 0] = post
        post_ref[down, 33] = post

    for part in range(10):
        rows = 8 * part

        def edge(ref, c, xa, xb, shift=0):
            a = (c * 12 + 2 + xa) * PITCH + rows + shift
            b = (c * 12 + 2 + xb) * PITCH + rows + shift
            return ref[a : a + 8, :], ref[b : b + 8, :]

        magnet = langevin(*[jnp.where(left, *edge(applied_ref, c, -1, 8)) for c in range(3)])
        force = []
        for c in range(3):
            d_x = jnp.where(left, *edge(total_ref, c, 0, 9)) - jnp.where(
                left, *edge(total_ref, c, -2, 7)
            )
            d_y = jnp.where(left, *edge(total_ref, c, -1, 8, 1)) - jnp.where(
                left, *edge(total_ref, c, -1, 8, -1)
            )
            a, b = edge(total_ref, c, -1, 8)
            d_z = jnp.where(left, pltpu.roll(a, 127, 1), pltpu.roll(b, 127, 1)) - jnp.where(
                left, pltpu.roll(a, 1, 1), pltpu.roll(b, 1, 1)
            )
            force.append(0.025 * (magnet[0] * d_x + magnet[1] * d_y + magnet[2] * d_z))
        values = [x_ref[k, rows : rows + 8, :] for k in range(9)]
        vel, scaled, base = macroscopic(values[5], values[6:], force)
        for slot, (cy, cz, up, down) in enumerate(X_FACE):
            even, odd = relax_terms((-sign, cy, cz), vel, force, scaled, base)
            post = shift_z((1.0 - OMEGA) * values[slot] + WEIGHTS[up] * (even + odd), cz, lane)
            turned = pltpu.roll(post, 64, 1)
            low_ref[slot, rows : rows + 8, :] = jnp.where(left, post, turned)
            high_ref[slot, rows : rows + 8, :] = jnp.where(left, turned, post)

    def collide(pair, carry):
        ya = 2 * pair
        here = pl.ds(pl.multiple_of(pair * 128, 128), 128)
        for c in range(3):
            at = (c * 12 + 2) * 64 + ya
            demag_ref[c, :, here] = jnp.where(
                left,
                field_ref[pl.ds(at, 8, stride=64), :],
                field_ref[pl.ds(at + 1, 8, stride=64), :],
            )
        force = force_at([magnet_ref[c, :, here] for c in range(3)], ya, ya + 1)
        popul = [pop_ref[n, :, here] for n in range(19)]
        density = popul[0]
        for n in range(1, 19):
            density = density + popul[n]
        momentum = []
        for k in range(3):
            total = None
            for n in range(1, 19):
                if VELOCITIES[n][k] == 1:
                    total = popul[n] if total is None else total + popul[n]
                elif VELOCITIES[n][k] == -1:
                    total = total - popul[n]
            momentum.append(total)
        vel, scaled, base = macroscopic(density, momentum, force)
        post_ref[0, 1 + pair] = (1.0 - OMEGA) * popul[0] + WEIGHTS[0] * base
        for n in range(1, 19, 2):
            even, odd = relax_terms(VELOCITIES[n], vel, force, scaled, base)
            for number, value in ((n, even + odd), (n + 1, even - odd)):
                post = (1.0 - OMEGA) * popul[number] + WEIGHTS[n] * value
                post_ref[number, 1 + pair] = shift_z(post, VELOCITIES[number][2], lane)
        return carry

    lax.fori_loop(0, 32, collide, 0)
    row = lax.broadcasted_iota(jnp.int32, (8, 128), 0)

    def stream(pair, carry):
        here = pl.ds(pl.multiple_of(pair * 128, 128), 128)
        for n in range(19):
            cx, cy, _ = VELOCITIES[n]
            tile = post_ref[n, 1 + pair]
            if cy == 1:
                tile = pltpu.roll(jnp.where(left, tile, post_ref[n, pair]), 64, 1)
            elif cy == -1:
                tile = pltpu.roll(jnp.where(left, post_ref[n, 2 + pair], tile), 64, 1)
            if cx != 0:
                ref = low_ref if cx == 1 else high_ref
                at = 8 + 2 * pair - cy
                slot = X_SLOT[n]
                enters = jnp.where(
                    left[:1], ref[slot, pl.ds(at, 1), :], ref[slot, pl.ds(at + 1, 1), :]
                )
                tile = jnp.where(
                    row == (0 if cx == 1 else 7),
                    jnp.broadcast_to(enters, (8, 128)),
                    pltpu.roll(tile, 1 if cx == 1 else 7, 0),
                )
            out_ref[n, :, here] = tile
        return carry

    lax.fori_loop(0, 32, stream, 0)


def call(kernel, out, scratch, flops, moved):
    return pl.pallas_call(
        kernel,
        out_shape=[jax.ShapeDtypeStruct(shape, F32) for shape in out],
        scratch_shapes=[pltpu.VMEM(shape, F32) for shape in scratch],
        compiler_params=pltpu.CompilerParams(vmem_limit_bytes=VMEM_BYTES),
        cost_estimate=pl.CostEstimate(flops=flops, bytes_accessed=moved, transcendentals=0),
    )


def ring(values, axis, step):
    size = lax.axis_size(axis)
    return lax.ppermute(values, axis, [(i, (i + step) % size) for i in range(size)])


def edge_moments(popul):
    density = jnp.sum(popul, axis=0)
    momentum = []
    for k in range(3):
        momentum.append(
            sum(VELOCITIES[n][k] * popul[n] for n in range(19) if VELOCITIES[n][k] != 0)
        )
    return [density] + momentum


def neighbours(populations, applied):
    popul = populations.reshape(19, 8, 64, 64)
    field = applied.reshape(3, 8, 64, 64)

    def package(edge, numbers):
        return jnp.stack([edge[n] for n in numbers] + edge_moments(edge))

    up_y = package(popul[:, :, 63], [f[2] for f in Y_FACE])
    down_y = package(popul[:, :, 0], [f[3] for f in Y_FACE])
    up_y = jnp.concatenate([up_y, field[:, :, 62], field[:, :, 63]])
    down_y = jnp.concatenate([down_y, field[:, :, 0], field[:, :, 1]])
    before = ring(up_y, "gy", 1)
    after = ring(down_y, "gy", -1)
    y_side = jnp.concatenate([after[:9], before[:9]], axis=-1)
    field_y = jnp.concatenate(
        [
            before[9:12, :, None],
            before[12:, :, None],
            field,
            after[9:12, :, None],
            after[12:, :, None],
        ],
        axis=2,
    )
    zero = jnp.zeros((64,), F32)

    def package_x(x, numbers, slot):
        edge = popul[:, x]
        rows = package(edge, numbers)
        moments_low, moments_high = before[5:9, x], after[5:9, x]
        low = jnp.stack([zero, before[slot, x], zero, zero, zero] + list(moments_low))
        high = jnp.stack([zero, zero, after[slot, x], zero, zero] + list(moments_high))
        rows = jnp.concatenate([low[:, None], rows, high[:, None]], axis=1)
        return jnp.pad(rows, ((0, 0), (1, 1), (0, 0)))

    up_x = jnp.concatenate(
        [package_x(7, [f[2] for f in X_FACE], 1), field_y[:, 6], field_y[:, 7]]
    )
    down_x = jnp.concatenate(
        [package_x(0, [f[3] for f in X_FACE], 2), field_y[:, 0], field_y[:, 1]]
    )
    lower = ring(up_x, "gx", 1)
    upper = ring(down_x, "gx", -1)
    x_side = jnp.concatenate([lower[:9], upper[:9]], axis=-1)
    x_side = jnp.pad(x_side, ((0, 0), (6, 6), (0, 0)))
    wide = jnp.concatenate(
        [
            lower[9:12, None],
            lower[12:, None],
            field_y,
            upper[9:12, None],
            upper[12:, None],
        ],
        axis=1,
    )
    wide = jnp.pad(wide, ((0, 0), (0, 0), (6, 6), (0, 0)), constant_values=1.0)
    wide = jnp.concatenate([wide, wide], axis=-1).reshape(36 * PITCH, 128)
    return wide, x_side, y_side


GROUPS = [[(2 * m + core) * GY + g for m in range(8) for g in range(GY)] for core in range(2)]


def exchange(rows, count):
    blocks = rows.reshape(64, 1, count * 128)
    blocks = lax.all_to_all(
        blocks, ("gx", "gy"), 0, 0, axis_index_groups=GROUPS, tiled=True
    )
    return blocks.reshape(64 * count, 128)


def on_device(populations, h_axial, h_transverse):
    t = tables()
    magnet, rows = call(
        first_kernel,
        [(3, 8, 4096), (64 * ROWS_FWD, 128)],
        [(1536, 128)],
        30_000_000,
        1_600_000,
    )(h_transverse, h_axial, t["fwd_z"])
    own = exchange(rows, ROWS_FWD)
    other = lax.ppermute(own, "gx", [(i, i ^ 1) for i in range(GX)])
    (rows,) = call(
        plane_kernel, [(64 * ROWS_BACK, 128)], [(128, 1536)], 400_000_000, 3_000_000
    )(
        own,
        other,
        t["fwd_x"],
        t["back_x"],
        t["even"],
        t["odd"],
        t["back_even"],
        t["back_odd"],
        t["wave_x"],
        t["wave_y"],
        t["wave_z"],
    )
    recv = exchange(rows, ROWS_BACK)
    applied = jnp.concatenate([h_transverse, h_axial[None]], axis=0)
    wide, x_side, y_side = neighbours(populations, applied)
    result, demag = call(
        cell_kernel,
        [(19, 8, 4096), (3, 8, 4096)],
        [
            (ROWS_BACK * 128, 128),
            (36 * PITCH, 128),
            (19, 34, 8, 128),
            (5, PITCH, 128),
            (5, PITCH, 128),
        ],
        60_000_000,
        8_000_000,
    )(recv, t["back_z"], wide, magnet, populations, x_side, y_side)
    return result, demag


def solution(mesh):
    placed = (P(None, "gx", "gy"), P("gx", "gy"), P(None, "gx", "gy"))
    return jax.shard_map(
        on_device,
        mesh=mesh,
        in_specs=placed,
        out_specs=(P(None, "gx", "gy"), P(None, "gx", "gy")),
        check_vma=False,
    )
```

time: 350 us -> 105 us (0.30)
  the two profiles are of different devices: /device:TPU:1 before, /device:TPU:0 now
where the time goes in v1:
time: 105 us; the launch traced here: 103 us
  local copies, waits for them, and re-layouts  38.9 us (37%)
  starting transfers between devices  25.6 us (24%)
  Pallas kernels  18.7 us (18%)
  other arithmetic  10.5 us (10%)
  waiting for transfers between devices  8.12 us (8%)
  between operations  1.25 us (1%)
    all_to_all x2, starting transfers between devices, exchange(): lax.all_to_all(blocks, ('gx', 'gy'), 0, 0, axis_index_groups=GROUPS, tile...  16.5 us
    pallas_call x1, Pallas kernels, on_device(): call(cell_kernel, [(19, 8, 4096), (3, 8, 4096)], [(ROWS_BACK * 128, 128),...  11.9 us
    unnamed x75, local copies, waits for them, and re-layouts  10.5 us
    ppermute x4, starting transfers between devices, ring(): lax.ppermute(values, axis, [(i, (i + step) % size) for i in range(size)])  9.06 us
    concatenate x1, local copies, waits for them, and re-layouts, neighbours(): jnp.concatenate([lower[9:12, None], lower[12:, None], field_y, upper[9:12...  8.52 us
    ppermute x4, waiting for transfers between devices, ring(): lax.ppermute(values, axis, [(i, (i + step) % size) for i in range(size)])  7.63 us
    reshape x1, local copies, waits for them, and re-layouts, neighbours(): popul = populations.reshape(19, 8, 64, 64)  5.45 us
    pallas_call x1, Pallas kernels, on_device(): call(plane_kernel, [(64 * ROWS_BACK, 128)], [(128, 1536)], 400000000, 300...  4.72 us
  transfers between devices with their start and end apart: 7, of which 3 were waited for; matrix products, arithmetic and copies ran while one was open for 34% of the time, Pallas kernels for 2%

profile of v1, /device:TPU:0, one launch (start us, length us, event | category | flops | bytes accessed | tf_op | source)
XLA Modules:
  0.0 103.1 jit_solution(5837207214574952623)
XLA Ops:
  0.7 5.4 %reshape.1506 = f32[19,8,64,64]{3,2,1,0:T(8,128)} reshape(f32[19,8,4096]{2,1,0:T(8,128)} %pop_ref.1) | data formatting | bytes 4980736 | tf_op jit(solution)/shard_map/reshape | solution.py:471
  6.1 1.1 %fusion.99 = (f32[1,8,1,64]{3,2,1,0:T(1,128)S(1)}, f32[1,8,1,64]{3,2,1,0:T(1,128)S(1)}, f32[1,8,1,64]{3,2,1,0:T(1,128)S(1)}, f32[1,8,1,64]{3,2,1,0:T(1,128)S(1)}...) fusion(f32[19,8,64,64]{3,2,1,0:T(8,128)} %reshape.1506), kind=kLoop, calls=%fused_computation.241 | loop fusion | bytes 77824 | tf_op jit(solution)/shard_map/slice | solution.py:465
  7.2 1.1 %fusion.100 = (f32[1,8,1,64]{3,2,1,0:T(1,128)S(1)}, f32[1,8,1,64]{3,2,1,0:T(1,128)S(1)}, f32[1,8,1,64]{3,2,1,0:T(1,128)S(1)}, f32[1,8,1,64]{3,2,1,0:T(1,128)S(1)...) fusion(f32[19,8,64,64]{3,2,1,0:T(8,128)} %reshape.1506), kind=kLoop, calls=%fused_computation.242 | loop fusion | bytes 69632 | tf_op jit(solution)/shard_map/slice | solution.py:465
  8.3 1.4 %slice_reduce_fusion.2 = (f32[8,64]{1,0:T(8,128)S(1)}, f32[8,64]{1,0:T(8,128)S(1)}) fusion(f32[19,8,64,64]{3,2,1,0:T(8,128)} %reshape.1506), kind=kLoop, calls=%fused_computation.72 | loop fusion | flops 18432 | bytes 81920 | tf_op jit(solution)/shard_map/reduce_sum | solution.py:461
  10.8 4.0 %collective-permute-start.1 = (f32[15,8,64]{2,1,0:T(8,128)S(1)}, f32[15,8,64]{2,1,0:T(8,128)S(1)}, u32[]{:S(2)}, u32[]{:S(2)}) collective-permute-start(f32[15,8,64]{2,1,0:T(8,128)S(1)} %get-tuple-element.61), channel_id=1, source_target_pairs={{0,1},{1,2},{2,3},{3,4},{4,5},{5,6},{6,7},{7,0},{8,9},{9,10},{10,1... | collective-permute-start | bytes 92168 | tf_op jit(solution)/shard_map/ppermute | solution.py:457
  14.9 2.3 %collective-permute-start.2 = (f32[15,8,64]{2,1,0:T(8,128)S(1)}, f32[15,8,64]{2,1,0:T(8,128)S(1)}, u32[]{:S(2)}, u32[]{:S(2)}) collective-permute-start(f32[15,8,64]{2,1,0:T(8,128)S(1)} %get-tuple-element.60), channel_id=1, source_target_pairs={{0,7},{1,0},{2,1},{3,2},{4,3},{5,4},{6,5},{7,6},{8,15},{9,8},{10,9... | collective-permute-start | bytes 92168 | tf_op jit(solution)/shard_map/ppermute | solution.py:457
  17.1 2.1 %shard_map.149 = (f32[3,8,4096]{2,1,0:T(8,128)S(1)}, f32[768,128]{1,0:T(8,128)}) custom-call(f32[2,8,4096]{2,1,0:T(8,128)S(1)} %copy-done.2, f32[8,4096]{1,0:T(8,128)S(1)} %copy-done.3, f32[64,128]{1,0:T(8,128)S(1)} %copy-done.15), custom_call_target="tpu_custom_call" | custom-call | flops 30000000 | bytes 1600000 | tf_op jit(solution)/shard_map/pallas_call | solution.py:543
  20.0 8.8 %all-to-all-start = ((f32[64,1,1536]{2,1,0:T(1,128)}), f32[64,1,1536]{2,1,0:T(1,128)S(1)}, u32[]{:S(2)}, u32[]{:S(2)}) async-start(f32[64,1,1536]{2,1,0:T(1,128)} %bitcast), calls=%async_computation | async-start | bytes 786432 | tf_op jit(solution)/shard_map/all_to_all | solution.py:535
  29.6 1.4 %slice_reduce_fusion = (f32[64,64]{1,0:T(8,128)S(1)}, f32[64,64]{1,0:T(8,128)S(1)}) fusion(f32[19,8,64,64]{3,2,1,0:T(8,128)} %reshape.1506), kind=kLoop, calls=%fused_computation.1 | loop fusion | flops 147456 | bytes 655360 | tf_op jit(solution)/shard_map/reduce_sum | solution.py:461
  40.6 1.0 fusion.101
  41.7 1.0 copy.420
  42.7 2.3 %collective-permute-start.4 = (f32[15,68,64]{1,2,0:T(8,128)}, f32[15,68,64]{1,2,0:T(8,128)S(1)}, u32[]{:S(2)}, u32[]{:S(2)}) collective-permute-start(f32[15,68,64]{1,2,0:T(8,128)} %copy.420), channel_id=1, source_target_pairs={{0,120},{8,0},{16,8},{24,16},{32,24},{40,32},{48,40},{56,48},{64,5... | collective-permute-start | bytes 783368 | tf_op jit(solution)/shard_map/ppermute | solution.py:457
  45.2 1.0 select_maximum_fusion.3
  48.0 1.0 copy.414
  52.6 7.2 %collective-permute-done.3 = f32[15,68,64]{1,2,0:T(8,128)} collective-permute-done((f32[15,68,64]{1,2,0:T(8,128)}, f32[15,68,64]{1,2,0:T(8,128)}, u32[]{:S(2)}, u32[]{:S(2)}) %collective-permute-start.3) | collective-permute-done | bytes 261152 | tf_op jit(solution)/shard_map/ppermute | solution.py:457
  59.7 1.0 slice.804
  61.7 4.7 %shard_map.150 = f32[1280,128]{1,0:T(8,128)} custom-call(f32[768,128]{1,0:T(8,128)S(1)} %bitcast.601, f32[768,128]{1,0:T(8,128)S(1)} %collective-permute-done.other_ref, f32[2,128,128]{2,1,0:T(8,128)S(1)} %copy-done.10, f32[2,96,128]{2,1,0:T(8,128)S(1)} %copy-done.11, f32[256,256]{1,0:T(8,128)S(1)} %copy-done.8, f32[256,256]{1,0:T(8,128)S(1)} %copy-done.9, ...), custom_call_target="tpu_custom_call" | custom-call | flops 400000000 | bytes 3000000 | tf_op jit(solution)/shard_map/pallas_call | solution.py:552
  66.4 7.7 %all-to-all-start.1 = ((f32[64,1,2560]{2,1,0:T(1,128)}), f32[64,1,2560]{2,1,0:T(1,128)S(1)}, u32[]{:S(2)}, u32[]{:S(2)}) async-start(f32[64,1,2560]{2,1,0:T(1,128)} %bitcast.2), calls=%async_computation.1 | async-start | bytes 1310720 | tf_op jit(solution)/shard_map/all_to_all | solution.py:535
  75.3 1.0 slice_bitcast_fusion.2
  76.5 8.5 %concatenate.51 = f32[3,12,68,64]{3,1,0,2:T(8,128)S(1)} concatenate(f32[3,1,68,64]{3,1,0,2:T(1,128)S(1)} %copy.421, f32[3,1,68,64]{3,1,0,2:T(1,128)S(1)} %copy.422, f32[3,8,68,64]{3,1,0,2:T(8,128)} %copy-done.17, f32[3,1,68,64]{3,1,0,2:T(1,128)S(1)} %copy.423, f32[3,1,68,64]{3,1,0,2:T(1,128)S(1)} %copy.424), dimensions={1} | concatenate | bytes 1253376 | tf_op jit(solution)/shard_map/concatenate | solution.py:515
  85.8 1.6 %copy.425 = f32[3,12,80,128]{3,2,1,0:T(8,128)} copy(f32[3,12,80,128]{3,1,0,2:T(8,128)S(1)} %pad_maximum_fusion) | data formatting | bytes 2949120 | tf_op jit(solution)/shard_map/concatenate | solution.py:526
  88.1 1.4 %copy-done.1 = f32[3,12,80,128]{3,2,1,0:T(8,128)S(1)} copy-done((f32[3,12,80,128]{3,2,1,0:T(8,128)S(1)}, f32[3,12,80,128]{3,2,1,0:T(8,128)}, u32[]{:S(2)}) %copy-start.1) | copy-done | bytes 1474584
  89.4 1.0 copy-done.5
  91.2 11.9 %shard_map.151 = (f32[19,8,4096]{2,1,0:T(8,128)}, f32[3,8,4096]{2,1,0:T(8,128)}) custom-call(f32[1280,128]{1,0:T(8,128)S(1)} %bitcast.599, f32[64,128]{1,0:T(8,128)S(1)} %copy-done.13, f32[2880,128]{1,0:T(8,128)S(1)} %bitcast.598, f32[3,8,4096]{2,1,0:T(8,128)S(1)} %copy-done.5, f32[19,8,4096]{2,1,0:T(8,128)S(1)} %copy-done, ...), custom_call_target="tpu_custom_call" | custom-call | flops 60000000 | bytes 8000000 | tf_op jit(solution)/shard_map/pallas_call | solution.py:570
  (129 shorter events, 22.0 us)
Async XLA Ops:
  0.6 16.5 %copy-start.15 = (f32[64,128]{1,0:T(8,128)S(1)}, f32[64,128]{1,0:T(8,128)}, u32[]{:S(2)}) copy-start(f32[64,128]{1,0:T(8,128)} %constant.17.clone.table_ref) | copy-start | bytes 98308
  0.6 9.1 %copy-start.2 = (f32[2,8,4096]{2,1,0:T(8,128)S(1)}, f32[2,8,4096]{2,1,0:T(8,128)}, u32[]{:S(2)}) copy-start(f32[2,8,4096]{2,1,0:T(8,128)} %ht_ref.1) | copy-start | bytes 786436
  0.7 9.7 %copy-start.3 = (f32[8,4096]{1,0:T(8,128)S(1)}, f32[8,4096]{1,0:T(8,128)}, u32[]{:S(2)}) copy-start(f32[8,4096]{1,0:T(8,128)} %ha_ref.1) | copy-start | bytes 393220
  10.8 28.9 %collective-permute-start.1 = (f32[15,8,64]{2,1,0:T(8,128)S(1)}, f32[15,8,64]{2,1,0:T(8,128)S(1)}, u32[]{:S(2)}, u32[]{:S(2)}) collective-permute-start(f32[15,8,64]{2,1,0:T(8,128)S(1)} %get-tuple-element.61), channel_id=1, source_target_pairs={{0,1},{1,2},{2,3},{3,4},{4,5},{5,6},{6,7},{7,0},{8,9},{9,10},{10,1... | collective-permute-start | bytes 92168 | tf_op jit(solution)/shard_map/ppermute | solution.py:457
  14.9 24.9 %collective-permute-start.2 = (f32[15,8,64]{2,1,0:T(8,128)S(1)}, f32[15,8,64]{2,1,0:T(8,128)S(1)}, u32[]{:S(2)}, u32[]{:S(2)}) collective-permute-start(f32[15,8,64]{2,1,0:T(8,128)S(1)} %get-tuple-element.60), channel_id=1, source_target_pairs={{0,7},{1,0},{2,1},{3,2},{4,3},{5,4},{6,5},{7,6},{8,15},{9,8},{10,9... | collective-permute-start | bytes 92168 | tf_op jit(solution)/shard_map/ppermute | solution.py:457
  20.0 25.1 %all-to-all-start = ((f32[64,1,1536]{2,1,0:T(1,128)}), f32[64,1,1536]{2,1,0:T(1,128)S(1)}, u32[]{:S(2)}, u32[]{:S(2)}) async-start(f32[64,1,1536]{2,1,0:T(1,128)} %bitcast), calls=%async_computation | async-start | bytes 786432 | tf_op jit(solution)/shard_map/all_to_all | solution.py:535
  40.5 21.2 %copy-start.6 = (f32[256,384]{1,0:T(8,128)S(1)}, f32[256,384]{1,0:T(8,128)}, u32[]{:S(2)}) copy-start(f32[256,384]{1,0:T(8,128)} %constant.38.clone.back_even_ref) | copy-start | bytes 1179652
  40.5 21.2 %copy-start.7 = (f32[256,384]{1,0:T(8,128)S(1)}, f32[256,384]{1,0:T(8,128)}, u32[]{:S(2)}) copy-start(f32[256,384]{1,0:T(8,128)} %constant.39.clone.back_odd_ref) | copy-start | bytes 1179652
  40.5 21.2 %copy-start.8 = (f32[256,256]{1,0:T(8,128)S(1)}, f32[256,256]{1,0:T(8,128)}, u32[]{:S(2)}) copy-start(f32[256,256]{1,0:T(8,128)} %constant.36.clone.even_ref) | copy-start | bytes 786436
  40.5 21.2 %copy-start.9 = (f32[256,256]{1,0:T(8,128)S(1)}, f32[256,256]{1,0:T(8,128)}, u32[]{:S(2)}) copy-start(f32[256,256]{1,0:T(8,128)} %constant.37.clone.odd_ref) | copy-start | bytes 786436
  40.5 21.2 %copy-start.10 = (f32[2,128,128]{2,1,0:T(8,128)S(1)}, f32[2,128,128]{2,1,0:T(8,128)}, u32[]{:S(2)}) copy-start(f32[2,128,128]{2,1,0:T(8,128)} %constant.12.clone.fwd_x_ref) | copy-start | bytes 393220
  40.5 21.2 %copy-start.11 = (f32[2,96,128]{2,1,0:T(8,128)S(1)}, f32[2,96,128]{2,1,0:T(8,128)}, u32[]{:S(2)}) copy-start(f32[2,96,128]{2,1,0:T(8,128)} %constant.13.clone.back_x_ref) | copy-start | bytes 294916
  40.5 21.2 %copy-start.12 = (f32[128,128]{1,0:T(8,128)S(1)}, f32[128,128]{1,0:T(8,128)}, u32[]{:S(2)}) copy-start(f32[128,128]{1,0:T(8,128)} %constant.40.clone.wave_x_ref) | copy-start | bytes 196612
  40.5 21.2 %copy-start.14 = (f32[64,128]{1,0:T(8,128)S(1)}, f32[64,128]{1,0:T(8,128)}, u32[]{:S(2)}) copy-start(f32[64,128]{1,0:T(8,128)} %constant.42.clone.wave_z_ref) | copy-start | bytes 98308
  40.5 21.2 %copy-start.16 = (f32[2,256]{1,0:T(2,128)S(1)}, f32[2,256]{1,0:T(2,128)}, u32[]{:S(2)}) copy-start(f32[2,256]{1,0:T(2,128)} %constant.41.clone.wave_y_ref) | copy-start | bytes 6148
  42.7 8.9 %collective-permute-start.4 = (f32[15,68,64]{1,2,0:T(8,128)}, f32[15,68,64]{1,2,0:T(8,128)S(1)}, u32[]{:S(2)}, u32[]{:S(2)}) collective-permute-start(f32[15,68,64]{1,2,0:T(8,128)} %copy.420), channel_id=1, source_target_pairs={{0,120},{8,0},{16,8},{24,16},{32,24},{40,32},{48,40},{56,48},{64,5... | collective-permute-start | bytes 783368 | tf_op jit(solution)/shard_map/ppermute | solution.py:457
  45.1 16.6 %collective-permute-start = (f32[768,128]{1,0:T(8,128)S(1)}, f32[768,128]{1,0:T(8,128)S(1)}, u32[]{:S(2)}, u32[]{:S(2)}) collective-permute-start(f32[768,128]{1,0:T(8,128)S(1)} %bitcast.600), channel_id=1, source_target_pairs={{0,8},{8,0},{16,24},{24,16},{32,40},{40,32},{48,56},{56,48},{64,72... | collective-permute-start | bytes 1179656 | tf_op jit(solution)/shard_map/ppermute | solution.py:551
  49.1 10.7 %collective-permute-start.3 = (f32[15,68,64]{1,2,0:T(8,128)}, f32[15,68,64]{1,2,0:T(8,128)}, u32[]{:S(2)}, u32[]{:S(2)}) collective-permute-start(f32[15,68,64]{1,2,0:T(8,128)} %copy.414), channel_id=1, source_target_pairs={{0,8},{8,16},{16,24},{24,32},{32,40},{40,48},{48,56},{56,64},{64,7... | collective-permute-start | bytes 783368 | tf_op jit(solution)/shard_map/ppermute | solution.py:457
  51.6 14.8 %copy-start.20 = (f32[15,68,64]{1,2,0:T(8,128)}, f32[15,68,64]{1,2,0:T(8,128)S(1)}, u32[]{:S(2)}) copy-start(f32[15,68,64]{1,2,0:T(8,128)S(1)} %collective-permute-done.4) | copy-start | bytes 783364
  66.4 21.6 %all-to-all-start.1 = ((f32[64,1,2560]{2,1,0:T(1,128)}), f32[64,1,2560]{2,1,0:T(1,128)S(1)}, u32[]{:S(2)}, u32[]{:S(2)}) async-start(f32[64,1,2560]{2,1,0:T(1,128)} %bitcast.2), calls=%async_computation.1 | async-start | bytes 1310720 | tf_op jit(solution)/shard_map/all_to_all | solution.py:535
  85.1 2.3 %copy-start.18 = (f32[9,68,64]{2,1,0:T(8,128)S(1)}, f32[9,68,64]{2,1,0:T(8,128)}, u32[]{:S(2)}) copy-start(f32[9,68,64]{2,1,0:T(8,128)} %copy.469) | copy-start | bytes 470020
  85.1 2.3 %copy-start.19 = (f32[9,68,64]{2,1,0:T(8,128)S(1)}, f32[9,68,64]{2,1,0:T(8,128)}, u32[]{:S(2)}) copy-start(f32[9,68,64]{2,1,0:T(8,128)} %copy.468) | copy-start | bytes 470020
  85.2 2.8 %copy-start = (f32[19,8,4096]{2,1,0:T(8,128)S(1)}, f32[19,8,4096]{2,1,0:T(8,128)}, u32[]{:S(2)}) copy-start(f32[19,8,4096]{2,1,0:T(8,128)} %pop_ref.1) | copy-start | bytes 7471108
  88.1 1.4 %copy-start.1 = (f32[3,12,80,128]{3,2,1,0:T(8,128)S(1)}, f32[3,12,80,128]{3,2,1,0:T(8,128)}, u32[]{:S(2)}) copy-start(f32[3,12,80,128]{3,2,1,0:T(8,128)} %copy.425) | copy-start | bytes 4423684
  (7 other events, 5.8 us)

commit v2 on v1

v2 whole, which is shorter than its diff:
```python
import functools

import jax
import jax.numpy as jnp
import numpy as np
from jax import lax
from jax.experimental import pallas as pl
from jax.experimental.pallas import tpu as pltpu
from jax.sharding import PartitionSpec as P

NX, NY, NZ = 128, 512, 64
GX, GY = 16, 8
VELOCITIES = (
    (0, 0, 0),
    (1, 0, 0),
    (-1, 0, 0),
    (0, 1, 0),
    (0, -1, 0),
    (0, 0, 1),
    (0, 0, -1),
    (1, 1, 0),
    (-1, -1, 0),
    (1, -1, 0),
    (-1, 1, 0),
    (1, 0, 1),
    (-1, 0, -1),
    (1, 0, -1),
    (-1, 0, 1),
    (0, 1, 1),
    (0, -1, -1),
    (0, 1, -1),
    (0, -1, 1),
)
WEIGHTS = (1.0 / 3.0,) + (1.0 / 18.0,) * 6 + (1.0 / 36.0,) * 12
OMEGA = 1.0 / 0.6
HIGHEST = lax.Precision.HIGHEST
F32 = jnp.float32

X_FACE = ((0, 0, 1, 2), (1, 0, 7, 10), (-1, 0, 9, 8), (0, 1, 11, 14), (0, -1, 13, 12))
Y_FACE = ((0, 0, 3, 4), (1, 0, 7, 9), (-1, 0, 10, 8), (0, 1, 15, 18), (0, -1, 17, 16))
X_SLOT = {n: s for s, row in enumerate(X_FACE) for n in row[2:]}

ROWS_FWD = 12
ROWS_BACK = 20
CORNER = 480
FACE_ROWS = CORNER + 48
PITCH = 80


def cas(rows, cols, count):
    angle = 2.0 * np.pi * ((rows[:, None] * cols[None, :]) % count) / count
    return np.cos(angle) + np.sin(angle)


def wave(index, count):
    return 2.0 * np.sin(np.pi * index / count)


@functools.lru_cache(maxsize=None)
def tables():
    every_x, every_z = np.arange(NX), np.arange(NZ)
    half = np.arange(NY // 2)
    out = {}
    fwd_z = np.zeros((NZ, 128))
    fwd_z[:, :NZ] = cas(every_z, every_z, NZ)
    out["fwd_z"] = fwd_z
    out["back_z"] = np.tile(cas(every_z, every_z, NZ), (1, 2))
    fwd_x, back_x = [], []
    m = np.arange(8)
    for parity in range(2):
        order = []
        for side in (parity, 1 - parity):
            for x2 in range(2):
                for x4 in range(4):
                    order += list(8 * (2 * m + side) + 2 * x4 + x2)
        fwd_x.append(cas(every_x, np.array(order), NX))
        order = []
        for x2 in range(2):
            for x6 in range(6):
                order += list((8 * (2 * m + parity) - 2 + 2 * x6 + x2) % NX)
        back_x.append(cas(np.array(order), every_x, NX))
    out["fwd_x"] = np.stack(fwd_x)
    out["back_x"] = np.stack(back_x)
    even, odd = 2 * half, 2 * half + 1
    halo = np.array(
        [
            (64 * g + (-2, -1, 64, 65)[k]) % NY
            for g in range(GY)
            for c in range(4)
            for k in range(4)
        ]
    )
    out["even"] = cas(half, even, NY)
    out["odd"] = cas(half, odd, NY)
    out["back_even"] = np.concatenate([cas(even, half, NY), cas(even, halo, NY)], axis=1)
    out["back_odd"] = np.concatenate([cas(odd, half, NY), cas(odd, halo, NY)], axis=1)
    out["wave_x"] = np.repeat(wave(every_x, NX)[:, None], 128, axis=1)
    out["wave_y"] = np.stack([wave(even, NY), wave(odd, NY)])
    out["wave_z"] = np.repeat(wave(every_z, NZ)[:, None], 128, axis=1)
    return {name: np.asarray(value, np.float32) for name, value in out.items()}


def dot(a, b, dims=(1, 0)):
    return lax.dot_general(
        a, b, (((dims[0],), (dims[1],)), ((), ())), precision=HIGHEST, preferred_element_type=F32
    )


def langevin(hx, hy, hz):
    magnitude = jnp.sqrt(hx * hx + hy * hy + hz * hz)
    argument = 1.5 * magnitude
    decay = jnp.exp(-2.0 * argument)
    scale = ((1.0 + decay) / (1.0 - decay) - 1.0 / argument) / magnitude
    return hx * scale, hy * scale, hz * scale


def lanes(shape=(8, 128)):
    return lax.broadcasted_iota(jnp.int32, shape, len(shape) - 1)


def moments_of(popul):
    density = popul[0]
    for n in range(1, 19):
        density = density + popul[n]
    momentum = []
    for k in range(3):
        total = None
        for n in range(1, 19):
            if VELOCITIES[n][k] == 1:
                total = popul[n] if total is None else total + popul[n]
            elif VELOCITIES[n][k] == -1:
                total = total - popul[n]
        momentum.append(total)
    return density, momentum


def first_kernel(
    ht_ref, ha_ref, low_ref, high_ref, table_ref, magnet_ref, send_ref, up_ref, down_ref, rows_ref
):
    magnet = langevin(ht_ref[:256, :], ht_ref[256:, :], ha_ref[...])
    for c in range(3):
        magnet_ref[c * 256 : c * 256 + 256, :] = magnet[c]
        for pair in range(32):
            tile = magnet[c][pair * 8 : pair * 8 + 8, :]
            rows_ref[pl.ds(c * 512 + 2 * pair, 8, stride=64), :] = tile
            rows_ref[pl.ds(c * 512 + 2 * pair + 1, 8, stride=64), :] = pltpu.roll(tile, 64, 1)
    spectrum = dot(table_ref[...], rows_ref[...], (1, 1))
    for row in range(ROWS_FWD):
        send_ref[pl.ds(row, NZ, stride=ROWS_FWD), :] = spectrum[:, row * 128 : row * 128 + 128]
    for edge_ref, out_ref, which, pair in ((high_ref, up_ref, 2, 31), (low_ref, down_ref, 3, 0)):
        popul = [edge_ref[n, 0] for n in range(19)]
        density, momentum = moments_of(popul)
        tiles = [popul[face[which]] for face in Y_FACE] + [density] + momentum
        for ref, at in ((ht_ref, 0), (ht_ref, 256), (ha_ref, 0)):
            tiles.append(ref[at + pair * 8 : at + pair * 8 + 8, :])
        for k, tile in enumerate(tiles):
            out_ref[k * 8 : k * 8 + 8, :] = tile


def face_kernel(pop_ref, ht_ref, ha_ref, before_ref, after_ref, pair_ref, next_ref):
    parity = lax.rem(lax.axis_index("gx"), 2)
    for out_ref, up in ((pair_ref, parity == 0), (next_ref, parity == 1)):
        face = jnp.where(up, 7, 0)
        second = jnp.where(up, 6, 1)

        def line(ref, at):
            return ref[pl.ds(at, 32, stride=8), :]

        popul = [line(pop_ref, n * 256 + face) for n in range(19)]
        density, momentum = moments_of(popul)
        lines = [jnp.where(up, popul[f[2]], popul[f[3]]) for f in X_FACE] + [density] + momentum
        for x in (face, second):
            lines += [line(ht_ref, x), line(ht_ref, 256 + x), line(ha_ref, x)]
        for k, value in enumerate(lines):
            out_ref[k * 32 : k * 32 + 32, :] = value
        for ref, at in ((before_ref, CORNER), (after_ref, CORNER + 16)):
            out_ref[at : at + 16, :] = jnp.zeros((16, 128), F32)
            out_ref[at : at + 12, :] = ref[pl.ds(face, 12, stride=8), :]
        for ref, at in ((before_ref, CORNER + 32), (after_ref, CORNER + 40)):
            out_ref[at : at + 8, :] = jnp.zeros((8, 128), F32)
            out_ref[at : at + 3, :] = ref[pl.ds(72 + second, 3, stride=8), :]


def transpose_blocks(tiles):
    block = lanes() // 16
    for bit in (1, 2, 4):
        low = (block & bit) == 0
        out = list(tiles)
        for i in range(8):
            if i & bit == 0:
                a, b = tiles[i], tiles[i | bit]
                out[i] = jnp.where(low, a, pltpu.roll(b, 16 * bit, 1))
                out[i | bit] = jnp.where(low, pltpu.roll(a, 128 - 16 * bit, 1), b)
        tiles = out
    return tiles


def plane_kernel(
    own_ref,
    other_ref,
    fwd_x_ref,
    back_x_ref,
    even_ref,
    odd_ref,
    back_even_ref,
    back_odd_ref,
    wave_x_ref,
    wave_y_ref,
    wave_z_ref,
    send_ref,
    cells_ref,
):
    row = lax.axis_index("gx")
    parity = lax.rem(row, 2)
    index_z = (row // 2) * GY + lax.axis_index("gy")
    left = lanes() < 64
    for side, ref in enumerate((own_ref, other_ref)):
        for c in range(3):
            for pair in range(4):
                for x4 in range(4):
                    start = 2 * pair * ROWS_FWD + c * 4 + x4
                    a = ref[pl.ds(start, 8, stride=GY * ROWS_FWD), :]
                    b = ref[pl.ds(start + ROWS_FWD, 8, stride=GY * ROWS_FWD), :]
                    at = side * 64 + x4 * 8
                    col = c * 512 + pair * 128
                    cells_ref[at : at + 8, col : col + 128] = jnp.where(
                        left, a, pltpu.roll(b, 64, 1)
                    )
                    cells_ref[at + 32 : at + 40, col : col + 128] = jnp.where(
                        left, pltpu.roll(a, 64, 1), b
                    )
    wave_x = wave_x_ref[:, 0:1]
    wave_z = wave_z_ref[pl.ds(index_z, 1), 0:1]
    spectrum = dot(fwd_x_ref[parity], cells_ref[...])
    along = wave_x * spectrum[:, :512] + wave_z * spectrum[:, 1024:]
    both = jnp.concatenate([along, spectrum[:, 512:1024]], axis=0)
    parts = (
        dot(both[:, :256] + both[:, 256:], even_ref[...]),
        dot(both[:, :256] - both[:, 256:], odd_ref[...]),
    )
    back = []
    for which in range(2):
        wave_y = wave_y_ref[which : which + 1, :]
        squared = wave_x * wave_x + wave_y * wave_y + wave_z * wave_z
        anchor = squared == 0.0
        factor = jnp.where(
            anchor, 0.0, (-1.0 / (NX * NY * NZ)) / jnp.where(anchor, 1.0, squared)
        )
        potential = (parts[which][:128] + wave_y * parts[which][128:]) * factor
        stacked = jnp.concatenate([potential, wave_y * potential], axis=0)
        back.append(dot(stacked, (back_even_ref, back_odd_ref)[which][...]))
    low, high = back[0] + back[1], back[0] - back[1]
    column = lanes((128, 128)) % 16
    halo_p, halo_q = low[:128, 256:], low[128:, 256:]
    halo = jnp.where(
        column < 4,
        wave_x * halo_p,
        jnp.where(column < 8, halo_q, jnp.where(column < 12, wave_z * halo_p, 0.0)),
    )
    potential = jnp.concatenate([low[:128, :256], high[:128, :256]], axis=1)
    fields = jnp.concatenate(
        [wave_x * potential, low[128:, :256], high[128:, :256], wave_z * potential, halo], axis=1
    )
    cells = dot(back_x_ref[parity], fields)
    step = GY * ROWS_BACK
    for x6 in range(6):
        for c in range(3):
            for pair in range(4):
                col = c * 512 + pair * 128
                a = cells[x6 * 8 : x6 * 8 + 8, col : col + 128]
                b = cells[48 + x6 * 8 : 56 + x6 * 8, col : col + 128]
                at = 2 * pair * ROWS_BACK + c * 6 + x6
                send_ref[pl.ds(at, 8, stride=step), :] = jnp.where(left, a, pltpu.roll(b, 64, 1))
                send_ref[pl.ds(at + ROWS_BACK, 8, stride=step), :] = jnp.where(
                    left, pltpu.roll(a, 64, 1), b
                )
    for part in range(2):
        tiles = []
        for x in range(part * 8, part * 8 + 8):
            if x < 12:
                at = (x % 2) * 48 + (x // 2) * 8
                tiles.append(cells[at : at + 8, 1536:])
            else:
                tiles.append(jnp.zeros((8, 128), F32))
        for g, tile in enumerate(transpose_blocks(tiles)):
            send_ref[pl.ds(g * ROWS_BACK + 18 + part, 8, stride=step), :] = tile


def macroscopic(density, momentum, force):
    inverse = 1.0 / density
    vel = [(momentum[k] + 0.5 * force[k]) * inverse for k in range(3)]
    u_square = vel[0] * vel[0] + vel[1] * vel[1] + vel[2] * vel[2]
    u_dot_f = vel[0] * force[0] + vel[1] * force[1] + vel[2] * force[2]
    scaled = OMEGA * density
    base = scaled * (1.0 - 1.5 * u_square) - 0.5 * u_dot_f
    return vel, scaled, base


def along(lattice, vector):
    total = None
    for sign, value in zip(lattice, vector):
        if isinstance(sign, int):
            if sign == 0:
                continue
            term = value if sign == 1 else -value
        else:
            term = sign * value
        total = term if total is None else total + term
    return total


def relax_terms(lattice, vel, force, scaled, base):
    along_u = along(lattice, vel)
    along_f = along(lattice, force)
    even = base + along_u * (4.5 * scaled * along_u + 1.5 * along_f)
    odd = 3.0 * scaled * along_u + 0.5 * along_f
    return even, odd


def shift_z(tile, step, lane):
    if step == 0:
        return tile
    if step == 1:
        return jnp.where(lane % 64 == 0, pltpu.roll(tile, 65, 1), pltpu.roll(tile, 1, 1))
    return jnp.where(lane % 64 == 63, pltpu.roll(tile, 63, 1), pltpu.roll(tile, 127, 1))


def cell_kernel(
    recv_ref,
    table_ref,
    ht_ref,
    ha_ref,
    magnet_ref,
    pop_ref,
    pair_ref,
    next_ref,
    before_ref,
    after_ref,
    out_ref,
    demag_ref,
    field_ref,
    total_ref,
    post_ref,
    side_ref,
    enter_ref,
):
    lane = lanes()
    left = lane < 64
    left4 = lanes((32, 128)) < 64
    parity = lax.rem(lax.axis_index("gx"), 2)
    side_of = ((next_ref, pair_ref), (pair_ref, next_ref))

    def side(which, at, count):
        even, odd = side_of[which]
        return jnp.where(parity == 0, even[at : at + count, :], odd[at : at + count, :])

    def base(c, x):
        return (c * 12 + 2 + x) * PITCH + 8

    def both(tile):
        turned = pltpu.roll(tile, 64, 1)
        first = lanes(tile.shape) < 64
        return jnp.where(first, tile, turned), jnp.where(first, turned, tile)

    own = ((ht_ref, 0), (ht_ref, 256), (ha_ref, 0))
    for c in range(3):
        ref, at = own[c]
        for pair in range(32):
            for odd, tile in enumerate(both(ref[at + pair * 8 : at + pair * 8 + 8, :])):
                total_ref[pl.ds(base(c, 0) + 2 * pair + odd, 8, stride=PITCH), :] = tile
        for edge_ref, y in ((before_ref, -2), (after_ref, 64)):
            for odd, tile in enumerate(both(edge_ref[72 + c * 8 : 80 + c * 8, :])):
                total_ref[pl.ds(base(c, 0) + y + odd, 8, stride=PITCH), :] = tile
        for which, near, far in ((0, -1, -2), (1, 8, 9)):
            for x, k, corner in ((near, 9 + c, 9 + c), (far, 12 + c, 32 + c)):
                for odd, tile in enumerate(both(side(which, k * 32, 32))):
                    total_ref[pl.ds(base(c, x) + odd, 32, stride=2), :] = tile
                after = 16 if x == near else 8
                for y, at in ((-2, CORNER + corner), (64, CORNER + corner + after)):
                    for odd, tile in enumerate(both(side(which, at, 1))):
                        at_row = base(c, x) + y + odd
                        total_ref[at_row : at_row + 1, :] = tile

    for row in range(ROWS_BACK):
        spectrum = recv_ref[pl.ds(row, NZ, stride=ROWS_BACK), :]
        cells = dot(spectrum, table_ref[...], (0, 0))
        if row < 18:
            field_ref[row * 128 : row * 128 + 128, :] = cells
            for half in range(2):
                c, x = row // 6, 2 * (row % 6) + half - 2
                at = base(c, x)
                total_ref[at : at + 64, :] += cells[half * 64 : half * 64 + 64, :]
        else:
            for k in range(8):
                x = (row - 18) * 8 + k - 2
                if x < 10:
                    for c in range(3):
                        at, src = base(c, x), k * 16 + c * 4
                        total_ref[at - 2 : at, :] += cells[src : src + 2, :]
                        total_ref[at + 64 : at + 66, :] += cells[src + 2 : src + 4, :]

    def forces(magnet, read, first):
        force = []
        for c in range(3):
            d_x = jnp.where(first, *read(c, 1, 0)) - jnp.where(first, *read(c, -1, 0))
            d_y = jnp.where(first, *read(c, 0, 1)) - jnp.where(first, *read(c, 0, -1))
            a, b = read(c, 0, 0)
            d_z = jnp.where(first, pltpu.roll(a, 127, 1), pltpu.roll(b, 127, 1)) - jnp.where(
                first, pltpu.roll(a, 1, 1), pltpu.roll(b, 1, 1)
            )
            force.append(0.025 * (magnet[0] * d_x + magnet[1] * d_y + magnet[2] * d_z))
        return force

    def column(c, x, y):
        return total_ref[pl.ds(base(c, x) + y, 8, stride=PITCH), :]

    sign = jnp.where(left, -1.0, 1.0)
    values = [
        jnp.where(left, after_ref[k * 8 : k * 8 + 8, :], before_ref[k * 8 : k * 8 + 8, :])
        for k in range(12)
    ]
    force = forces(
        langevin(*values[9:]),
        lambda c, dx, dy: (column(c, dx, 64 + dy), column(c, dx, dy - 1)),
        left,
    )
    vel, scaled, rest = macroscopic(values[5], values[6:9], force)
    for slot, (cx, cz, up, down) in enumerate(Y_FACE):
        even, odd = relax_terms((cx, sign, cz), vel, force, scaled, rest)
        post = shift_z((1.0 - OMEGA) * values[slot] + WEIGHTS[up] * (even + odd), cz, lane)
        post_ref[up, 0] = post
        post_ref[down, 33] = post

    row = lax.broadcasted_iota(jnp.int32, (8, 128), 0)
    upper = row == 7

    def edge_rows(k_low, k_high):
        pair = []
        for which, k in ((0, k_low), (1, k_high)):
            value = jnp.where(
                left[:1], side(which, CORNER + 16 + k, 1), side(which, CORNER + k, 1)
            )
            pair.append(jnp.broadcast_to(value, (8, 128)))
        return jnp.where(upper, pair[1], pair[0])

    def corner(c, dx, y):
        return jnp.where(upper, column(c, 1 + dx, y), column(c, dx - 1, y))

    force = forces(
        langevin(*[edge_rows(k, k) for k in (9, 10, 11)]),
        lambda c, dx, dy: (corner(c, dx, 64 + dy), corner(c, dx, dy - 1)),
        left,
    )
    vel, scaled, rest = macroscopic(edge_rows(5, 5), [edge_rows(k, k) for k in (6, 7, 8)], force)
    even, odd = relax_terms((jnp.where(upper, -1.0, 1.0), sign, 0), vel, force, scaled, rest)
    edges = (1.0 - OMEGA) * edge_rows(1, 2) + WEIGHTS[7] * (even + odd)

    for which, x, step in ((0, -1, 1), (1, 8, -1)):

        def read(c, dx, dy):
            at = base(c, x + dx) + dy
            return (
                total_ref[pl.ds(at, 32, stride=2), :],
                total_ref[pl.ds(at + 1, 32, stride=2), :],
            )

        values = [side(which, k * 32, 32) for k in range(12)]
        force = forces(langevin(*values[9:]), read, left4)
        vel, scaled, rest = macroscopic(values[5], values[6:9], force)
        at_edge = 7 * which
        lane4 = lanes((32, 128))
        for slot, (cy, cz, up, down) in enumerate(X_FACE):
            even, odd = relax_terms((step, cy, cz), vel, force, scaled, rest)
            post = shift_z((1.0 - OMEGA) * values[slot] + WEIGHTS[up] * (even + odd), cz, lane4)
            if cy != 0:
                side_ref[8:40, :] = post
                if cy == 1:
                    side_ref[7:8, :] = edges[at_edge : at_edge + 1, :]
                    post = jnp.where(left4, post, side_ref[7:39, :])
                else:
                    side_ref[40:41, :] = edges[at_edge : at_edge + 1, :]
                    post = jnp.where(left4, side_ref[9:41, :], post)
                post = pltpu.roll(post, 64, 1)
            enter_ref[which, slot] = post

    def collide(pair, carry):
        ya = 2 * pair
        at = pl.multiple_of(pair * 8, 8)
        for c in range(3):
            src = (c * 12 + 2) * 64 + ya
            demag_ref[pl.ds(c * 256 + at, 8), :] = jnp.where(
                left,
                field_ref[pl.ds(src, 8, stride=64), :],
                field_ref[pl.ds(src + 1, 8, stride=64), :],
            )
        force = forces(
            [magnet_ref[pl.ds(c * 256 + at, 8), :] for c in range(3)],
            lambda c, dx, dy: (column(c, dx, ya + dy), column(c, dx, ya + 1 + dy)),
            left,
        )
        popul = [pop_ref[pl.ds(n * 256 + at, 8), :] for n in range(19)]
        density, momentum = moments_of(popul)
        vel, scaled, rest = macroscopic(density, momentum, force)
        post_ref[0, 1 + pair] = (1.0 - OMEGA) * popul[0] + WEIGHTS[0] * rest
        for n in range(1, 19, 2):
            even, odd = relax_terms(VELOCITIES[n], vel, force, scaled, rest)
            for number, value in ((n, even + odd), (n + 1, even - odd)):
                post = (1.0 - OMEGA) * popul[number] + WEIGHTS[n] * value
                post_ref[number, 1 + pair] = shift_z(post, VELOCITIES[number][2], lane)
        return carry

    lax.fori_loop(0, 32, collide, 0)

    def stream(pair, carry):
        at = pl.multiple_of(pair * 8, 8)
        for n in range(19):
            cx, cy, _ = VELOCITIES[n]
            tile = post_ref[n, 1 + pair]
            if cy == 1:
                tile = pltpu.roll(jnp.where(left, tile, post_ref[n, pair]), 64, 1)
            elif cy == -1:
                tile = pltpu.roll(jnp.where(left, post_ref[n, 2 + pair], tile), 64, 1)
            if cx != 0:
                enters = enter_ref[0 if cx == 1 else 1, X_SLOT[n], pl.ds(pair, 1), :]
                tile = jnp.where(
                    row == (0 if cx == 1 else 7),
                    jnp.broadcast_to(enters, (8, 128)),
                    pltpu.roll(tile, 1 if cx == 1 else 7, 0),
                )
            out_ref[pl.ds(n * 256 + at, 8), :] = tile
        return carry

    lax.fori_loop(0, 32, stream, 0)


def call(kernel, out, scratch, flops, moved, vmem, **more):
    return pl.pallas_call(
        kernel,
        out_shape=[jax.ShapeDtypeStruct(shape, F32) for shape in out],
        scratch_shapes=[pltpu.VMEM(shape, F32) for shape in scratch],
        compiler_params=pltpu.CompilerParams(vmem_limit_bytes=vmem * 1024 * 1024),
        cost_estimate=pl.CostEstimate(flops=flops, bytes_accessed=moved, transcendentals=0),
        **more,
    )


def ring(values, axis, step):
    size = lax.axis_size(axis)
    return lax.ppermute(values, axis, [(i, (i + step) % size) for i in range(size)])


GROUPS = [[(2 * m + core) * GY + g for m in range(8) for g in range(GY)] for core in range(2)]


def exchange(rows, count):
    blocks = rows.reshape(64, 1, count * 128)
    blocks = lax.all_to_all(
        blocks, ("gx", "gy"), 0, 0, axis_index_groups=GROUPS, tiled=True
    )
    return blocks.reshape(64 * count, 128)


def as_tiles(values):
    return values.reshape(-1, 8, 32, 128).transpose(0, 2, 1, 3)


def from_rows(rows):
    return rows.reshape(-1, 32, 8, 128).transpose(0, 2, 1, 3).reshape(-1, 8, 4096)


def on_device(populations, h_axial, h_transverse):
    t = tables()
    pop_tiles = as_tiles(populations)
    pop_rows = pop_tiles.reshape(19 * 256, 128)
    ht_rows = as_tiles(h_transverse).reshape(512, 128)
    ha_rows = as_tiles(h_axial).reshape(256, 128)
    whole = pl.BlockSpec(memory_space=pltpu.VMEM)
    magnet, rows, up, down = call(
        first_kernel,
        [(768, 128), (64 * ROWS_FWD, 128), (96, 128), (96, 128)],
        [(1536, 128)],
        30_000_000,
        1_800_000,
        8,
        grid=(1,),
        in_specs=[
            whole,
            whole,
            pl.BlockSpec((19, 1, 8, 128), lambda i: (0, 0, 0, 0)),
            pl.BlockSpec((19, 1, 8, 128), lambda i: (0, 31, 0, 0)),
            whole,
        ],
        out_specs=[whole] * 4,
    )(ht_rows, ha_rows, pop_tiles, pop_tiles, t["fwd_z"])
    own = exchange(rows, ROWS_FWD)
    before = ring(up, "gy", 1)
    after = ring(down, "gy", -1)
    to_pair, to_next = call(
        face_kernel,
        [(FACE_ROWS, 128), (FACE_ROWS, 128)],
        [],
        1_000_000,
        4_000_000,
        8,
    )(pop_rows, ht_rows, ha_rows, before, after)
    other = lax.ppermute(own, "gx", [(i, i ^ 1) for i in range(GX)])
    pair = lax.ppermute(to_pair, "gx", [(i, i ^ 1) for i in range(GX)])
    beyond = lax.ppermute(to_next, "gx", [(i, ((i + 1) ^ 1) - 1 & 15) for i in range(GX)])
    (rows,) = call(
        plane_kernel, [(64 * ROWS_BACK, 128)], [(128, 1536)], 400_000_000, 3_000_000, 16
    )(
        own,
        other,
        t["fwd_x"],
        t["back_x"],
        t["even"],
        t["odd"],
        t["back_even"],
        t["back_odd"],
        t["wave_x"],
        t["wave_y"],
        t["wave_z"],
    )
    recv = exchange(rows, ROWS_BACK)
    result, demag = call(
        cell_kernel,
        [(19 * 256, 128), (3 * 256, 128)],
        [
            (18 * 128, 128),
            (36 * PITCH, 128),
            (19, 34, 8, 128),
            (48, 128),
            (2, 5, 32, 128),
        ],
        60_000_000,
        8_000_000,
        24,
    )(recv, t["back_z"], ht_rows, ha_rows, magnet, pop_rows, pair, beyond, before, after)
    return from_rows(result), from_rows(demag)


def solution(mesh):
    placed = (P(None, "gx", "gy"), P("gx", "gy"), P(None, "gx", "gy"))
    return jax.shard_map(
        on_device,
        mesh=mesh,
        in_specs=placed,
        out_specs=(P(None, "gx", "gy"), P(None, "gx", "gy")),
        check_vma=False,
    )
```

time: 105 us -> 85.3 us (0.81)
  the two profiles are of different devices: /device:TPU:0 before, /device:TPU:1 now
where the time goes in v2:
time: 85.3 us; the launch traced here: 84.6 us
  blocking collectives  22.9 us (27%)
  Pallas kernels  17.7 us (21%)
  waiting for transfers between devices  17 us (20%)
  starting transfers between devices  14.2 us (17%)
  local copies, waits for them, and re-layouts  11.9 us (14%)
    all_to_all x1, blocking collectives, exchange(): lax.all_to_all(blocks, ('gx', 'gy'), 0, 0, axis_index_groups=GROUPS, tile...  22.9 us
    pallas_call x1, Pallas kernels, on_device(): call(cell_kernel, [(19 * 256, 128), (3 * 256, 128)], [(18 * 128, 128), (3...  12.3 us
    unnamed x60, local copies, waits for them, and re-layouts  11.9 us
    ppermute x2, waiting for transfers between devices, ring(): lax.ppermute(values, axis, [(i, (i + step) % size) for i in range(size)])  7.56 us
    ppermute x1, waiting for transfers between devices, on_device(): lax.ppermute(to_next, 'gx', [(i, (i + 1 ^ 1) - 1 & 15) for i in range(GX)])  6.9 us
    ppermute x2, starting transfers between devices, ring(): lax.ppermute(values, axis, [(i, (i + step) % size) for i in range(size)])  5.15 us
    all_to_all x1, starting transfers between devices, exchange(): lax.all_to_all(blocks, ('gx', 'gy'), 0, 0, axis_index_groups=GROUPS, tile...  4.77 us
    pallas_call x1, Pallas kernels, on_device(): call(plane_kernel, [(64 * ROWS_BACK, 128)], [(128, 1536)], 400000000, 300...  3.88 us
  transfers between devices with their start and end apart: 6, of which 4 were waited for; matrix products, arithmetic and copies ran while one was open for 0% of the time, Pallas kernels for 0%

profile of v2, /device:TPU:1, one launch (start us, length us, event | category | flops | bytes accessed | tf_op | source)
XLA Modules:
  0.0 84.6 jit_solution(15677261717465302918)
XLA Ops:
  0.6 1.7 %copy-done = f32[19,8,4096]{2,1,0:T(8,128)S(1)} copy-done((f32[19,8,4096]{2,1,0:T(8,128)S(1)}, f32[19,8,4096]{2,1,0:T(8,128)}, u32[]{:S(2)}) %copy-start) | copy-done | bytes 2490392
  2.3 0.9 %copy-done.3 = f32[2,8,4096]{2,1,0:T(8,128)S(1)} copy-done((f32[2,8,4096]{2,1,0:T(8,128)S(1)}, f32[2,8,4096]{2,1,0:T(8,128)}, u32[]{:S(2)}) %copy-start.3) | copy-done | bytes 262168
  3.3 0.9 %copy-done.5 = f32[8,4096]{1,0:T(8,128)S(1)} copy-done((f32[8,4096]{1,0:T(8,128)S(1)}, f32[8,4096]{1,0:T(8,128)}, u32[]{:S(2)}) %copy-start.5) | copy-done | bytes 131096
  4.2 0.8 copy-done.26
  5.0 1.4 %shard_map.149 = (f32[768,128]{1,0:T(8,128)S(1)}, f32[768,128]{1,0:T(8,128)S(1)}, f32[96,128]{1,0:T(8,128)S(1)}, f32[96,128]{1,0:T(8,128)S(1)}) custom-call(f32[512,128]{1,0:T(8,128)S(1)} %bitcast.35, f32[256,128]{1,0:T(8,128)S(1)} %bitcast.40, f32[19,32,8,128]{3,2,1,0:T(8,128)S(1)} %bitcast.29, f32[19,32,8,128]{3,2,1,0:T(8,128)S(1)} %bitcast.30, ...), custom_call_target="tpu_custom_call" | custom-call | flops 30000000 | bytes 1800000 | tf_op jit(solution)/shard_map/pallas_call | solution.py:578
  6.4 22.9 %all_to_all.10 = f32[64,1,1536]{2,1,0:T(1,128)S(1)} all-to-all(f32[64,1,1536]{2,1,0:T(1,128)S(1)} %bitcast.43), channel_id=1, replica_groups={{0,1,2,3,4,5,6,7,16,17,18,19,20,21,22,23,32,33,34,35,36,37,38,39,48,49,..., dimensions={0} | all-to-all | bytes 786432 | tf_op jit(solution)/shard_map/all_to_all | solution.py:557
  29.4 1.9 %collective-permute-start = (f32[768,128]{1,0:T(8,128)S(1)}, f32[768,128]{1,0:T(8,128)S(1)}, u32[]{:S(2)}, u32[]{:S(2)}) collective-permute-start(f32[768,128]{1,0:T(8,128)S(1)} %bitcast.38), channel_id=1, source_target_pairs={{0,8},{8,0},{16,24},{24,16},{32,40},{40,32},{48,56},{56,48},{64,72... | collective-permute-start | bytes 1179656 | tf_op jit(solution)/shard_map/ppermute | solution.py:606
  31.3 1.3 %collective-permute-done.other_ref = f32[768,128]{1,0:T(8,128)S(1)} collective-permute-done((f32[768,128]{1,0:T(8,128)S(1)}, f32[768,128]{1,0:T(8,128)S(1)}, u32[]{:S(2)}, u32[]{:S(2)}) %collective-permute-start) | collective-permute-done | bytes 393248 | tf_op jit(solution)/shard_map/ppermute | solution.py:606
  32.7 3.9 %shard_map.150 = f32[1280,128]{1,0:T(8,128)S(1)} custom-call(f32[768,128]{1,0:T(8,128)S(1)} %bitcast.39, f32[768,128]{1,0:T(8,128)S(1)} %collective-permute-done.other_ref, f32[2,128,128]{2,1,0:T(8,128)S(1)} %copy-done.21, f32[2,96,128]{2,1,0:T(8,128)S(1)} %copy-done.22, f32[256,256]{1,0:T(8,128)S(1)} %copy-done.16, f32[256,256]{1,0:T(8,128)S(1)} %copy-done.15, ...), custom_call_target="tpu_custom_call" | custom-call | flops 400000000 | bytes 3000000 | tf_op jit(solution)/shard_map/pallas_call | solution.py:609
  36.6 0.8 copy-done.2
  37.5 4.8 %all-to-all-start.1 = ((f32[64,1,2560]{2,1,0:T(1,128)}), f32[64,1,2560]{2,1,0:T(1,128)S(1)}, u32[]{:S(2)}, u32[]{:S(2)}) async-start(f32[64,1,2560]{2,1,0:T(1,128)} %bitcast.34), calls=%async_computation.1 | async-start | bytes 1310720 | tf_op jit(solution)/shard_map/all_to_all | solution.py:557
  42.2 2.6 %collective-permute-start.1 = (f32[96,128]{1,0:T(8,128)}, f32[96,128]{1,0:T(8,128)S(1)}, u32[]{:S(2)}, u32[]{:S(2)}) collective-permute-start(f32[96,128]{1,0:T(8,128)} %copy-done.29), channel_id=1, source_target_pairs={{0,1},{1,2},{2,3},{3,4},{4,5},{5,6},{6,7},{7,0},{8,9},{9,10},{10,1... | collective-permute-start | bytes 147464 | tf_op jit(solution)/shard_map/ppermute | solution.py:549
  44.8 2.6 %collective-permute-start.2 = (f32[96,128]{1,0:T(8,128)}, f32[96,128]{1,0:T(8,128)S(1)}, u32[]{:S(2)}, u32[]{:S(2)}) collective-permute-start(f32[96,128]{1,0:T(8,128)} %copy-done.28), channel_id=1, source_target_pairs={{0,7},{1,0},{2,1},{3,2},{4,3},{5,4},{6,5},{7,6},{8,15},{9,8},{10,9... | collective-permute-start | bytes 147464 | tf_op jit(solution)/shard_map/ppermute | solution.py:549
  47.4 7.6 %collective-permute-done.1.before_ref = f32[96,128]{1,0:T(8,128)S(1)} collective-permute-done((f32[96,128]{1,0:T(8,128)}, f32[96,128]{1,0:T(8,128)S(1)}, u32[]{:S(2)}, u32[]{:S(2)}) %collective-permute-start.1) | collective-permute-done | bytes 49184 | tf_op jit(solution)/shard_map/ppermute | solution.py:549
  55.2 2.4 %collective-permute-start.3 = (f32[528,128]{1,0:T(8,128)S(1)}, f32[528,128]{1,0:T(8,128)S(1)}, u32[]{:S(2)}, u32[]{:S(2)}) collective-permute-start(f32[528,128]{1,0:T(8,128)S(1)} %get-tuple-element.14), channel_id=1, source_target_pairs={{0,8},{8,0},{16,24},{24,16},{32,40},{40,32},{48,56},{56,48},{64,72... | collective-permute-start | bytes 811016 | tf_op jit(solution)/shard_map/ppermute | solution.py:607
  57.6 1.2 %collective-permute-done.3.pair_ref = f32[528,128]{1,0:T(8,128)S(1)} collective-permute-done((f32[528,128]{1,0:T(8,128)S(1)}, f32[528,128]{1,0:T(8,128)S(1)}, u32[]{:S(2)}, u32[]{:S(2)}) %collective-permute-start.3) | collective-permute-done | bytes 270368 | tf_op jit(solution)/shard_map/ppermute | solution.py:607
  59.5 6.9 %collective-permute-done.4.next_ref = f32[528,128]{1,0:T(8,128)S(1)} collective-permute-done((f32[528,128]{1,0:T(8,128)S(1)}, f32[528,128]{1,0:T(8,128)S(1)}, u32[]{:S(2)}, u32[]{:S(2)}) %collective-permute-start.4) | collective-permute-done | bytes 270368 | tf_op jit(solution)/shard_map/ppermute | solution.py:608
  67.1 1.0 %copy-done.8 = f32[768,128]{1,0:T(8,128)S(1)} copy-done((f32[768,128]{1,0:T(8,128)S(1)}, f32[768,128]{1,0:T(8,128)}, u32[]{:S(2)}) %copy-start.8) | copy-done | bytes 393240
  68.1 1.0 %copy-done.12 = f32[528,128]{1,0:T(8,128)S(1)} copy-done((f32[528,128]{1,0:T(8,128)S(1)}, f32[528,128]{1,0:T(8,128)}, u32[]{:S(2)}) %copy-start.12) | copy-done | bytes 270360
  69.1 1.0 %copy-done.14 = f32[528,128]{1,0:T(8,128)S(1)} copy-done((f32[528,128]{1,0:T(8,128)S(1)}, f32[528,128]{1,0:T(8,128)}, u32[]{:S(2)}) %copy-start.14) | copy-done | bytes 270360
  70.0 0.8 copy-done.18
  70.8 0.8 copy-done.20
  71.6 0.8 copy-done.24
  72.4 12.3 %shard_map.152 = (f32[4864,128]{1,0:T(8,128)}, f32[768,128]{1,0:T(8,128)}) custom-call(f32[1280,128]{1,0:T(8,128)S(1)} %bitcast.33, f32[64,128]{1,0:T(8,128)S(1)} %copy-done.24, f32[512,128]{1,0:T(8,128)S(1)} %bitcast.37, f32[256,128]{1,0:T(8,128)S(1)} %bitcast.42, f32[768,128]{1,0:T(8,128)S(1)} %copy-done.8, f32[4864,128]{1,0:T(8,128)S(1)} %bitcast.32, ...), custom_call_target="tpu_custom_call" | custom-call | flops 60000000 | bytes 8000000 | tf_op jit(solution)/shard_map/pallas_call | solution.py:625
  (53 shorter events, 1.8 us)
Async XLA Ops:
  0.6 1.7 %copy-start = (f32[19,8,4096]{2,1,0:T(8,128)S(1)}, f32[19,8,4096]{2,1,0:T(8,128)}, u32[]{:S(2)}) copy-start(f32[19,8,4096]{2,1,0:T(8,128)} %param.14) | copy-start | bytes 7471108
  4.9 27.7 %copy-start.9 = (f32[256,384]{1,0:T(8,128)S(1)}, f32[256,384]{1,0:T(8,128)}, u32[]{:S(2)}) copy-start(f32[256,384]{1,0:T(8,128)} %constant.28.clone.back_odd_ref) | copy-start | bytes 1179652
  5.0 27.7 %copy-start.10 = (f32[256,384]{1,0:T(8,128)S(1)}, f32[256,384]{1,0:T(8,128)}, u32[]{:S(2)}) copy-start(f32[256,384]{1,0:T(8,128)} %constant.27.clone.back_even_ref) | copy-start | bytes 1179652
  5.0 27.7 %copy-start.15 = (f32[256,256]{1,0:T(8,128)S(1)}, f32[256,256]{1,0:T(8,128)}, u32[]{:S(2)}) copy-start(f32[256,256]{1,0:T(8,128)} %constant.26.clone.odd_ref) | copy-start | bytes 786436
  5.0 27.7 %copy-start.16 = (f32[256,256]{1,0:T(8,128)S(1)}, f32[256,256]{1,0:T(8,128)}, u32[]{:S(2)}) copy-start(f32[256,256]{1,0:T(8,128)} %constant.25.clone.even_ref) | copy-start | bytes 786436
  5.0 27.7 %copy-start.21 = (f32[2,128,128]{2,1,0:T(8,128)S(1)}, f32[2,128,128]{2,1,0:T(8,128)}, u32[]{:S(2)}) copy-start(f32[2,128,128]{2,1,0:T(8,128)} %constant.23.clone.fwd_x_ref) | copy-start | bytes 393220
  5.0 27.7 %copy-start.22 = (f32[2,96,128]{2,1,0:T(8,128)S(1)}, f32[2,96,128]{2,1,0:T(8,128)}, u32[]{:S(2)}) copy-start(f32[2,96,128]{2,1,0:T(8,128)} %constant.24.clone.back_x_ref) | copy-start | bytes 294916
  5.0 27.7 %copy-start.23 = (f32[128,128]{1,0:T(8,128)S(1)}, f32[128,128]{1,0:T(8,128)}, u32[]{:S(2)}) copy-start(f32[128,128]{1,0:T(8,128)} %constant.29.clone.wave_x_ref) | copy-start | bytes 196612
  5.0 27.7 %copy-start.25 = (f32[64,128]{1,0:T(8,128)S(1)}, f32[64,128]{1,0:T(8,128)}, u32[]{:S(2)}) copy-start(f32[64,128]{1,0:T(8,128)} %constant.31.clone.wave_z_ref) | copy-start | bytes 98308
  5.0 27.7 %copy-start.27 = (f32[2,256]{1,0:T(2,128)S(1)}, f32[2,256]{1,0:T(2,128)}, u32[]{:S(2)}) copy-start(f32[2,256]{1,0:T(2,128)} %constant.30.clone.wave_y_ref) | copy-start | bytes 6148
  6.4 24.9 %copy-start.7 = (f32[768,128]{1,0:T(8,128)}, f32[768,128]{1,0:T(8,128)S(1)}, u32[]{:S(2)}) copy-start(f32[768,128]{1,0:T(8,128)S(1)} %get-tuple-element.11.magnet_ref) | copy-start | bytes 1179652
  6.4 24.9 %copy-start.28 = (f32[96,128]{1,0:T(8,128)}, f32[96,128]{1,0:T(8,128)S(1)}, u32[]{:S(2)}) copy-start(f32[96,128]{1,0:T(8,128)S(1)} %get-tuple-element.13) | copy-start | bytes 147460
  6.4 24.9 %copy-start.29 = (f32[96,128]{1,0:T(8,128)}, f32[96,128]{1,0:T(8,128)S(1)}, u32[]{:S(2)}) copy-start(f32[96,128]{1,0:T(8,128)S(1)} %get-tuple-element.12) | copy-start | bytes 147460
  6.4 48.6 %copy-start.1 = (f32[19,8,4096]{2,1,0:T(8,128)S(1)}, f32[19,8,4096]{2,1,0:T(8,128)}, u32[]{:S(2)}) copy-start(f32[19,8,4096]{2,1,0:T(8,128)} %param.14) | copy-start | bytes 7471108
  6.4 48.5 %copy-start.4 = (f32[2,8,4096]{2,1,0:T(8,128)S(1)}, f32[2,8,4096]{2,1,0:T(8,128)}, u32[]{:S(2)}) copy-start(f32[2,8,4096]{2,1,0:T(8,128)} %param.16) | copy-start | bytes 786436
  6.4 48.5 %copy-start.6 = (f32[8,4096]{1,0:T(8,128)S(1)}, f32[8,4096]{1,0:T(8,128)}, u32[]{:S(2)}) copy-start(f32[8,4096]{1,0:T(8,128)} %param.15) | copy-start | bytes 393220
  29.4 3.3 %collective-permute-start = (f32[768,128]{1,0:T(8,128)S(1)}, f32[768,128]{1,0:T(8,128)S(1)}, u32[]{:S(2)}, u32[]{:S(2)}) collective-permute-start(f32[768,128]{1,0:T(8,128)S(1)} %bitcast.38), channel_id=1, source_target_pairs={{0,8},{8,0},{16,24},{24,16},{32,40},{40,32},{48,56},{56,48},{64,72... | collective-permute-start | bytes 1179656 | tf_op jit(solution)/shard_map/ppermute | solution.py:606
  37.5 29.6 %all-to-all-start.1 = ((f32[64,1,2560]{2,1,0:T(1,128)}), f32[64,1,2560]{2,1,0:T(1,128)S(1)}, u32[]{:S(2)}, u32[]{:S(2)}) async-start(f32[64,1,2560]{2,1,0:T(1,128)} %bitcast.34), calls=%async_computation.1 | async-start | bytes 1310720 | tf_op jit(solution)/shard_map/all_to_all | solution.py:557
  42.2 12.7 %collective-permute-start.1 = (f32[96,128]{1,0:T(8,128)}, f32[96,128]{1,0:T(8,128)S(1)}, u32[]{:S(2)}, u32[]{:S(2)}) collective-permute-start(f32[96,128]{1,0:T(8,128)} %copy-done.29), channel_id=1, source_target_pairs={{0,1},{1,2},{2,3},{3,4},{4,5},{5,6},{6,7},{7,0},{8,9},{9,10},{10,1... | collective-permute-start | bytes 147464 | tf_op jit(solution)/shard_map/ppermute | solution.py:549
  44.8 10.1 %collective-permute-start.2 = (f32[96,128]{1,0:T(8,128)}, f32[96,128]{1,0:T(8,128)S(1)}, u32[]{:S(2)}, u32[]{:S(2)}) collective-permute-start(f32[96,128]{1,0:T(8,128)} %copy-done.28), channel_id=1, source_target_pairs={{0,7},{1,0},{2,1},{3,2},{4,3},{5,4},{6,5},{7,6},{8,15},{9,8},{10,9... | collective-permute-start | bytes 147464 | tf_op jit(solution)/shard_map/ppermute | solution.py:549
  55.0 3.8 %copy-start.17 = (f32[96,128]{1,0:T(8,128)}, f32[96,128]{1,0:T(8,128)S(1)}, u32[]{:S(2)}) copy-start(f32[96,128]{1,0:T(8,128)S(1)} %collective-permute-done.1.before_ref) | copy-start | bytes 147460
  55.0 3.8 %copy-start.19 = (f32[96,128]{1,0:T(8,128)}, f32[96,128]{1,0:T(8,128)S(1)}, u32[]{:S(2)}) copy-start(f32[96,128]{1,0:T(8,128)S(1)} %collective-permute-done.2.after_ref) | copy-start | bytes 147460
  55.2 3.5 %collective-permute-start.3 = (f32[528,128]{1,0:T(8,128)S(1)}, f32[528,128]{1,0:T(8,128)S(1)}, u32[]{:S(2)}, u32[]{:S(2)}) collective-permute-start(f32[528,128]{1,0:T(8,128)S(1)} %get-tuple-element.14), channel_id=1, source_target_pairs={{0,8},{8,0},{16,24},{24,16},{32,40},{40,32},{48,56},{56,48},{64,72... | collective-permute-start | bytes 811016 | tf_op jit(solution)/shard_map/ppermute | solution.py:607
  57.6 8.8 %collective-permute-start.4 = (f32[528,128]{1,0:T(8,128)S(1)}, f32[528,128]{1,0:T(8,128)S(1)}, u32[]{:S(2)}, u32[]{:S(2)}) collective-permute-start(f32[528,128]{1,0:T(8,128)S(1)} %get-tuple-element.15), channel_id=1, source_target_pairs={{0,120},{8,16},{16,8},{24,32},{32,24},{40,48},{48,40},{56,64},{64,... | collective-permute-start | bytes 811016 | tf_op jit(solution)/shard_map/ppermute | solution.py:608
  (12 other events, 10.1 us)

commit v3 on v2

--- a/solution.py
+++ b/solution.py
@@ -134,21 +134,52 @@
     return density, momentum
 
 
+def start(*copies):
+    started = [pltpu.make_async_copy(*copy) for copy in copies]
+    for copy in started:
+        copy.start()
+    return started
+
+
 def first_kernel(
-    ht_ref, ha_ref, low_ref, high_ref, table_ref, magnet_ref, send_ref, up_ref, down_ref, rows_ref
+    ht_hbm,
+    ha_hbm,
+    pop_hbm,
+    table_hbm,
+    send_ref,
+    up_ref,
+    down_ref,
+    ht_ref,
+    ha_ref,
+    low_ref,
+    high_ref,
+    table_ref,
+    rows_ref,
+    sems,
 ):
+    copies = start(
+        (ht_hbm, ht_ref, sems.at[0]),
+        (ha_hbm, ha_ref, sems.at[1]),
+        (table_hbm, table_ref, sems.at[2]),
+        (pop_hbm.at[:, 0], low_ref, sems.at[3]),
+        (pop_hbm.at[:, 31], high_ref, sems.at[4]),
+    )
+    copies[0].wait()
+    copies[1].wait()
     magnet = langevin(ht_ref[:256, :], ht_ref[256:, :], ha_ref[...])
     for c in range(3):
-        magnet_ref[c * 256 : c * 256 + 256, :] = magnet[c]
         for pair in range(32):
             tile = magnet[c][pair * 8 : pair * 8 + 8, :]
             rows_ref[pl.ds(c * 512 + 2 * pair, 8, stride=64), :] = tile
             rows_ref[pl.ds(c * 512 + 2 * pair + 1, 8, stride=64), :] = pltpu.roll(tile, 64, 1)
+    copies[2].wait()
     spectrum = dot(table_ref[...], rows_ref[...], (1, 1))
     for row in range(ROWS_FWD):
         send_ref[pl.ds(row, NZ, stride=ROWS_FWD), :] = spectrum[:, row * 128 : row * 128 + 128]
+    copies[3].wait()
+    copies[4].wait()
     for edge_ref, out_ref, which, pair in ((high_ref, up_ref, 2, 31), (low_ref, down_ref, 3, 0)):
-        popul = [edge_ref[n, 0] for n in range(19)]
+        popul = [edge_ref[n] for n in range(19)]
         density, momentum = moments_of(popul)
         tiles = [popul[face[which]] for face in Y_FACE] + [density] + momentum
         for ref, at in ((ht_ref, 0), (ht_ref, 256), (ha_ref, 0)):
@@ -157,7 +188,29 @@
             out_ref[k * 8 : k * 8 + 8, :] = tile
 
 
-def face_kernel(pop_ref, ht_ref, ha_ref, before_ref, after_ref, pair_ref, next_ref):
+def face_kernel(
+    pop_hbm,
+    ht_hbm,
+    ha_hbm,
+    before_ref,
+    after_ref,
+    pair_ref,
+    next_ref,
+    magnet_ref,
+    pop_ref,
+    ht_ref,
+    ha_ref,
+    sems,
+):
+    copies = start(
+        (pop_hbm, pop_ref, sems.at[0]), (ht_hbm, ht_ref, sems.at[1]), (ha_hbm, ha_ref, sems.at[2])
+    )
+    copies[1].wait()
+    copies[2].wait()
+    magnet = langevin(ht_ref[:256, :], ht_ref[256:, :], ha_ref[...])
+    for c in range(3):
+        magnet_ref[c * 256 : c * 256 + 256, :] = magnet[c]
+    copies[0].wait()
     parity = lax.rem(lax.axis_index("gx"), 2)
     for out_ref, up in ((pair_ref, parity == 0), (next_ref, parity == 1)):
         face = jnp.where(up, 7, 0)
@@ -336,6 +389,8 @@
     next_ref,
     before_ref,
     after_ref,
+    out_hbm,
+    demag_hbm,
     out_ref,
     demag_ref,
     field_ref,
@@ -343,6 +398,7 @@
     post_ref,
     side_ref,
     enter_ref,
+    out_sems,
 ):
     lane = lanes()
     left = lane < 64
@@ -498,7 +554,7 @@
             lambda c, dx, dy: (column(c, dx, ya + dy), column(c, dx, ya + 1 + dy)),
             left,
         )
-        popul = [pop_ref[pl.ds(n * 256 + at, 8), :] for n in range(19)]
+        popul = [pop_ref[n, pl.ds(at, 8), :] for n in range(19)]
         density, momentum = moments_of(popul)
         vel, scaled, rest = macroscopic(density, momentum, force)
         post_ref[0, 1 + pair] = (1.0 - OMEGA) * popul[0] + WEIGHTS[0] * rest
@@ -509,7 +565,8 @@
                 post_ref[number, 1 + pair] = shift_z(post, VELOCITIES[number][2], lane)
         return carry
 
-    lax.fori_loop(0, 32, collide, 0)
+    lax.fori_loop(0, 32, collide, 0, unroll=4)
+    sent = start((demag_ref, demag_hbm, out_sems.at[4]))
 
     def stream(pair, carry):
         at = pl.multiple_of(pair * 8, 8)
@@ -527,20 +584,32 @@
                     jnp.broadcast_to(enters, (8, 128)),
                     pltpu.roll(tile, 1 if cx == 1 else 7, 0),
                 )
-            out_ref[pl.ds(n * 256 + at, 8), :] = tile
+            out_ref[n, pl.ds(at, 8), :] = tile
         return carry
 
-    lax.fori_loop(0, 32, stream, 0)
-
-
-def call(kernel, out, scratch, flops, moved, vmem, **more):
+    for part in range(4):
+        lax.fori_loop(8 * part, 8 * part + 8, stream, 0, unroll=4)
+        rows = pl.ds(64 * part, 64)
+        sent += start((out_ref.at[:, rows], out_hbm.at[:, rows], out_sems.at[part]))
+    for copy in sent:
+        copy.wait()
+
+
+HBM = pl.BlockSpec(memory_space=pltpu.HBM)
+ANY = pl.BlockSpec(memory_space=pl.ANY)
+VMEM = pl.BlockSpec(memory_space=pltpu.VMEM)
+
+
+def call(kernel, ins, outs, scratch, sems, flops, moved, vmem=60):
     return pl.pallas_call(
         kernel,
-        out_shape=[jax.ShapeDtypeStruct(shape, F32) for shape in out],
-        scratch_shapes=[pltpu.VMEM(shape, F32) for shape in scratch],
+        out_shape=[jax.ShapeDtypeStruct(shape, F32) for shape, _ in outs],
+        in_specs=ins,
+        out_specs=[spec for _, spec in outs],
+        scratch_shapes=[pltpu.VMEM(shape, F32) for shape in scratch]
+        + [pltpu.SemaphoreType.DMA((count,)) for count in sems],
         compiler_params=pltpu.CompilerParams(vmem_limit_bytes=vmem * 1024 * 1024),
         cost_estimate=pl.CostEstimate(flops=flops, bytes_accessed=moved, transcendentals=0),
-        **more,
     )
 
 
@@ -574,40 +643,39 @@
     pop_rows = pop_tiles.reshape(19 * 256, 128)
     ht_rows = as_tiles(h_transverse).reshape(512, 128)
     ha_rows = as_tiles(h_axial).reshape(256, 128)
-    whole = pl.BlockSpec(memory_space=pltpu.VMEM)
-    magnet, rows, up, down = call(
+    rows, up, down = call(
         first_kernel,
-        [(768, 128), (64 * ROWS_FWD, 128), (96, 128), (96, 128)],
-        [(1536, 128)],
+        [HBM] * 4,
+        [((64 * ROWS_FWD, 128), VMEM), ((96, 128), VMEM), ((96, 128), VMEM)],
+        [(512, 128), (256, 128), (19, 8, 128), (19, 8, 128), (64, 128), (1536, 128)],
+        [5],
         30_000_000,
         1_800_000,
-        8,
-        grid=(1,),
-        in_specs=[
-            whole,
-            whole,
-            pl.BlockSpec((19, 1, 8, 128), lambda i: (0, 0, 0, 0)),
-            pl.BlockSpec((19, 1, 8, 128), lambda i: (0, 31, 0, 0)),
-            whole,
-        ],
-        out_specs=[whole] * 4,
-    )(ht_rows, ha_rows, pop_tiles, pop_tiles, t["fwd_z"])
+    )(ht_rows, ha_rows, pop_tiles, t["fwd_z"])
     own = exchange(rows, ROWS_FWD)
     before = ring(up, "gy", 1)
     after = ring(down, "gy", -1)
-    to_pair, to_next = call(
+    to_pair, to_next, magnet = call(
         face_kernel,
-        [(FACE_ROWS, 128), (FACE_ROWS, 128)],
-        [],
+        [HBM, HBM, HBM, VMEM, VMEM],
+        [((FACE_ROWS, 128), VMEM), ((FACE_ROWS, 128), VMEM), ((768, 128), VMEM)],
+        [(19 * 256, 128), (512, 128), (256, 128)],
+        [3],
         1_000_000,
         4_000_000,
-        8,
     )(pop_rows, ht_rows, ha_rows, before, after)
-    other = lax.ppermute(own, "gx", [(i, i ^ 1) for i in range(GX)])
+    own, to_pair, to_next = lax.optimization_barrier((own, to_pair, to_next))
     pair = lax.ppermute(to_pair, "gx", [(i, i ^ 1) for i in range(GX)])
     beyond = lax.ppermute(to_next, "gx", [(i, ((i + 1) ^ 1) - 1 & 15) for i in range(GX)])
+    other = lax.ppermute(own, "gx", [(i, i ^ 1) for i in range(GX)])
     (rows,) = call(
-        plane_kernel, [(64 * ROWS_BACK, 128)], [(128, 1536)], 400_000_000, 3_000_000, 16
+        plane_kernel,
+        [VMEM] * 11,
+        [((64 * ROWS_BACK, 128), VMEM)],
+        [(128, 1536)],
+        [],
+        400_000_000,
+        3_000_000,
     )(
         own,
         other,
@@ -621,21 +689,37 @@
         t["wave_y"],
         t["wave_z"],
     )
+    rows, pair, beyond = lax.optimization_barrier((rows, pair, beyond))
     recv = exchange(rows, ROWS_BACK)
     result, demag = call(
         cell_kernel,
-        [(19 * 256, 128), (3 * 256, 128)],
+        [VMEM] * 10,
+        [((19, 256, 128), HBM), ((3 * 256, 128), HBM)],
         [
+            (19, 256, 128),
+            (768, 128),
             (18 * 128, 128),
             (36 * PITCH, 128),
             (19, 34, 8, 128),
             (48, 128),
             (2, 5, 32, 128),
         ],
+        [5],
         60_000_000,
         8_000_000,
         24,
-    )(recv, t["back_z"], ht_rows, ha_rows, magnet, pop_rows, pair, beyond, before, after)
+    )(
+        recv,
+        t["back_z"],
+        ht_rows,
+        ha_rows,
+        magnet,
+        pop_rows.reshape(19, 256, 128),
+        pair,
+        beyond,
+        before,
+        after,
+    )
     return from_rows(result), from_rows(demag)
 
 

time: 85.3 us -> 70.7 us (0.83)
  local copies, waits for them, and re-layouts: 11.9 us -> 0.66 us
  waiting for transfers between devices: 17 us -> 8.75 us
  starting transfers between devices: 14.2 us -> 18.6 us
  Pallas kernels: 17.7 us -> 20.1 us
  blocking collectives: 22.9 us -> 20.8 us
    unnamed x60 -> x18, local copies, waits for them, and re-layouts: 11.9 us -> 0.66 us
    all_to_all x1, starting transfers between devices: 4.77 us -> 12.2 us  [exchange(): lax.all_to_all(blocks, ('gx', 'gy'), 0, 0, axis_index_groups=GROUPS, tile...]
    ppermute x1, waiting for transfers between devices: 6.9 us -> 1.11 us  [on_device(): lax.ppermute(to_next, 'gx', [(i, (i + 1 ^ 1) - 1 & 15) for i in range(GX)])]
    pallas_call x4, Pallas kernels: 17.7 us -> 20.1 us  [the longest x1 6.68 us: on_device(): call(cell_kernel, [VMEM] * 10, [((19, 256, 128), HBM), ((3 * 256, 128), H...]
    ppermute x1, starting transfers between devices: 2.37 us -> 0.09 us  [on_device(): pair = lax.ppermute(to_pair, 'gx', [(i, i ^ 1) for i in range(GX)])]
    all_to_all x1, blocking collectives: 22.9 us -> 20.8 us  [exchange(): lax.all_to_all(blocks, ('gx', 'gy'), 0, 0, axis_index_groups=GROUPS, tile...]
    ppermute x1, starting transfers between devices: 1.93 us -> 0.71 us  [on_device(): other = lax.ppermute(own, 'gx', [(i, i ^ 1) for i in range(GX)])]
    ppermute x1, waiting for transfers between devices: 1.17 us -> 0.01 us  [on_device(): pair = lax.ppermute(to_pair, 'gx', [(i, i ^ 1) for i in range(GX)])]
  transfers between devices with their start and end apart: 6 -> 6, of which waited for: 4 -> 4; matrix products, arithmetic and copies ran while one was open for 0% -> 0% of each run, Pallas kernels for 0% -> 15%
where the time goes in v3:
time: 70.7 us; the launch traced here: 69.7 us
  blocking collectives  20.8 us (29%)
  Pallas kernels  20.1 us (28%)
  starting transfers between devices  18.6 us (26%)
  waiting for transfers between devices  8.75 us (12%)
  between operations  0.76 us (1%)
    all_to_all x1, blocking collectives, exchange(): lax.all_to_all(blocks, ('gx', 'gy'), 0, 0, axis_index_groups=GROUPS, tile...  20.8 us
    all_to_all x1, starting transfers between devices, exchange(): lax.all_to_all(blocks, ('gx', 'gy'), 0, 0, axis_index_groups=GROUPS, tile...  12.2 us
    pallas_call x1, Pallas kernels, on_device(): call(cell_kernel, [VMEM] * 10, [((19, 256, 128), HBM), ((3 * 256, 128), H...  6.68 us
    ppermute x2, waiting for transfers between devices, ring(): lax.ppermute(values, axis, [(i, (i + step) % size) for i in range(size)])  6.47 us
    pallas_call x1, Pallas kernels, on_device(): call(plane_kernel, [VMEM] * 11, [((64 * ROWS_BACK, 128), VMEM)], [(128, 1...  6.28 us
    ppermute x2, starting transfers between devices, ring(): lax.ppermute(values, axis, [(i, (i + step) % size) for i in range(size)])  5.15 us
    pallas_call x1, Pallas kernels, on_device(): call(face_kernel, [HBM, HBM, HBM, VMEM, VMEM], [((FACE_ROWS, 128), VMEM),...  3.86 us
    pallas_call x1, Pallas kernels, on_device(): call(first_kernel, [HBM] * 4, [((64 * ROWS_FWD, 128), VMEM), ((96, 128),...  3.29 us
  transfers between devices with their start and end apart: 6, of which 4 were waited for; matrix products, arithmetic and copies ran while one was open for 0% of the time, Pallas kernels for 15%

profile of v3, /device:TPU:1, one launch (start us, length us, event | category | flops | bytes accessed | tf_op | source)
XLA Modules:
  0.0 69.7 jit_solution(10385117330437610166)
XLA Ops:
  0.6 3.3 %shard_map.149 = (f32[768,128]{1,0:T(8,128)}, f32[96,128]{1,0:T(8,128)}, f32[96,128]{1,0:T(8,128)}) custom-call(f32[512,128]{1,0:T(8,128)} %bitcast.35, f32[256,128]{1,0:T(8,128)} %bitcast.38, f32[19,32,8,128]{3,2,1,0:T(8,128)} %bitcast.31, f32[64,128]{1,0:T(8,128)} %constant.22.clone.table_hbm), custom_call_target="tpu_custom_call" | custom-call | flops 30000000 | bytes 1800000 | tf_op jit(solution)/shard_map/pallas_call | solution.py:646
  3.9 12.2 %all-to-all-start = ((f32[64,1,1536]{2,1,0:T(1,128)}), f32[64,1,1536]{2,1,0:T(1,128)}, u32[]{:S(2)}, u32[]{:S(2)}) async-start(f32[64,1,1536]{2,1,0:T(1,128)} %bitcast.42), calls=%async_computation | async-start | bytes 786432 | tf_op jit(solution)/shard_map/all_to_all | solution.py:626
  16.1 2.5 %collective-permute-start = (f32[96,128]{1,0:T(8,128)}, f32[96,128]{1,0:T(8,128)S(1)}, u32[]{:S(2)}, u32[]{:S(2)}) collective-permute-start(f32[96,128]{1,0:T(8,128)} %get-tuple-element.17), channel_id=1, source_target_pairs={{0,1},{1,2},{2,3},{3,4},{4,5},{5,6},{6,7},{7,0},{8,9},{9,10},{10,1... | collective-permute-start | bytes 147464 | tf_op jit(solution)/shard_map/ppermute | solution.py:618
  18.7 2.6 %collective-permute-start.1 = (f32[96,128]{1,0:T(8,128)}, f32[96,128]{1,0:T(8,128)S(1)}, u32[]{:S(2)}, u32[]{:S(2)}) collective-permute-start(f32[96,128]{1,0:T(8,128)} %get-tuple-element.18), channel_id=1, source_target_pairs={{0,7},{1,0},{2,1},{3,2},{4,3},{5,4},{6,5},{7,6},{8,15},{9,8},{10,9... | collective-permute-start | bytes 147464 | tf_op jit(solution)/shard_map/ppermute | solution.py:618
  21.3 4.2 %collective-permute-done.before_ref = f32[96,128]{1,0:T(8,128)S(1)} collective-permute-done((f32[96,128]{1,0:T(8,128)}, f32[96,128]{1,0:T(8,128)S(1)}, u32[]{:S(2)}, u32[]{:S(2)}) %collective-permute-start) | collective-permute-done | bytes 49184 | tf_op jit(solution)/shard_map/ppermute | solution.py:618
  25.5 2.3 %collective-permute-done.1.after_ref = f32[96,128]{1,0:T(8,128)S(1)} collective-permute-done((f32[96,128]{1,0:T(8,128)}, f32[96,128]{1,0:T(8,128)S(1)}, u32[]{:S(2)}, u32[]{:S(2)}) %collective-permute-start.1) | collective-permute-done | bytes 49184 | tf_op jit(solution)/shard_map/ppermute | solution.py:618
  27.8 0.0 copy-done.4
  27.8 0.6 copy-done.6
  28.4 3.9 %shard_map.150 = (f32[528,128]{1,0:T(8,128)}, f32[528,128]{1,0:T(8,128)}, f32[768,128]{1,0:T(8,128)}) custom-call(f32[4864,128]{1,0:T(8,128)} %bitcast.32, f32[512,128]{1,0:T(8,128)} %bitcast.36, f32[256,128]{1,0:T(8,128)} %bitcast.39, f32[96,128]{1,0:T(8,128)} %copy-done.4, f32[96,128]{1,0:T(8,128)} %copy-done.6), custom_call_target="tpu_custom_call" | custom-call | flops 1000000 | bytes 4000000 | tf_op jit(solution)/shard_map/pallas_call | solution.py:658
  32.3 0.0 copy-start
  32.3 0.0 copy-start.1
  32.3 0.0 copy-start.2
  32.3 0.0 copy-start.8
  32.3 0.0 all-to-all-done
  32.3 0.7 %collective-permute-start.2 = (f32[768,128]{1,0:T(8,128)}, f32[768,128]{1,0:T(8,128)}, u32[]{:S(2)}, u32[]{:S(2)}) collective-permute-start(f32[768,128]{1,0:T(8,128)} %bitcast.9.own_ref), channel_id=1, source_target_pairs={{0,8},{8,0},{16,24},{24,16},{32,40},{40,32},{48,56},{56,48},{64,72... | collective-permute-start | bytes 1179656 | tf_op jit(solution)/shard_map/ppermute | solution.py:670
  33.1 0.1 collective-permute-start.3
  33.2 0.4 collective-permute-start.4
  33.6 1.2 %collective-permute-done.2.other_ref = f32[768,128]{1,0:T(8,128)} collective-permute-done((f32[768,128]{1,0:T(8,128)}, f32[768,128]{1,0:T(8,128)}, u32[]{:S(2)}, u32[]{:S(2)}) %collective-permute-start.2) | collective-permute-done | bytes 393248 | tf_op jit(solution)/shard_map/ppermute | solution.py:670
  34.7 6.3 %shard_map.151 = f32[1280,128]{1,0:T(8,128)} custom-call(f32[768,128]{1,0:T(8,128)} %bitcast.9.own_ref, f32[768,128]{1,0:T(8,128)} %collective-permute-done.2.other_ref, f32[2,128,128]{2,1,0:T(8,128)} %constant.23.clone.fwd_x_ref, f32[2,96,128]{2,1,0:T(8,128)} %constant.24.clone.back_x_ref, f32[256,256]{1,0:T(8,128)} %constant.25.clone.even_ref, ...), custom_call_target="tpu_custom_call" | custom-call | flops 400000000 | bytes 3000000 | tf_op jit(solution)/shard_map/pallas_call | solution.py:671
  41.0 0.0 collective-permute-done.3.pair_ref
  41.0 1.1 %collective-permute-done.4.next_ref = f32[528,128]{1,0:T(8,128)S(1)} collective-permute-done((f32[528,128]{1,0:T(8,128)}, f32[528,128]{1,0:T(8,128)S(1)}, u32[]{:S(2)}, u32[]{:S(2)}) %collective-permute-start.4) | collective-permute-done | bytes 270368 | tf_op jit(solution)/shard_map/ppermute | solution.py:669
  42.1 20.8 %all_to_all.10 = f32[64,1,2560]{2,1,0:T(1,128)S(1)} all-to-all(f32[64,1,2560]{2,1,0:T(1,128)} %bitcast.41), channel_id=1, replica_groups={{0,1,2,3,4,5,6,7,16,17,18,19,20,21,22,23,32,33,34,35,36,37,38,39,48,49,..., dimensions={0} | all-to-all | bytes 1310720 | tf_op jit(solution)/shard_map/all_to_all | solution.py:626
  62.9 0.0 copy-done.2
  63.0 6.7 %shard_map.152 = (f32[19,256,128]{2,1,0:T(8,128)}, f32[768,128]{1,0:T(8,128)}) custom-call(f32[1280,128]{1,0:T(8,128)S(1)} %bitcast.34, f32[64,128]{1,0:T(8,128)S(1)} %copy-done.8, f32[512,128]{1,0:T(8,128)S(1)} %bitcast.37, f32[256,128]{1,0:T(8,128)S(1)} %bitcast.40, f32[768,128]{1,0:T(8,128)S(1)} %copy-done.3, f32[19,256,128]{2,1,0:T(8,128)S(1)} %bitcast.33, ...), custom_call_target="tpu_custom_call" | custom-call | flops 60000000 | bytes 8000000 | tf_op jit(solution)/shard_map/pallas_call | solution.py:694
  (11 shorter events, 0.0 us)
Async XLA Ops:
  3.9 28.4 %all-to-all-start = ((f32[64,1,1536]{2,1,0:T(1,128)}), f32[64,1,1536]{2,1,0:T(1,128)}, u32[]{:S(2)}, u32[]{:S(2)}) async-start(f32[64,1,1536]{2,1,0:T(1,128)} %bitcast.42), calls=%async_computation | async-start | bytes 786432 | tf_op jit(solution)/shard_map/all_to_all | solution.py:626
  16.1 9.3 %collective-permute-start = (f32[96,128]{1,0:T(8,128)}, f32[96,128]{1,0:T(8,128)S(1)}, u32[]{:S(2)}, u32[]{:S(2)}) collective-permute-start(f32[96,128]{1,0:T(8,128)} %get-tuple-element.17), channel_id=1, source_target_pairs={{0,1},{1,2},{2,3},{3,4},{4,5},{5,6},{6,7},{7,0},{8,9},{9,10},{10,1... | collective-permute-start | bytes 147464 | tf_op jit(solution)/shard_map/ppermute | solution.py:618
  18.7 9.1 %collective-permute-start.1 = (f32[96,128]{1,0:T(8,128)}, f32[96,128]{1,0:T(8,128)S(1)}, u32[]{:S(2)}, u32[]{:S(2)}) collective-permute-start(f32[96,128]{1,0:T(8,128)} %get-tuple-element.18), channel_id=1, source_target_pairs={{0,7},{1,0},{2,1},{3,2},{4,3},{5,4},{6,5},{7,6},{8,15},{9,8},{10,9... | collective-permute-start | bytes 147464 | tf_op jit(solution)/shard_map/ppermute | solution.py:618
  25.5 2.3 %copy-start.4 = (f32[96,128]{1,0:T(8,128)}, f32[96,128]{1,0:T(8,128)S(1)}, u32[]{:S(2)}) copy-start(f32[96,128]{1,0:T(8,128)S(1)} %collective-permute-done.before_ref) | copy-start | bytes 147460
  27.8 0.6 copy-start.6
  32.3 30.7 %copy-start = (f32[19,8,4096]{2,1,0:T(8,128)S(1)}, f32[19,8,4096]{2,1,0:T(8,128)}, u32[]{:S(2)}) copy-start(f32[19,8,4096]{2,1,0:T(8,128)} %param.14) | copy-start | bytes 7471108
  32.3 30.7 %copy-start.1 = (f32[2,8,4096]{2,1,0:T(8,128)S(1)}, f32[2,8,4096]{2,1,0:T(8,128)}, u32[]{:S(2)}) copy-start(f32[2,8,4096]{2,1,0:T(8,128)} %param.16) | copy-start | bytes 786436
  32.3 30.7 %copy-start.2 = (f32[8,4096]{1,0:T(8,128)S(1)}, f32[8,4096]{1,0:T(8,128)}, u32[]{:S(2)}) copy-start(f32[8,4096]{1,0:T(8,128)} %param.15) | copy-start | bytes 393220
  32.3 30.7 %copy-start.3 = (f32[768,128]{1,0:T(8,128)S(1)}, f32[768,128]{1,0:T(8,128)}, u32[]{:S(2)}) copy-start(f32[768,128]{1,0:T(8,128)} %get-tuple-element.25.magnet_ref) | copy-start | bytes 1179652
  32.3 30.7 %copy-start.5 = (f32[96,128]{1,0:T(8,128)S(1)}, f32[96,128]{1,0:T(8,128)}, u32[]{:S(2)}) copy-start(f32[96,128]{1,0:T(8,128)} %copy-done.4) | copy-start | bytes 147460
  32.3 30.7 %copy-start.7 = (f32[96,128]{1,0:T(8,128)S(1)}, f32[96,128]{1,0:T(8,128)}, u32[]{:S(2)}) copy-start(f32[96,128]{1,0:T(8,128)} %copy-done.6) | copy-start | bytes 147460
  32.3 30.7 %copy-start.8 = (f32[64,128]{1,0:T(8,128)S(1)}, f32[64,128]{1,0:T(8,128)}, u32[]{:S(2)}) copy-start(f32[64,128]{1,0:T(8,128)} %constant.32.clone.table_ref) | copy-start | bytes 98308
  32.3 2.4 %collective-permute-start.2 = (f32[768,128]{1,0:T(8,128)}, f32[768,128]{1,0:T(8,128)}, u32[]{:S(2)}, u32[]{:S(2)}) collective-permute-start(f32[768,128]{1,0:T(8,128)} %bitcast.9.own_ref), channel_id=1, source_target_pairs={{0,8},{8,0},{16,24},{24,16},{32,40},{40,32},{48,56},{56,48},{64,72... | collective-permute-start | bytes 1179656 | tf_op jit(solution)/shard_map/ppermute | solution.py:670
  33.1 8.0 %collective-permute-start.3 = (f32[528,128]{1,0:T(8,128)}, f32[528,128]{1,0:T(8,128)S(1)}, u32[]{:S(2)}, u32[]{:S(2)}) collective-permute-start(f32[528,128]{1,0:T(8,128)} %get-tuple-element.22), channel_id=1, source_target_pairs={{0,8},{8,0},{16,24},{24,16},{32,40},{40,32},{48,56},{56,48},{64,72... | collective-permute-start | bytes 811016 | tf_op jit(solution)/shard_map/ppermute | solution.py:668
  33.2 9.0 %collective-permute-start.4 = (f32[528,128]{1,0:T(8,128)}, f32[528,128]{1,0:T(8,128)S(1)}, u32[]{:S(2)}, u32[]{:S(2)}) collective-permute-start(f32[528,128]{1,0:T(8,128)} %get-tuple-element.23), channel_id=1, source_target_pairs={{0,120},{8,16},{16,8},{24,32},{32,24},{40,48},{48,40},{56,64},{64,... | collective-permute-start | bytes 811016 | tf_op jit(solution)/shard_map/ppermute | solution.py:669

commit v4 on v3

--- a/solution.py
+++ b/solution.py
@@ -2,6 +2,7 @@
 
 import jax
 import jax.numpy as jnp
+import ml_dtypes
 import numpy as np
 from jax import lax
 from jax.experimental import pallas as pl
@@ -33,7 +34,6 @@
 )
 WEIGHTS = (1.0 / 3.0,) + (1.0 / 18.0,) * 6 + (1.0 / 36.0,) * 12
 OMEGA = 1.0 / 0.6
-HIGHEST = lax.Precision.HIGHEST
 F32 = jnp.float32
 
 X_FACE = ((0, 0, 1, 2), (1, 0, 7, 10), (-1, 0, 9, 8), (0, 1, 11, 14), (0, -1, 13, 12))
@@ -97,13 +97,42 @@
     out["wave_x"] = np.repeat(wave(every_x, NX)[:, None], 128, axis=1)
     out["wave_y"] = np.stack([wave(even, NY), wave(odd, NY)])
     out["wave_z"] = np.repeat(wave(every_z, NZ)[:, None], 128, axis=1)
-    return {name: np.asarray(value, np.float32) for name, value in out.items()}
-
-
-def dot(a, b, dims=(1, 0)):
-    return lax.dot_general(
-        a, b, (((dims[0],), (dims[1],)), ((), ())), precision=HIGHEST, preferred_element_type=F32
-    )
+    out = {name: np.asarray(value, np.float32) for name, value in out.items()}
+    for name, axis in SPLIT_TABLES.items():
+        high = out[name].astype(ml_dtypes.bfloat16)
+        low = (out[name] - high.astype(np.float32)).astype(ml_dtypes.bfloat16)
+        out[name] = np.concatenate([high, low, high], axis=axis)
+    return out
+
+
+SPLIT_TABLES = {
+    "fwd_z": 1,
+    "back_z": 0,
+    "fwd_x": 2,
+    "back_x": 2,
+    "even": 0,
+    "odd": 0,
+    "back_even": 0,
+    "back_odd": 0,
+}
+
+
+def terms(values, axis):
+    high = values.astype(jnp.bfloat16)
+    low = (values - high.astype(F32)).astype(jnp.bfloat16)
+    return jnp.concatenate([high, high, low], axis=axis)
+
+
+def product(a, b, dims):
+    return lax.dot_general(a, b, (((dims[0],), (dims[1],)), ((), ())), preferred_element_type=F32)
+
+
+def apply_left(table, values, axis=0):
+    return product(table, terms(values, axis), (1, axis))
+
+
+def apply_right(values, table, axis=1):
+    return product(terms(values, axis), table, (axis, 0))
 
 
 def langevin(hx, hy, hz):
@@ -141,76 +170,44 @@
     return started
 
 
-def first_kernel(
-    ht_hbm,
-    ha_hbm,
-    pop_hbm,
-    table_hbm,
-    send_ref,
-    up_ref,
-    down_ref,
-    ht_ref,
-    ha_ref,
-    low_ref,
-    high_ref,
-    table_ref,
-    rows_ref,
-    sems,
-):
+def edge_kernel(pop_hbm, ht_hbm, ha_hbm, up_ref, down_ref, pop_ref, sems):
     copies = start(
-        (ht_hbm, ht_ref, sems.at[0]),
-        (ha_hbm, ha_ref, sems.at[1]),
-        (table_hbm, table_ref, sems.at[2]),
-        (pop_hbm.at[:, 0], low_ref, sems.at[3]),
-        (pop_hbm.at[:, 31], high_ref, sems.at[4]),
-    )
-    copies[0].wait()
-    copies[1].wait()
+        (pop_hbm.at[:, 31], pop_ref.at[0], sems.at[0]),
+        (pop_hbm.at[:, 0], pop_ref.at[1], sems.at[1]),
+        (ht_hbm.at[pl.ds(31 * 8, 8)], up_ref.at[pl.ds(72, 8)], sems.at[2]),
+        (ht_hbm.at[pl.ds(256 + 31 * 8, 8)], up_ref.at[pl.ds(80, 8)], sems.at[3]),
+        (ha_hbm.at[pl.ds(31 * 8, 8)], up_ref.at[pl.ds(88, 8)], sems.at[4]),
+        (ht_hbm.at[pl.ds(0, 8)], down_ref.at[pl.ds(72, 8)], sems.at[5]),
+        (ht_hbm.at[pl.ds(256, 8)], down_ref.at[pl.ds(80, 8)], sems.at[6]),
+        (ha_hbm.at[pl.ds(0, 8)], down_ref.at[pl.ds(88, 8)], sems.at[7]),
+    )
+    for copy in copies:
+        copy.wait()
+    for side, (out_ref, which) in enumerate(((up_ref, 2), (down_ref, 3))):
+        popul = [pop_ref[side, n] for n in range(19)]
+        density, momentum = moments_of(popul)
+        for k, tile in enumerate([popul[face[which]] for face in Y_FACE] + [density] + momentum):
+            out_ref[k * 8 : k * 8 + 8, :] = tile
+
+
+def first_kernel(ht_ref, ha_ref, table_ref, send_ref, rows_ref):
     magnet = langevin(ht_ref[:256, :], ht_ref[256:, :], ha_ref[...])
     for c in range(3):
         for pair in range(32):
             tile = magnet[c][pair * 8 : pair * 8 + 8, :]
             rows_ref[pl.ds(c * 512 + 2 * pair, 8, stride=64), :] = tile
             rows_ref[pl.ds(c * 512 + 2 * pair + 1, 8, stride=64), :] = pltpu.roll(tile, 64, 1)
-    copies[2].wait()
-    spectrum = dot(table_ref[...], rows_ref[...], (1, 1))
+    spectrum = apply_left(table_ref[...], rows_ref[...], 1)
     for row in range(ROWS_FWD):
         send_ref[pl.ds(row, NZ, stride=ROWS_FWD), :] = spectrum[:, row * 128 : row * 128 + 128]
-    copies[3].wait()
-    copies[4].wait()
-    for edge_ref, out_ref, which, pair in ((high_ref, up_ref, 2, 31), (low_ref, down_ref, 3, 0)):
-        popul = [edge_ref[n] for n in range(19)]
-        density, momentum = moments_of(popul)
-        tiles = [popul[face[which]] for face in Y_FACE] + [density] + momentum
-        for ref, at in ((ht_ref, 0), (ht_ref, 256), (ha_ref, 0)):
-            tiles.append(ref[at + pair * 8 : at + pair * 8 + 8, :])
-        for k, tile in enumerate(tiles):
-            out_ref[k * 8 : k * 8 + 8, :] = tile
 
 
 def face_kernel(
-    pop_hbm,
-    ht_hbm,
-    ha_hbm,
-    before_ref,
-    after_ref,
-    pair_ref,
-    next_ref,
-    magnet_ref,
-    pop_ref,
-    ht_ref,
-    ha_ref,
-    sems,
+    pop_ref, ht_ref, ha_ref, before_ref, after_ref, pair_ref, next_ref, magnet_ref
 ):
-    copies = start(
-        (pop_hbm, pop_ref, sems.at[0]), (ht_hbm, ht_ref, sems.at[1]), (ha_hbm, ha_ref, sems.at[2])
-    )
-    copies[1].wait()
-    copies[2].wait()
     magnet = langevin(ht_ref[:256, :], ht_ref[256:, :], ha_ref[...])
     for c in range(3):
         magnet_ref[c * 256 : c * 256 + 256, :] = magnet[c]
-    copies[0].wait()
     parity = lax.rem(lax.axis_index("gx"), 2)
     for out_ref, up in ((pair_ref, parity == 0), (next_ref, parity == 1)):
         face = jnp.where(up, 7, 0)
@@ -284,12 +281,12 @@
                     )
     wave_x = wave_x_ref[:, 0:1]
     wave_z = wave_z_ref[pl.ds(index_z, 1), 0:1]
-    spectrum = dot(fwd_x_ref[parity], cells_ref[...])
+    spectrum = apply_left(fwd_x_ref[parity], cells_ref[...])
     along = wave_x * spectrum[:, :512] + wave_z * spectrum[:, 1024:]
     both = jnp.concatenate([along, spectrum[:, 512:1024]], axis=0)
     parts = (
-        dot(both[:, :256] + both[:, 256:], even_ref[...]),
-        dot(both[:, :256] - both[:, 256:], odd_ref[...]),
+        apply_right(both[:, :256] + both[:, 256:], even_ref[...]),
+        apply_right(both[:, :256] - both[:, 256:], odd_ref[...]),
     )
     back = []
     for which in range(2):
@@ -301,7 +298,7 @@
         )
         potential = (parts[which][:128] + wave_y * parts[which][128:]) * factor
         stacked = jnp.concatenate([potential, wave_y * potential], axis=0)
-        back.append(dot(stacked, (back_even_ref, back_odd_ref)[which][...]))
+        back.append(apply_right(stacked, (back_even_ref, back_odd_ref)[which][...]))
     low, high = back[0] + back[1], back[0] - back[1]
     column = lanes((128, 128)) % 16
     halo_p, halo_q = low[:128, 256:], low[128:, 256:]
@@ -314,7 +311,7 @@
     fields = jnp.concatenate(
         [wave_x * potential, low[128:, :256], high[128:, :256], wave_z * potential, halo], axis=1
     )
-    cells = dot(back_x_ref[parity], fields)
+    cells = apply_left(back_x_ref[parity], fields)
     step = GY * ROWS_BACK
     for x6 in range(6):
         for c in range(3):
@@ -439,7 +436,7 @@
 
     for row in range(ROWS_BACK):
         spectrum = recv_ref[pl.ds(row, NZ, stride=ROWS_BACK), :]
-        cells = dot(spectrum, table_ref[...], (0, 0))
+        cells = apply_right(spectrum, table_ref[...], 0)
         if row < 18:
             field_ref[row * 128 : row * 128 + 128, :] = cells
             for half in range(2):
@@ -588,7 +585,7 @@
         return carry
 
     for part in range(4):
-        lax.fori_loop(8 * part, 8 * part + 8, stream, 0, unroll=4)
+        lax.fori_loop(8 * part, 8 * part + 8, stream, 0, unroll=8)
         rows = pl.ds(64 * part, 64)
         sent += start((out_ref.at[:, rows], out_hbm.at[:, rows], out_sems.at[part]))
     for copy in sent:
@@ -643,39 +640,51 @@
     pop_rows = pop_tiles.reshape(19 * 256, 128)
     ht_rows = as_tiles(h_transverse).reshape(512, 128)
     ha_rows = as_tiles(h_axial).reshape(256, 128)
-    rows, up, down = call(
+    up, down = call(
+        edge_kernel,
+        [HBM] * 3,
+        [((96, 128), VMEM), ((96, 128), VMEM)],
+        [(2, 19, 8, 128)],
+        [8],
+        100_000,
+        300_000,
+    )(pop_tiles, ht_rows, ha_rows)
+    before = ring(up, "gy", 1)
+    after = ring(down, "gy", -1)
+    (rows,) = call(
         first_kernel,
-        [HBM] * 4,
-        [((64 * ROWS_FWD, 128), VMEM), ((96, 128), VMEM), ((96, 128), VMEM)],
-        [(512, 128), (256, 128), (19, 8, 128), (19, 8, 128), (64, 128), (1536, 128)],
-        [5],
+        [VMEM] * 3,
+        [((64 * ROWS_FWD, 128), VMEM)],
+        [(1536, 128)],
+        [],
         30_000_000,
         1_800_000,
-    )(ht_rows, ha_rows, pop_tiles, t["fwd_z"])
-    own = exchange(rows, ROWS_FWD)
-    before = ring(up, "gy", 1)
-    after = ring(down, "gy", -1)
+        8,
+    )(ht_rows, ha_rows, t["fwd_z"])
     to_pair, to_next, magnet = call(
         face_kernel,
-        [HBM, HBM, HBM, VMEM, VMEM],
+        [VMEM] * 5,
         [((FACE_ROWS, 128), VMEM), ((FACE_ROWS, 128), VMEM), ((768, 128), VMEM)],
-        [(19 * 256, 128), (512, 128), (256, 128)],
-        [3],
+        [],
+        [],
         1_000_000,
         4_000_000,
+        8,
     )(pop_rows, ht_rows, ha_rows, before, after)
-    own, to_pair, to_next = lax.optimization_barrier((own, to_pair, to_next))
+    rows, to_pair, to_next = lax.optimization_barrier((rows, to_pair, to_next))
+    own = exchange(rows, ROWS_FWD)
+    other = lax.ppermute(own, "gx", [(i, i ^ 1) for i in range(GX)])
     pair = lax.ppermute(to_pair, "gx", [(i, i ^ 1) for i in range(GX)])
     beyond = lax.ppermute(to_next, "gx", [(i, ((i + 1) ^ 1) - 1 & 15) for i in range(GX)])
-    other = lax.ppermute(own, "gx", [(i, i ^ 1) for i in range(GX)])
     (rows,) = call(
         plane_kernel,
         [VMEM] * 11,
         [((64 * ROWS_BACK, 128), VMEM)],
         [(128, 1536)],
         [],
-        400_000_000,
-        3_000_000,
+        1_000,
+        1_000,
+        16,
     )(
         own,
         other,

time: 70.7 us -> 68.8 us (0.973)
  blocking collectives: 20.8 us -> 37.4 us
  Pallas kernels: 20.1 us -> 11.5 us
  starting transfers between devices: 18.6 us -> 10.6 us
  waiting for transfers between devices: 8.75 us -> 7.19 us
    all_to_all x1 -> x2, blocking collectives: 20.8 us -> 37.4 us  [exchange(): lax.all_to_all(blocks, ('gx', 'gy'), 0, 0, axis_index_groups=GROUPS, tile...]
    all_to_all x1 -> x0, starting transfers between devices: 12.2 us -> none  [exchange(): lax.all_to_all(blocks, ('gx', 'gy'), 0, 0, axis_index_groups=GROUPS, tile...]
    ppermute x2, waiting for transfers between devices: 6.47 us -> 1.15 us  [ring(): lax.ppermute(values, axis, [(i, (i + step) % size) for i in range(size)])]
    pallas_call x2 -> x3, Pallas kernels: 7.15 us -> 3.1 us  [the longest x1 1.81 us: on_device(): call(edge_kernel, [HBM] * 3, [((96, 128), VMEM), ((96, 128), VMEM)], [(2,...]
    pallas_call x1, Pallas kernels: 6.28 us -> 2.37 us  [on_device(): call(plane_kernel, [VMEM] * 11, [((64 * ROWS_BACK, 128), VMEM)], [(128, 1...]
    ppermute x1, waiting for transfers between devices: 1.11 us -> 4.98 us  [on_device(): lax.ppermute(to_next, 'gx', [(i, (i + 1 ^ 1) - 1 & 15) for i in range(GX)])]
    ppermute x1, starting transfers between devices: 0.71 us -> 3.53 us  [on_device(): other = lax.ppermute(own, 'gx', [(i, i ^ 1) for i in range(GX)])]
    ppermute x2, starting transfers between devices: 5.15 us -> 6.77 us  [ring(): lax.ppermute(values, axis, [(i, (i + step) % size) for i in range(size)])]
  transfers between devices with their start and end apart: 6 -> 5, of which waited for: 4 -> 3; matrix products, arithmetic and copies ran while one was open for 0% -> 0% of each run, Pallas kernels for 15% -> 5%
where the time goes in v4:
time: 68.8 us; the launch traced here: 68.3 us
  blocking collectives  37.4 us (54%)
  Pallas kernels  11.5 us (17%)
  starting transfers between devices  10.6 us (15%)
  waiting for transfers between devices  7.19 us (10%)
  local copies, waits for them, and re-layouts  0.87 us (1%)
  between operations  0.81 us (1%)
    all_to_all x2, blocking collectives, exchange(): lax.all_to_all(blocks, ('gx', 'gy'), 0, 0, axis_index_groups=GROUPS, tile...  37.4 us
    ppermute x2, starting transfers between devices, ring(): lax.ppermute(values, axis, [(i, (i + step) % size) for i in range(size)])  6.77 us
    pallas_call x1, Pallas kernels, on_device(): call(cell_kernel, [VMEM] * 10, [((19, 256, 128), HBM), ((3 * 256, 128), H...  5.98 us
    ppermute x1, waiting for transfers between devices, on_device(): lax.ppermute(to_next, 'gx', [(i, (i + 1 ^ 1) - 1 & 15) for i in range(GX)])  4.98 us
    ppermute x1, starting transfers between devices, on_device(): other = lax.ppermute(own, 'gx', [(i, i ^ 1) for i in range(GX)])  3.53 us
    pallas_call x1, Pallas kernels, on_device(): call(plane_kernel, [VMEM] * 11, [((64 * ROWS_BACK, 128), VMEM)], [(128, 1...  2.37 us
    pallas_call x1, Pallas kernels, on_device(): call(edge_kernel, [HBM] * 3, [((96, 128), VMEM), ((96, 128), VMEM)], [(2,...  1.81 us
  transfers between devices with their start and end apart: 5, of which 3 were waited for; matrix products, arithmetic and copies ran while one was open for 0% of the time, Pallas kernels for 5%

profile of v4, /device:TPU:1, one launch (start us, length us, event | category | flops | bytes accessed | tf_op | source)
XLA Modules:
  0.0 68.3 jit_solution(4764419222178874881)
XLA Ops:
  0.7 0.0 copy-start.13
  0.7 1.8 %shard_map.150 = (f32[96,128]{1,0:T(8,128)}, f32[96,128]{1,0:T(8,128)}) custom-call(f32[19,32,8,128]{3,2,1,0:T(8,128)} %bitcast.31, f32[512,128]{1,0:T(8,128)} %bitcast.34, f32[256,128]{1,0:T(8,128)} %bitcast.40), custom_call_target="tpu_custom_call" | custom-call | flops 100000 | bytes 300000 | tf_op jit(solution)/shard_map/pallas_call | solution.py:643
  2.5 0.0 copy-start.3
  2.5 0.0 copy-start.4
  2.5 0.0 copy-start.5
  2.5 0.0 copy-start.6
  2.5 0.0 copy-start.7
  2.6 0.0 copy-start.8
  2.6 0.0 copy-start.9
  2.6 4.5 %collective-permute-start = (f32[96,128]{1,0:T(8,128)}, f32[96,128]{1,0:T(8,128)S(1)}, u32[]{:S(2)}, u32[]{:S(2)}) collective-permute-start(f32[96,128]{1,0:T(8,128)} %get-tuple-element.15), channel_id=1, source_target_pairs={{0,1},{1,2},{2,3},{3,4},{4,5},{5,6},{6,7},{7,0},{8,9},{9,10},{10,1... | collective-permute-start | bytes 147464 | tf_op jit(solution)/shard_map/ppermute | solution.py:615
  7.1 2.3 %collective-permute-start.1 = (f32[96,128]{1,0:T(8,128)}, f32[96,128]{1,0:T(8,128)S(1)}, u32[]{:S(2)}, u32[]{:S(2)}) collective-permute-start(f32[96,128]{1,0:T(8,128)} %get-tuple-element.16), channel_id=1, source_target_pairs={{0,7},{1,0},{2,1},{3,2},{4,3},{5,4},{6,5},{7,6},{8,15},{9,8},{10,9... | collective-permute-start | bytes 147464 | tf_op jit(solution)/shard_map/ppermute | solution.py:615
  9.4 0.8 %copy-done.11 = bf16[64,384]{1,0:T(8,128)(2,1)S(1)} copy-done((bf16[64,384]{1,0:T(8,128)(2,1)S(1)}, bf16[64,384]{1,0:T(8,128)(2,1)}, u32[]{:S(2)}) %copy-start.11) | copy-done | bytes 49176
  10.2 0.9 %shard_map.149 = f32[768,128]{1,0:T(8,128)S(1)} custom-call(f32[512,128]{1,0:T(8,128)S(1)} %bitcast.35, f32[256,128]{1,0:T(8,128)S(1)} %bitcast.41, bf16[64,384]{1,0:T(8,128)(2,1)S(1)} %copy-done.11), custom_call_target="tpu_custom_call" | custom-call | flops 30000000 | bytes 1800000 | tf_op jit(solution)/shard_map/pallas_call | solution.py:654
  11.1 1.2 %collective-permute-done.1.after_ref = f32[96,128]{1,0:T(8,128)S(1)} collective-permute-done((f32[96,128]{1,0:T(8,128)}, f32[96,128]{1,0:T(8,128)S(1)}, u32[]{:S(2)}, u32[]{:S(2)}) %collective-permute-start.1) | collective-permute-done | bytes 49184 | tf_op jit(solution)/shard_map/ppermute | solution.py:615
  12.3 0.4 shard_map.151
  12.6 18.9 %all_to_all.10 = f32[64,1,1536]{2,1,0:T(1,128)S(1)} all-to-all(f32[64,1,1536]{2,1,0:T(1,128)S(1)} %bitcast.46), channel_id=1, replica_groups={{0,1,2,3,4,5,6,7,16,17,18,19,20,21,22,23,32,33,34,35,36,37,38,39,48,49,..., dimensions={0} | all-to-all | bytes 786432 | tf_op jit(solution)/shard_map/all_to_all | solution.py:623
  31.5 3.5 %collective-permute-start.2 = (f32[768,128]{1,0:T(8,128)S(1)}, f32[768,128]{1,0:T(8,128)S(1)}, u32[]{:S(2)}, u32[]{:S(2)}) collective-permute-start(f32[768,128]{1,0:T(8,128)S(1)} %bitcast.44), channel_id=1, source_target_pairs={{0,8},{8,0},{16,24},{24,16},{32,40},{40,32},{48,56},{56,48},{64,72... | collective-permute-start | bytes 1179656 | tf_op jit(solution)/shard_map/ppermute | solution.py:676
  35.1 0.0 collective-permute-start.3
  35.1 0.3 collective-permute-start.4
  35.4 1.1 %collective-permute-done.2.other_ref = f32[768,128]{1,0:T(8,128)S(1)} collective-permute-done((f32[768,128]{1,0:T(8,128)S(1)}, f32[768,128]{1,0:T(8,128)S(1)}, u32[]{:S(2)}, u32[]{:S(2)}) %collective-permute-start.2) | collective-permute-done | bytes 393248 | tf_op jit(solution)/shard_map/ppermute | solution.py:676
  36.5 2.4 %shard_map.152 = f32[1280,128]{1,0:T(8,128)S(1)} custom-call(f32[768,128]{1,0:T(8,128)S(1)} %bitcast.45, f32[768,128]{1,0:T(8,128)S(1)} %collective-permute-done.2.other_ref, bf16[2,128,384]{2,1,0:T(8,128)(2,1)S(1)} %copy-done.7, bf16[2,96,384]{2,1,0:T(8,128)(2,1)S(1)} %copy-done.8, bf16[768,256]{1,0:T(8,128)(2,1)S(1)} %copy-done.6, ...), custom_call_target="tpu_custom_call" | custom-call | flops 1000 | bytes 1000 | tf_op jit(solution)/shard_map/pallas_call | solution.py:679
  38.9 5.0 %collective-permute-done.4.next_ref = f32[528,128]{1,0:T(8,128)S(1)} collective-permute-done((f32[528,128]{1,0:T(8,128)S(1)}, f32[528,128]{1,0:T(8,128)S(1)}, u32[]{:S(2)}, u32[]{:S(2)}) %collective-permute-start.4) | collective-permute-done | bytes 270368 | tf_op jit(solution)/shard_map/ppermute | solution.py:678
  43.8 18.5 %all_to_all.11 = f32[64,1,2560]{2,1,0:T(1,128)S(1)} all-to-all(f32[64,1,2560]{2,1,0:T(1,128)S(1)} %bitcast.38), channel_id=1, replica_groups={{0,1,2,3,4,5,6,7,16,17,18,19,20,21,22,23,32,33,34,35,36,37,38,39,48,49,..., dimensions={0} | all-to-all | bytes 1310720 | tf_op jit(solution)/shard_map/all_to_all | solution.py:623
  62.3 6.0 %shard_map.153 = (f32[19,256,128]{2,1,0:T(8,128)}, f32[768,128]{1,0:T(8,128)}) custom-call(f32[1280,128]{1,0:T(8,128)S(1)} %bitcast.39, bf16[192,128]{1,0:T(8,128)(2,1)S(1)} %copy-done.10, f32[512,128]{1,0:T(8,128)S(1)} %bitcast.37, f32[256,128]{1,0:T(8,128)S(1)} %bitcast.43, f32[768,128]{1,0:T(8,128)S(1)} %get-tuple-element.23.magnet_ref, ...), custom_call_target="tpu_custom_call" | custom-call | flops 60000000 | bytes 8000000 | tf_op jit(solution)/shard_map/pallas_call | solution.py:703
  (21 shorter events, 0.0 us)
Async XLA Ops:
  0.6 11.6 %copy-start = (f32[19,8,4096]{2,1,0:T(8,128)S(1)}, f32[19,8,4096]{2,1,0:T(8,128)}, u32[]{:S(2)}) copy-start(f32[19,8,4096]{2,1,0:T(8,128)} %param.14) | copy-start | bytes 7471108
  0.6 8.7 %copy-start.1 = (f32[2,8,4096]{2,1,0:T(8,128)S(1)}, f32[2,8,4096]{2,1,0:T(8,128)}, u32[]{:S(2)}) copy-start(f32[2,8,4096]{2,1,0:T(8,128)} %param.16) | copy-start | bytes 786436
  0.6 8.7 %copy-start.2 = (f32[8,4096]{1,0:T(8,128)S(1)}, f32[8,4096]{1,0:T(8,128)}, u32[]{:S(2)}) copy-start(f32[8,4096]{1,0:T(8,128)} %param.15) | copy-start | bytes 393220
  0.7 35.7 %copy-start.13 = (f32[2,256]{1,0:T(2,128)S(1)}, f32[2,256]{1,0:T(2,128)}, u32[]{:S(2)}) copy-start(f32[2,256]{1,0:T(2,128)} %constant.30.clone.wave_y_ref) | copy-start | bytes 6148
  2.5 33.9 %copy-start.3 = (bf16[768,384]{1,0:T(8,128)(2,1)S(1)}, bf16[768,384]{1,0:T(8,128)(2,1)}, u32[]{:S(2)}) copy-start(bf16[768,384]{1,0:T(8,128)(2,1)} %constant.28.clone.back_odd_ref) | copy-start | bytes 1769476
  2.5 33.9 %copy-start.4 = (bf16[768,384]{1,0:T(8,128)(2,1)S(1)}, bf16[768,384]{1,0:T(8,128)(2,1)}, u32[]{:S(2)}) copy-start(bf16[768,384]{1,0:T(8,128)(2,1)} %constant.27.clone.back_even_ref) | copy-start | bytes 1769476
  2.5 33.9 %copy-start.5 = (bf16[768,256]{1,0:T(8,128)(2,1)S(1)}, bf16[768,256]{1,0:T(8,128)(2,1)}, u32[]{:S(2)}) copy-start(bf16[768,256]{1,0:T(8,128)(2,1)} %constant.26.clone.odd_ref) | copy-start | bytes 1179652
  2.5 33.9 %copy-start.6 = (bf16[768,256]{1,0:T(8,128)(2,1)S(1)}, bf16[768,256]{1,0:T(8,128)(2,1)}, u32[]{:S(2)}) copy-start(bf16[768,256]{1,0:T(8,128)(2,1)} %constant.25.clone.even_ref) | copy-start | bytes 1179652
  2.5 33.9 %copy-start.7 = (bf16[2,128,384]{2,1,0:T(8,128)(2,1)S(1)}, bf16[2,128,384]{2,1,0:T(8,128)(2,1)}, u32[]{:S(2)}) copy-start(bf16[2,128,384]{2,1,0:T(8,128)(2,1)} %constant.23.clone.fwd_x_ref) | copy-start | bytes 589828
  2.6 33.9 %copy-start.8 = (bf16[2,96,384]{2,1,0:T(8,128)(2,1)S(1)}, bf16[2,96,384]{2,1,0:T(8,128)(2,1)}, u32[]{:S(2)}) copy-start(bf16[2,96,384]{2,1,0:T(8,128)(2,1)} %constant.24.clone.back_x_ref) | copy-start | bytes 442372
  2.6 33.9 %copy-start.9 = (f32[128,128]{1,0:T(8,128)S(1)}, f32[128,128]{1,0:T(8,128)}, u32[]{:S(2)}) copy-start(f32[128,128]{1,0:T(8,128)} %constant.29.clone.wave_x_ref) | copy-start | bytes 196612
  2.6 8.5 %collective-permute-start = (f32[96,128]{1,0:T(8,128)}, f32[96,128]{1,0:T(8,128)S(1)}, u32[]{:S(2)}, u32[]{:S(2)}) collective-permute-start(f32[96,128]{1,0:T(8,128)} %get-tuple-element.15), channel_id=1, source_target_pairs={{0,1},{1,2},{2,3},{3,4},{4,5},{5,6},{6,7},{7,0},{8,9},{9,10},{10,1... | collective-permute-start | bytes 147464 | tf_op jit(solution)/shard_map/ppermute | solution.py:615
  7.1 5.2 %collective-permute-start.1 = (f32[96,128]{1,0:T(8,128)}, f32[96,128]{1,0:T(8,128)S(1)}, u32[]{:S(2)}, u32[]{:S(2)}) collective-permute-start(f32[96,128]{1,0:T(8,128)} %get-tuple-element.16), channel_id=1, source_target_pairs={{0,7},{1,0},{2,1},{3,2},{4,3},{5,4},{6,5},{7,6},{8,15},{9,8},{10,9... | collective-permute-start | bytes 147464 | tf_op jit(solution)/shard_map/ppermute | solution.py:615
  9.4 0.8 %copy-start.11 = (bf16[64,384]{1,0:T(8,128)(2,1)S(1)}, bf16[64,384]{1,0:T(8,128)(2,1)}, u32[]{:S(2)}) copy-start(bf16[64,384]{1,0:T(8,128)(2,1)} %constant.22.clone.table_ref) | copy-start | bytes 147460
  10.2 26.3 %copy-start.12 = (f32[64,128]{1,0:T(8,128)S(1)}, f32[64,128]{1,0:T(8,128)}, u32[]{:S(2)}) copy-start(f32[64,128]{1,0:T(8,128)} %constant.31.clone.wave_z_ref) | copy-start | bytes 98308
  31.5 30.8 %copy-start.10 = (bf16[192,128]{1,0:T(8,128)(2,1)S(1)}, bf16[192,128]{1,0:T(8,128)(2,1)}, u32[]{:S(2)}) copy-start(bf16[192,128]{1,0:T(8,128)(2,1)} %constant.32.clone.table_ref) | copy-start | bytes 147460
  31.5 4.9 %collective-permute-start.2 = (f32[768,128]{1,0:T(8,128)S(1)}, f32[768,128]{1,0:T(8,128)S(1)}, u32[]{:S(2)}, u32[]{:S(2)}) collective-permute-start(f32[768,128]{1,0:T(8,128)S(1)} %bitcast.44), channel_id=1, source_target_pairs={{0,8},{8,0},{16,24},{24,16},{32,40},{40,32},{48,56},{56,48},{64,72... | collective-permute-start | bytes 1179656 | tf_op jit(solution)/shard_map/ppermute | solution.py:676
  35.1 3.8 %collective-permute-start.3 = (f32[528,128]{1,0:T(8,128)S(1)}, f32[528,128]{1,0:T(8,128)S(1)}, u32[]{:S(2)}, u32[]{:S(2)}) collective-permute-start(f32[528,128]{1,0:T(8,128)S(1)} %get-tuple-element.20), channel_id=1, source_target_pairs={{0,8},{8,0},{16,24},{24,16},{32,40},{40,32},{48,56},{56,48},{64,72... | collective-permute-start | bytes 811016 | tf_op jit(solution)/shard_map/ppermute | solution.py:677
  35.1 8.8 %collective-permute-start.4 = (f32[528,128]{1,0:T(8,128)S(1)}, f32[528,128]{1,0:T(8,128)S(1)}, u32[]{:S(2)}, u32[]{:S(2)}) collective-permute-start(f32[528,128]{1,0:T(8,128)S(1)} %get-tuple-element.21), channel_id=1, source_target_pairs={{0,120},{8,16},{16,8},{24,32},{32,24},{40,48},{48,40},{56,64},{64,... | collective-permute-start | bytes 811016 | tf_op jit(solution)/shard_map/ppermute | solution.py:678

commit v5 on v4

--- a/solution.py
+++ b/solution.py
@@ -44,7 +44,8 @@
 ROWS_BACK = 20
 CORNER = 480
 FACE_ROWS = CORNER + 48
-PITCH = 80
+PITCH = 69
+OWN_PITCH = 65
 
 
 def cas(rows, cols, count):
@@ -245,6 +246,21 @@
     return tiles
 
 
+def cells_kernel(recv_ref, cells_ref):
+    left = lanes() < 64
+    for c in range(3):
+        for pair in range(4):
+            for x4 in range(4):
+                start = 16 * pair * ROWS_FWD + c * 4 + x4
+                a = recv_ref[pl.ds(start, 8, stride=ROWS_FWD), :]
+                b = recv_ref[pl.ds(start + 8 * ROWS_FWD, 8, stride=ROWS_FWD), :]
+                at, col = x4 * 8, c * 512 + pair * 128
+                cells_ref[at : at + 8, col : col + 128] = jnp.where(left, a, pltpu.roll(b, 64, 1))
+                cells_ref[at + 32 : at + 40, col : col + 128] = jnp.where(
+                    left, pltpu.roll(a, 64, 1), b
+                )
+
+
 def plane_kernel(
     own_ref,
     other_ref,
@@ -258,30 +274,15 @@
     wave_y_ref,
     wave_z_ref,
     send_ref,
-    cells_ref,
 ):
     row = lax.axis_index("gx")
     parity = lax.rem(row, 2)
-    index_z = (row // 2) * GY + lax.axis_index("gy")
+    index_z = lax.axis_index("gy") * 8 + row // 2
     left = lanes() < 64
-    for side, ref in enumerate((own_ref, other_ref)):
-        for c in range(3):
-            for pair in range(4):
-                for x4 in range(4):
-                    start = 2 * pair * ROWS_FWD + c * 4 + x4
-                    a = ref[pl.ds(start, 8, stride=GY * ROWS_FWD), :]
-                    b = ref[pl.ds(start + ROWS_FWD, 8, stride=GY * ROWS_FWD), :]
-                    at = side * 64 + x4 * 8
-                    col = c * 512 + pair * 128
-                    cells_ref[at : at + 8, col : col + 128] = jnp.where(
-                        left, a, pltpu.roll(b, 64, 1)
-                    )
-                    cells_ref[at + 32 : at + 40, col : col + 128] = jnp.where(
-                        left, pltpu.roll(a, 64, 1), b
-                    )
     wave_x = wave_x_ref[:, 0:1]
     wave_z = wave_z_ref[pl.ds(index_z, 1), 0:1]
-    spectrum = apply_left(fwd_x_ref[parity], cells_ref[...])
+    cells = jnp.concatenate([own_ref[...], other_ref[...]], axis=0)
+    spectrum = apply_left(fwd_x_ref[parity], cells)
     along = wave_x * spectrum[:, :512] + wave_z * spectrum[:, 1024:]
     both = jnp.concatenate([along, spectrum[:, 512:1024]], axis=0)
     parts = (
@@ -312,16 +313,15 @@
         [wave_x * potential, low[128:, :256], high[128:, :256], wave_z * potential, halo], axis=1
     )
     cells = apply_left(back_x_ref[parity], fields)
-    step = GY * ROWS_BACK
     for x6 in range(6):
         for c in range(3):
             for pair in range(4):
                 col = c * 512 + pair * 128
                 a = cells[x6 * 8 : x6 * 8 + 8, col : col + 128]
                 b = cells[48 + x6 * 8 : 56 + x6 * 8, col : col + 128]
-                at = 2 * pair * ROWS_BACK + c * 6 + x6
-                send_ref[pl.ds(at, 8, stride=step), :] = jnp.where(left, a, pltpu.roll(b, 64, 1))
-                send_ref[pl.ds(at + ROWS_BACK, 8, stride=step), :] = jnp.where(
+                at = 16 * pair * ROWS_BACK + c * 6 + x6
+                send_ref[pl.ds(at, 8, stride=ROWS_BACK), :] = jnp.where(left, a, pltpu.roll(b, 64, 1))
+                send_ref[pl.ds(at + 8 * ROWS_BACK, 8, stride=ROWS_BACK), :] = jnp.where(
                     left, pltpu.roll(a, 64, 1), b
                 )
     for part in range(2):
@@ -333,7 +333,8 @@
             else:
                 tiles.append(jnp.zeros((8, 128), F32))
         for g, tile in enumerate(transpose_blocks(tiles)):
-            send_ref[pl.ds(g * ROWS_BACK + 18 + part, 8, stride=step), :] = tile
+            at = 8 * g * ROWS_BACK + 18 + part
+            send_ref[pl.ds(at, 8, stride=ROWS_BACK), :] = tile
 
 
 def macroscopic(density, momentum, force):
@@ -408,7 +409,7 @@
         return jnp.where(parity == 0, even[at : at + count, :], odd[at : at + count, :])
 
     def base(c, x):
-        return (c * 12 + 2 + x) * PITCH + 8
+        return (c * 12 + 2 + x) * PITCH + 2
 
     def both(tile):
         turned = pltpu.roll(tile, 64, 1)
@@ -438,11 +439,14 @@
         spectrum = recv_ref[pl.ds(row, NZ, stride=ROWS_BACK), :]
         cells = apply_right(spectrum, table_ref[...], 0)
         if row < 18:
-            field_ref[row * 128 : row * 128 + 128, :] = cells
             for half in range(2):
                 c, x = row // 6, 2 * (row % 6) + half - 2
                 at = base(c, x)
-                total_ref[at : at + 64, :] += cells[half * 64 : half * 64 + 64, :]
+                part = cells[half * 64 : half * 64 + 64, :]
+                total_ref[at : at + 64, :] += part
+                if 0 <= x < 8:
+                    at = (c * 8 + x) * OWN_PITCH
+                    field_ref[at : at + 64, :] = part
         else:
             for k in range(8):
                 x = (row - 18) * 8 + k - 2
@@ -540,11 +544,11 @@
         ya = 2 * pair
         at = pl.multiple_of(pair * 8, 8)
         for c in range(3):
-            src = (c * 12 + 2) * 64 + ya
+            src = c * 8 * OWN_PITCH + ya
             demag_ref[pl.ds(c * 256 + at, 8), :] = jnp.where(
                 left,
-                field_ref[pl.ds(src, 8, stride=64), :],
-                field_ref[pl.ds(src + 1, 8, stride=64), :],
+                field_ref[pl.ds(src, 8, stride=OWN_PITCH), :],
+                field_ref[pl.ds(src + 1, 8, stride=OWN_PITCH), :],
             )
         force = forces(
             [magnet_ref[pl.ds(c * 256 + at, 8), :] for c in range(3)],
@@ -615,7 +619,7 @@
     return lax.ppermute(values, axis, [(i, (i + step) % size) for i in range(size)])
 
 
-GROUPS = [[(2 * m + core) * GY + g for m in range(8) for g in range(GY)] for core in range(2)]
+GROUPS = [[(2 * m + core) * GY + g for g in range(GY) for m in range(8)] for core in range(2)]
 
 
 def exchange(rows, count):
@@ -673,6 +677,9 @@
     )(pop_rows, ht_rows, ha_rows, before, after)
     rows, to_pair, to_next = lax.optimization_barrier((rows, to_pair, to_next))
     own = exchange(rows, ROWS_FWD)
+    (own,) = call(
+        cells_kernel, [VMEM], [((64, 1536), VMEM)], [], [], 1_000, 40000000, 8
+    )(own)
     other = lax.ppermute(own, "gx", [(i, i ^ 1) for i in range(GX)])
     pair = lax.ppermute(to_pair, "gx", [(i, i ^ 1) for i in range(GX)])
     beyond = lax.ppermute(to_next, "gx", [(i, ((i + 1) ^ 1) - 1 & 15) for i in range(GX)])
@@ -680,7 +687,7 @@
         plane_kernel,
         [VMEM] * 11,
         [((64 * ROWS_BACK, 128), VMEM)],
-        [(128, 1536)],
+        [],
         [],
         1_000,
         1_000,
@@ -707,7 +714,7 @@
         [
             (19, 256, 128),
             (768, 128),
-            (18 * 128, 128),
+            (24 * OWN_PITCH, 128),
             (36 * PITCH, 128),
             (19, 34, 8, 128),
             (48, 128),

time: 68.8 us -> 67.5 us (0.981)
  Pallas kernels: 11.5 us -> 10.1 us
  blocking collectives: 37.4 us -> 36.4 us
    pallas_call x1, Pallas kernels: 5.98 us -> 5.01 us  [on_device(): call(cell_kernel, [VMEM] * 10, [((19, 256, 128), HBM), ((3 * 256, 128), H...]
    all_to_all x2, blocking collectives: 37.4 us -> 36.4 us  [exchange(): lax.all_to_all(blocks, ('gx', 'gy'), 0, 0, axis_index_groups=GROUPS, tile...]
    pallas_call x1 -> x2, Pallas kernels: 2.37 us -> 2.01 us  [the longest x1 1.84 us: on_device(): call(plane_kernel, [VMEM] * 11, [((64 * ROWS_BACK, 128), VMEM)], [], [],...]
  transfers between devices with their start and end apart: 5 -> 5, of which waited for: 3 -> 3; matrix products, arithmetic and copies ran while one was open for 0% -> 0% of each run, Pallas kernels for 5% -> 4%
where the time goes in v5:
time: 67.5 us; the launch traced here: 66.6 us
  blocking collectives  36.4 us (54%)
  starting transfers between devices  10.8 us (16%)
  Pallas kernels  10.1 us (15%)
  waiting for transfers between devices  7.5 us (11%)
  local copies, waits for them, and re-layouts  0.88 us (1%)
  between operations  0.83 us (1%)
    all_to_all x2, blocking collectives, exchange(): lax.all_to_all(blocks, ('gx', 'gy'), 0, 0, axis_index_groups=GROUPS, tile...  36.4 us
    ppermute x2, starting transfers between devices, ring(): lax.ppermute(values, axis, [(i, (i + step) % size) for i in range(size)])  6.77 us
    ppermute x1, waiting for transfers between devices, on_device(): lax.ppermute(to_next, 'gx', [(i, (i + 1 ^ 1) - 1 & 15) for i in range(GX)])  5.6 us
    pallas_call x1, Pallas kernels, on_device(): call(cell_kernel, [VMEM] * 10, [((19, 256, 128), HBM), ((3 * 256, 128), H...  5.01 us
    ppermute x1, starting transfers between devices, on_device(): other = lax.ppermute(own, 'gx', [(i, i ^ 1) for i in range(GX)])  3.55 us
    pallas_call x1, Pallas kernels, on_device(): call(plane_kernel, [VMEM] * 11, [((64 * ROWS_BACK, 128), VMEM)], [], [],...  1.84 us
    pallas_call x1, Pallas kernels, on_device(): call(edge_kernel, [HBM] * 3, [((96, 128), VMEM), ((96, 128), VMEM)], [(2,...  1.81 us
  transfers between devices with their start and end apart: 5, of which 3 were waited for; matrix products, arithmetic and copies ran while one was open for 0% of the time, Pallas kernels for 4%

profile of v5, /device:TPU:1, one launch (start us, length us, event | category | flops | bytes accessed | tf_op | source)
XLA Modules:
  0.0 66.6 jit_solution(8133996622742788910)
XLA Ops:
  0.7 1.8 %shard_map.150 = (f32[96,128]{1,0:T(8,128)}, f32[96,128]{1,0:T(8,128)}) custom-call(f32[19,32,8,128]{3,2,1,0:T(8,128)} %bitcast.31, f32[512,128]{1,0:T(8,128)} %bitcast.34, f32[256,128]{1,0:T(8,128)} %bitcast.40), custom_call_target="tpu_custom_call" | custom-call | flops 100000 | bytes 300000 | tf_op jit(solution)/shard_map/pallas_call | solution.py:647
  2.5 4.5 %collective-permute-start = (f32[96,128]{1,0:T(8,128)}, f32[96,128]{1,0:T(8,128)S(1)}, u32[]{:S(2)}, u32[]{:S(2)}) collective-permute-start(f32[96,128]{1,0:T(8,128)} %get-tuple-element.15), channel_id=1, source_target_pairs={{0,1},{1,2},{2,3},{3,4},{4,5},{5,6},{6,7},{7,0},{8,9},{9,10},{10,1... | collective-permute-start | bytes 147464 | tf_op jit(solution)/shard_map/ppermute | solution.py:619
  7.0 2.3 %collective-permute-start.1 = (f32[96,128]{1,0:T(8,128)}, f32[96,128]{1,0:T(8,128)S(1)}, u32[]{:S(2)}, u32[]{:S(2)}) collective-permute-start(f32[96,128]{1,0:T(8,128)} %get-tuple-element.16), channel_id=1, source_target_pairs={{0,7},{1,0},{2,1},{3,2},{4,3},{5,4},{6,5},{7,6},{8,15},{9,8},{10,9... | collective-permute-start | bytes 147464 | tf_op jit(solution)/shard_map/ppermute | solution.py:619
  9.3 0.8 %copy-done.11 = bf16[64,384]{1,0:T(8,128)(2,1)S(1)} copy-done((bf16[64,384]{1,0:T(8,128)(2,1)S(1)}, bf16[64,384]{1,0:T(8,128)(2,1)}, u32[]{:S(2)}) %copy-start.11) | copy-done | bytes 49176
  10.1 0.9 %shard_map.149 = f32[768,128]{1,0:T(8,128)S(1)} custom-call(f32[512,128]{1,0:T(8,128)S(1)} %bitcast.35, f32[256,128]{1,0:T(8,128)S(1)} %bitcast.41, bf16[64,384]{1,0:T(8,128)(2,1)S(1)} %copy-done.11), custom_call_target="tpu_custom_call" | custom-call | flops 30000000 | bytes 1800000 | tf_op jit(solution)/shard_map/pallas_call | solution.py:658
  11.0 0.0 copy-start.3
  11.0 0.0 copy-start.4
  11.0 0.0 copy-start.6
  11.0 0.0 copy-start.7
  11.1 0.0 copy-start.8
  11.1 0.0 copy-start.9
  11.1 0.0 copy-start.13
  11.1 1.0 %collective-permute-done.1.after_ref = f32[96,128]{1,0:T(8,128)S(1)} collective-permute-done((f32[96,128]{1,0:T(8,128)}, f32[96,128]{1,0:T(8,128)S(1)}, u32[]{:S(2)}, u32[]{:S(2)}) %collective-permute-start.1) | collective-permute-done | bytes 49184 | tf_op jit(solution)/shard_map/ppermute | solution.py:619
  12.2 0.4 shard_map.151
  12.5 19.0 %all_to_all.10 = f32[64,1,1536]{2,1,0:T(1,128)S(1)} all-to-all(f32[64,1,1536]{2,1,0:T(1,128)S(1)} %bitcast.44), channel_id=1, replica_groups={{0,16,32,48,64,80,96,112,1,17,33,49,65,81,97,113,2,18,34,50,66,82,98,11..., dimensions={0} | all-to-all | bytes 786432 | tf_op jit(solution)/shard_map/all_to_all | solution.py:627
  31.5 0.2 shard_map.152.own_ref
  31.7 3.5 %collective-permute-start.2 = (f32[64,1536]{1,0:T(8,128)S(1)}, f32[64,1536]{1,0:T(8,128)S(1)}, u32[]{:S(2)}, u32[]{:S(2)}) collective-permute-start(f32[64,1536]{1,0:T(8,128)S(1)} %shard_map.152.own_ref), channel_id=1, source_target_pairs={{0,8},{8,0},{16,24},{24,16},{32,40},{40,32},{48,56},{56,48},{64,72... | collective-permute-start | bytes 1179656 | tf_op jit(solution)/shard_map/ppermute | solution.py:683
  35.2 0.1 collective-permute-start.3
  35.3 0.4 collective-permute-start.4
  35.7 0.9 %collective-permute-done.2.other_ref = f32[64,1536]{1,0:T(8,128)S(1)} collective-permute-done((f32[64,1536]{1,0:T(8,128)S(1)}, f32[64,1536]{1,0:T(8,128)S(1)}, u32[]{:S(2)}, u32[]{:S(2)}) %collective-permute-start.2) | collective-permute-done | bytes 393248 | tf_op jit(solution)/shard_map/ppermute | solution.py:683
  36.6 1.8 %shard_map.153 = f32[1280,128]{1,0:T(8,128)S(1)} custom-call(f32[64,1536]{1,0:T(8,128)S(1)} %shard_map.152.own_ref, f32[64,1536]{1,0:T(8,128)S(1)} %collective-permute-done.2.other_ref, bf16[2,128,384]{2,1,0:T(8,128)(2,1)S(1)} %copy-done.7, bf16[2,96,384]{2,1,0:T(8,128)(2,1)S(1)} %copy-done.8, bf16[768,256]{1,0:T(8,128)(2,1)S(1)} %copy-done.6, ...), custom_call_target="tpu_custom_call" | custom-call | flops 1000 | bytes 1000 | tf_op jit(solution)/shard_map/pallas_call | solution.py:686
  38.5 5.6 %collective-permute-done.4.next_ref = f32[528,128]{1,0:T(8,128)S(1)} collective-permute-done((f32[528,128]{1,0:T(8,128)S(1)}, f32[528,128]{1,0:T(8,128)S(1)}, u32[]{:S(2)}, u32[]{:S(2)}) %collective-permute-start.4) | collective-permute-done | bytes 270368 | tf_op jit(solution)/shard_map/ppermute | solution.py:685
  44.1 17.5 %all_to_all.11 = f32[64,1,2560]{2,1,0:T(1,128)S(1)} all-to-all(f32[64,1,2560]{2,1,0:T(1,128)S(1)} %bitcast.38), channel_id=1, replica_groups={{0,16,32,48,64,80,96,112,1,17,33,49,65,81,97,113,2,18,34,50,66,82,98,11..., dimensions={0} | all-to-all | bytes 1310720 | tf_op jit(solution)/shard_map/all_to_all | solution.py:627
  61.6 5.0 %shard_map.154 = (f32[19,256,128]{2,1,0:T(8,128)}, f32[768,128]{1,0:T(8,128)}) custom-call(f32[1280,128]{1,0:T(8,128)S(1)} %bitcast.39, bf16[192,128]{1,0:T(8,128)(2,1)S(1)} %copy-done.10, f32[512,128]{1,0:T(8,128)S(1)} %bitcast.37, f32[256,128]{1,0:T(8,128)S(1)} %bitcast.43, f32[768,128]{1,0:T(8,128)S(1)} %get-tuple-element.23.magnet_ref, ...), custom_call_target="tpu_custom_call" | custom-call | flops 60000000 | bytes 8000000 | tf_op jit(solution)/shard_map/pallas_call | solution.py:710
  (22 shorter events, 0.1 us)
Async XLA Ops:
  0.6 11.5 %copy-start = (f32[19,8,4096]{2,1,0:T(8,128)S(1)}, f32[19,8,4096]{2,1,0:T(8,128)}, u32[]{:S(2)}) copy-start(f32[19,8,4096]{2,1,0:T(8,128)} %param.14) | copy-start | bytes 7471108
  0.6 8.6 %copy-start.1 = (f32[2,8,4096]{2,1,0:T(8,128)S(1)}, f32[2,8,4096]{2,1,0:T(8,128)}, u32[]{:S(2)}) copy-start(f32[2,8,4096]{2,1,0:T(8,128)} %param.16) | copy-start | bytes 786436
  0.6 8.6 %copy-start.2 = (f32[8,4096]{1,0:T(8,128)S(1)}, f32[8,4096]{1,0:T(8,128)}, u32[]{:S(2)}) copy-start(f32[8,4096]{1,0:T(8,128)} %param.15) | copy-start | bytes 393220
  2.5 8.6 %collective-permute-start = (f32[96,128]{1,0:T(8,128)}, f32[96,128]{1,0:T(8,128)S(1)}, u32[]{:S(2)}, u32[]{:S(2)}) collective-permute-start(f32[96,128]{1,0:T(8,128)} %get-tuple-element.15), channel_id=1, source_target_pairs={{0,1},{1,2},{2,3},{3,4},{4,5},{5,6},{6,7},{7,0},{8,9},{9,10},{10,1... | collective-permute-start | bytes 147464 | tf_op jit(solution)/shard_map/ppermute | solution.py:619
  7.0 5.2 %collective-permute-start.1 = (f32[96,128]{1,0:T(8,128)}, f32[96,128]{1,0:T(8,128)S(1)}, u32[]{:S(2)}, u32[]{:S(2)}) collective-permute-start(f32[96,128]{1,0:T(8,128)} %get-tuple-element.16), channel_id=1, source_target_pairs={{0,7},{1,0},{2,1},{3,2},{4,3},{5,4},{6,5},{7,6},{8,15},{9,8},{10,9... | collective-permute-start | bytes 147464 | tf_op jit(solution)/shard_map/ppermute | solution.py:619
  9.3 0.8 %copy-start.11 = (bf16[64,384]{1,0:T(8,128)(2,1)S(1)}, bf16[64,384]{1,0:T(8,128)(2,1)}, u32[]{:S(2)}) copy-start(bf16[64,384]{1,0:T(8,128)(2,1)} %constant.22.clone.table_ref) | copy-start | bytes 147460
  11.0 25.6 %copy-start.3 = (bf16[768,384]{1,0:T(8,128)(2,1)S(1)}, bf16[768,384]{1,0:T(8,128)(2,1)}, u32[]{:S(2)}) copy-start(bf16[768,384]{1,0:T(8,128)(2,1)} %constant.28.clone.back_odd_ref) | copy-start | bytes 1769476
  11.0 25.6 %copy-start.4 = (bf16[768,384]{1,0:T(8,128)(2,1)S(1)}, bf16[768,384]{1,0:T(8,128)(2,1)}, u32[]{:S(2)}) copy-start(bf16[768,384]{1,0:T(8,128)(2,1)} %constant.27.clone.back_even_ref) | copy-start | bytes 1769476
  11.0 25.6 %copy-start.5 = (bf16[768,256]{1,0:T(8,128)(2,1)S(1)}, bf16[768,256]{1,0:T(8,128)(2,1)}, u32[]{:S(2)}) copy-start(bf16[768,256]{1,0:T(8,128)(2,1)} %constant.26.clone.odd_ref) | copy-start | bytes 1179652
  11.0 25.5 %copy-start.6 = (bf16[768,256]{1,0:T(8,128)(2,1)S(1)}, bf16[768,256]{1,0:T(8,128)(2,1)}, u32[]{:S(2)}) copy-start(bf16[768,256]{1,0:T(8,128)(2,1)} %constant.25.clone.even_ref) | copy-start | bytes 1179652
  11.0 25.5 %copy-start.7 = (bf16[2,128,384]{2,1,0:T(8,128)(2,1)S(1)}, bf16[2,128,384]{2,1,0:T(8,128)(2,1)}, u32[]{:S(2)}) copy-start(bf16[2,128,384]{2,1,0:T(8,128)(2,1)} %constant.23.clone.fwd_x_ref) | copy-start | bytes 589828
  11.1 25.5 %copy-start.8 = (bf16[2,96,384]{2,1,0:T(8,128)(2,1)S(1)}, bf16[2,96,384]{2,1,0:T(8,128)(2,1)}, u32[]{:S(2)}) copy-start(bf16[2,96,384]{2,1,0:T(8,128)(2,1)} %constant.24.clone.back_x_ref) | copy-start | bytes 442372
  11.1 25.5 %copy-start.9 = (f32[128,128]{1,0:T(8,128)S(1)}, f32[128,128]{1,0:T(8,128)}, u32[]{:S(2)}) copy-start(f32[128,128]{1,0:T(8,128)} %constant.29.clone.wave_x_ref) | copy-start | bytes 196612
  11.1 25.5 %copy-start.12 = (f32[64,128]{1,0:T(8,128)S(1)}, f32[64,128]{1,0:T(8,128)}, u32[]{:S(2)}) copy-start(f32[64,128]{1,0:T(8,128)} %constant.31.clone.wave_z_ref) | copy-start | bytes 98308
  11.1 25.5 %copy-start.13 = (f32[2,256]{1,0:T(2,128)S(1)}, f32[2,256]{1,0:T(2,128)}, u32[]{:S(2)}) copy-start(f32[2,256]{1,0:T(2,128)} %constant.30.clone.wave_y_ref) | copy-start | bytes 6148
  31.6 29.9 %copy-start.10 = (bf16[192,128]{1,0:T(8,128)(2,1)S(1)}, bf16[192,128]{1,0:T(8,128)(2,1)}, u32[]{:S(2)}) copy-start(bf16[192,128]{1,0:T(8,128)(2,1)} %constant.32.clone.table_ref) | copy-start | bytes 147460
  31.7 4.9 %collective-permute-start.2 = (f32[64,1536]{1,0:T(8,128)S(1)}, f32[64,1536]{1,0:T(8,128)S(1)}, u32[]{:S(2)}, u32[]{:S(2)}) collective-permute-start(f32[64,1536]{1,0:T(8,128)S(1)} %shard_map.152.own_ref), channel_id=1, source_target_pairs={{0,8},{8,0},{16,24},{24,16},{32,40},{40,32},{48,56},{56,48},{64,72... | collective-permute-start | bytes 1179656 | tf_op jit(solution)/shard_map/ppermute | solution.py:683
  35.2 3.3 %collective-permute-start.3 = (f32[528,128]{1,0:T(8,128)S(1)}, f32[528,128]{1,0:T(8,128)S(1)}, u32[]{:S(2)}, u32[]{:S(2)}) collective-permute-start(f32[528,128]{1,0:T(8,128)S(1)} %get-tuple-element.20), channel_id=1, source_target_pairs={{0,8},{8,0},{16,24},{24,16},{32,40},{40,32},{48,56},{56,48},{64,72... | collective-permute-start | bytes 811016 | tf_op jit(solution)/shard_map/ppermute | solution.py:684
  35.3 8.8 %collective-permute-start.4 = (f32[528,128]{1,0:T(8,128)S(1)}, f32[528,128]{1,0:T(8,128)S(1)}, u32[]{:S(2)}, u32[]{:S(2)}) collective-permute-start(f32[528,128]{1,0:T(8,128)S(1)} %get-tuple-element.21), channel_id=1, source_target_pairs={{0,120},{8,16},{16,8},{24,32},{32,24},{40,48},{48,40},{56,64},{64,... | collective-permute-start | bytes 811016 | tf_op jit(solution)/shard_map/ppermute | solution.py:685

commit v6 on v5

--- a/solution.py
+++ b/solution.py
@@ -34,6 +34,7 @@
 )
 WEIGHTS = (1.0 / 3.0,) + (1.0 / 18.0,) * 6 + (1.0 / 36.0,) * 12
 OMEGA = 1.0 / 0.6
+PULL = 0.05 / 2
 F32 = jnp.float32
 
 X_FACE = ((0, 0, 1, 2), (1, 0, 7, 10), (-1, 0, 9, 8), (0, 1, 11, 14), (0, -1, 13, 12))
@@ -208,7 +209,7 @@
 ):
     magnet = langevin(ht_ref[:256, :], ht_ref[256:, :], ha_ref[...])
     for c in range(3):
-        magnet_ref[c * 256 : c * 256 + 256, :] = magnet[c]
+        magnet_ref[c * 256 : c * 256 + 256, :] = PULL * magnet[c]
     parity = lax.rem(lax.axis_index("gx"), 2)
     for out_ref, up in ((pair_ref, parity == 0), (next_ref, parity == 1)):
         face = jnp.where(up, 7, 0)
@@ -465,7 +466,7 @@
             d_z = jnp.where(first, pltpu.roll(a, 127, 1), pltpu.roll(b, 127, 1)) - jnp.where(
                 first, pltpu.roll(a, 1, 1), pltpu.roll(b, 1, 1)
             )
-            force.append(0.025 * (magnet[0] * d_x + magnet[1] * d_y + magnet[2] * d_z))
+            force.append(magnet[0] * d_x + magnet[1] * d_y + magnet[2] * d_z)
         return force
 
     def column(c, x, y):
@@ -477,14 +478,14 @@
         for k in range(12)
     ]
     force = forces(
-        langevin(*values[9:]),
+        [PULL * value for value in langevin(*values[9:])],
         lambda c, dx, dy: (column(c, dx, 64 + dy), column(c, dx, dy - 1)),
         left,
     )
     vel, scaled, rest = macroscopic(values[5], values[6:9], force)
     for slot, (cx, cz, up, down) in enumerate(Y_FACE):
         even, odd = relax_terms((cx, sign, cz), vel, force, scaled, rest)
-        post = shift_z((1.0 - OMEGA) * values[slot] + WEIGHTS[up] * (even + odd), cz, lane)
+        post = (1.0 - OMEGA) * values[slot] + WEIGHTS[up] * (even + odd)
         post_ref[up, 0] = post
         post_ref[down, 33] = post
 
@@ -504,7 +505,7 @@
         return jnp.where(upper, column(c, 1 + dx, y), column(c, dx - 1, y))
 
     force = forces(
-        langevin(*[edge_rows(k, k) for k in (9, 10, 11)]),
+        [PULL * value for value in langevin(*[edge_rows(k, k) for k in (9, 10, 11)])],
         lambda c, dx, dy: (corner(c, dx, 64 + dy), corner(c, dx, dy - 1)),
         left,
     )
@@ -522,7 +523,7 @@
             )
 
         values = [side(which, k * 32, 32) for k in range(12)]
-        force = forces(langevin(*values[9:]), read, left4)
+        force = forces([PULL * value for value in langevin(*values[9:])], read, left4)
         vel, scaled, rest = macroscopic(values[5], values[6:9], force)
         at_edge = 7 * which
         lane4 = lanes((32, 128))
@@ -555,29 +556,59 @@
             lambda c, dx, dy: (column(c, dx, ya + dy), column(c, dx, ya + 1 + dy)),
             left,
         )
-        popul = [pop_ref[n, pl.ds(at, 8), :] for n in range(19)]
-        density, momentum = moments_of(popul)
+        rest_popul = pop_ref[0, pl.ds(at, 8), :]
+        sums, diffs, density = {}, {}, rest_popul
+        for n in range(1, 19, 2):
+            up, down = pop_ref[n, pl.ds(at, 8), :], pop_ref[n + 1, pl.ds(at, 8), :]
+            sums[n], diffs[n] = up + down, up - down
+            density = density + sums[n]
+        momentum = []
+        for k in range(3):
+            signs = [(VELOCITIES[n][k], diffs[n]) for n in range(1, 19, 2)]
+            total = None
+            for sign_of, value in sorted(signs, key=lambda item: -item[0]):
+                if sign_of == 1:
+                    total = value if total is None else total + value
+                elif sign_of == -1:
+                    total = total - value
+            momentum.append(total)
         vel, scaled, rest = macroscopic(density, momentum, force)
-        post_ref[0, 1 + pair] = (1.0 - OMEGA) * popul[0] + WEIGHTS[0] * rest
-        for n in range(1, 19, 2):
-            even, odd = relax_terms(VELOCITIES[n], vel, force, scaled, rest)
-            for number, value in ((n, even + odd), (n + 1, even - odd)):
-                post = (1.0 - OMEGA) * popul[number] + WEIGHTS[n] * value
-                post_ref[number, 1 + pair] = shift_z(post, VELOCITIES[number][2], lane)
+        post_ref[0, 1 + pair] = (1.0 - OMEGA) * rest_popul + WEIGHTS[0] * rest
+        half = 0.5 * (1.0 - OMEGA)
+        for first, last in ((1, 7), (7, 19)):
+            weight = WEIGHTS[first]
+            rest_w = weight * rest
+            slope, curve = (3.0 * weight) * scaled, (4.5 * weight) * scaled
+            pull = [(0.5 * weight) * value for value in force]
+            push = [(1.5 * weight) * value for value in force]
+            for n in range(first, last, 2):
+                along_u = along(VELOCITIES[n], vel)
+                even = rest_w + along_u * (curve * along_u + along(VELOCITIES[n], push))
+                odd = slope * along_u + along(VELOCITIES[n], pull)
+                even, odd = half * sums[n] + even, half * diffs[n] + odd
+                for number, post in ((n, even + odd), (n + 1, even - odd)):
+                    cz = 0 if number > 14 else VELOCITIES[number][2]
+                    post_ref[number, 1 + pair] = shift_z(post, cz, lane)
         return carry
 
-    lax.fori_loop(0, 32, collide, 0, unroll=4)
+    lax.fori_loop(0, 32, collide, 0, unroll=8)
     sent = start((demag_ref, demag_hbm, out_sems.at[4]))
 
     def stream(pair, carry):
         at = pl.multiple_of(pair * 8, 8)
         for n in range(19):
-            cx, cy, _ = VELOCITIES[n]
+            cx, cy, cz = VELOCITIES[n]
             tile = post_ref[n, 1 + pair]
             if cy == 1:
-                tile = pltpu.roll(jnp.where(left, tile, post_ref[n, pair]), 64, 1)
+                tile = jnp.where(left, tile, post_ref[n, pair])
             elif cy == -1:
-                tile = pltpu.roll(jnp.where(left, post_ref[n, 2 + pair], tile), 64, 1)
+                tile = jnp.where(left, post_ref[n, 2 + pair], tile)
+            if cy != 0 and cz == 0:
+                tile = pltpu.roll(tile, 64, 1)
+            elif cy != 0:
+                edge = lane % 64 == (0 if cz == 1 else 63)
+                near, far = (1, 65) if cz == 1 else (127, 63)
+                tile = jnp.where(edge, pltpu.roll(tile, near, 1), pltpu.roll(tile, far, 1))
             if cx != 0:
                 enters = enter_ref[0 if cx == 1 else 1, X_SLOT[n], pl.ds(pair, 1), :]
                 tile = jnp.where(

time: 67.5 us -> 67.4 us (level)
  no operation moved by 1% of the time
where the time goes in v6:
time: 67.4 us; the launch traced here: 66.5 us
  blocking collectives  36.4 us (54%)
  starting transfers between devices  10.8 us (16%)
  Pallas kernels  10 us (15%)
  waiting for transfers between devices  7.49 us (11%)
  local copies, waits for them, and re-layouts  0.88 us (1%)
  between operations  0.83 us (1%)
    all_to_all x2, blocking collectives, exchange(): lax.all_to_all(blocks, ('gx', 'gy'), 0, 0, axis_index_groups=GROUPS, tile...  36.4 us
    ppermute x2, starting transfers between devices, ring(): lax.ppermute(values, axis, [(i, (i + step) % size) for i in range(size)])  6.77 us
    ppermute x1, waiting for transfers between devices, on_device(): lax.ppermute(to_next, 'gx', [(i, (i + 1 ^ 1) - 1 & 15) for i in range(GX)])  5.59 us
    pallas_call x1, Pallas kernels, on_device(): call(cell_kernel, [VMEM] * 10, [((19, 256, 128), HBM), ((3 * 256, 128), H...  4.91 us
    ppermute x1, starting transfers between devices, on_device(): other = lax.ppermute(own, 'gx', [(i, i ^ 1) for i in range(GX)])  3.55 us
    pallas_call x1, Pallas kernels, on_device(): call(plane_kernel, [VMEM] * 11, [((64 * ROWS_BACK, 128), VMEM)], [], [],...  1.86 us
    pallas_call x1, Pallas kernels, on_device(): call(edge_kernel, [HBM] * 3, [((96, 128), VMEM), ((96, 128), VMEM)], [(2,...  1.81 us
  transfers between devices with their start and end apart: 5, of which 3 were waited for; matrix products, arithmetic and copies ran while one was open for 0% of the time, Pallas kernels for 4%

profile of v6, /device:TPU:1, one launch (start us, length us, event | category | flops | bytes accessed | tf_op | source)
XLA Modules:
  0.0 66.5 jit_solution(10108586608914213695)
XLA Ops:
  0.7 1.8 %shard_map.150 = (f32[96,128]{1,0:T(8,128)}, f32[96,128]{1,0:T(8,128)}) custom-call(f32[19,32,8,128]{3,2,1,0:T(8,128)} %bitcast.31, f32[512,128]{1,0:T(8,128)} %bitcast.34, f32[256,128]{1,0:T(8,128)} %bitcast.40), custom_call_target="tpu_custom_call" | custom-call | flops 100000 | bytes 300000 | tf_op jit(solution)/shard_map/pallas_call | solution.py:678
  2.5 4.5 %collective-permute-start = (f32[96,128]{1,0:T(8,128)}, f32[96,128]{1,0:T(8,128)S(1)}, u32[]{:S(2)}, u32[]{:S(2)}) collective-permute-start(f32[96,128]{1,0:T(8,128)} %get-tuple-element.15), channel_id=1, source_target_pairs={{0,1},{1,2},{2,3},{3,4},{4,5},{5,6},{6,7},{7,0},{8,9},{9,10},{10,1... | collective-permute-start | bytes 147464 | tf_op jit(solution)/shard_map/ppermute | solution.py:650
  7.0 2.3 %collective-permute-start.1 = (f32[96,128]{1,0:T(8,128)}, f32[96,128]{1,0:T(8,128)S(1)}, u32[]{:S(2)}, u32[]{:S(2)}) collective-permute-start(f32[96,128]{1,0:T(8,128)} %get-tuple-element.16), channel_id=1, source_target_pairs={{0,7},{1,0},{2,1},{3,2},{4,3},{5,4},{6,5},{7,6},{8,15},{9,8},{10,9... | collective-permute-start | bytes 147464 | tf_op jit(solution)/shard_map/ppermute | solution.py:650
  9.3 0.8 %copy-done.11 = bf16[64,384]{1,0:T(8,128)(2,1)S(1)} copy-done((bf16[64,384]{1,0:T(8,128)(2,1)S(1)}, bf16[64,384]{1,0:T(8,128)(2,1)}, u32[]{:S(2)}) %copy-start.11) | copy-done | bytes 49176
  10.1 0.9 %shard_map.149 = f32[768,128]{1,0:T(8,128)S(1)} custom-call(f32[512,128]{1,0:T(8,128)S(1)} %bitcast.35, f32[256,128]{1,0:T(8,128)S(1)} %bitcast.41, bf16[64,384]{1,0:T(8,128)(2,1)S(1)} %copy-done.11), custom_call_target="tpu_custom_call" | custom-call | flops 30000000 | bytes 1800000 | tf_op jit(solution)/shard_map/pallas_call | solution.py:689
  11.0 0.0 copy-start.3
  11.0 0.0 copy-start.4
  11.0 0.0 copy-start.5
  11.0 0.0 copy-start.6
  11.0 0.0 copy-start.7
  11.1 0.0 copy-start.8
  11.1 0.0 copy-start.12
  11.1 1.0 %collective-permute-done.1.after_ref = f32[96,128]{1,0:T(8,128)S(1)} collective-permute-done((f32[96,128]{1,0:T(8,128)}, f32[96,128]{1,0:T(8,128)S(1)}, u32[]{:S(2)}, u32[]{:S(2)}) %collective-permute-start.1) | collective-permute-done | bytes 49184 | tf_op jit(solution)/shard_map/ppermute | solution.py:650
  12.2 0.4 shard_map.151
  12.5 19.0 %all_to_all.10 = f32[64,1,1536]{2,1,0:T(1,128)S(1)} all-to-all(f32[64,1,1536]{2,1,0:T(1,128)S(1)} %bitcast.44), channel_id=1, replica_groups={{0,16,32,48,64,80,96,112,1,17,33,49,65,81,97,113,2,18,34,50,66,82,98,11..., dimensions={0} | all-to-all | bytes 786432 | tf_op jit(solution)/shard_map/all_to_all | solution.py:658
  31.5 0.2 shard_map.152.own_ref
  31.7 3.5 %collective-permute-start.2 = (f32[64,1536]{1,0:T(8,128)S(1)}, f32[64,1536]{1,0:T(8,128)S(1)}, u32[]{:S(2)}, u32[]{:S(2)}) collective-permute-start(f32[64,1536]{1,0:T(8,128)S(1)} %shard_map.152.own_ref), channel_id=1, source_target_pairs={{0,8},{8,0},{16,24},{24,16},{32,40},{40,32},{48,56},{56,48},{64,72... | collective-permute-start | bytes 1179656 | tf_op jit(solution)/shard_map/ppermute | solution.py:714
  35.2 0.1 collective-permute-start.3
  35.3 0.4 collective-permute-start.4
  35.7 0.9 %collective-permute-done.2.other_ref = f32[64,1536]{1,0:T(8,128)S(1)} collective-permute-done((f32[64,1536]{1,0:T(8,128)S(1)}, f32[64,1536]{1,0:T(8,128)S(1)}, u32[]{:S(2)}, u32[]{:S(2)}) %collective-permute-start.2) | collective-permute-done | bytes 393248 | tf_op jit(solution)/shard_map/ppermute | solution.py:714
  36.6 1.9 %shard_map.153 = f32[1280,128]{1,0:T(8,128)S(1)} custom-call(f32[64,1536]{1,0:T(8,128)S(1)} %shard_map.152.own_ref, f32[64,1536]{1,0:T(8,128)S(1)} %collective-permute-done.2.other_ref, bf16[2,128,384]{2,1,0:T(8,128)(2,1)S(1)} %copy-done.7, bf16[2,96,384]{2,1,0:T(8,128)(2,1)S(1)} %copy-done.8, bf16[768,256]{1,0:T(8,128)(2,1)S(1)} %copy-done.6, ...), custom_call_target="tpu_custom_call" | custom-call | flops 1000 | bytes 1000 | tf_op jit(solution)/shard_map/pallas_call | solution.py:717
  38.5 5.6 %collective-permute-done.4.next_ref = f32[528,128]{1,0:T(8,128)S(1)} collective-permute-done((f32[528,128]{1,0:T(8,128)S(1)}, f32[528,128]{1,0:T(8,128)S(1)}, u32[]{:S(2)}, u32[]{:S(2)}) %collective-permute-start.4) | collective-permute-done | bytes 270368 | tf_op jit(solution)/shard_map/ppermute | solution.py:716
  44.1 17.5 %all_to_all.11 = f32[64,1,2560]{2,1,0:T(1,128)S(1)} all-to-all(f32[64,1,2560]{2,1,0:T(1,128)S(1)} %bitcast.38), channel_id=1, replica_groups={{0,16,32,48,64,80,96,112,1,17,33,49,65,81,97,113,2,18,34,50,66,82,98,11..., dimensions={0} | all-to-all | bytes 1310720 | tf_op jit(solution)/shard_map/all_to_all | solution.py:658
  61.6 4.9 %shard_map.154 = (f32[19,256,128]{2,1,0:T(8,128)}, f32[768,128]{1,0:T(8,128)}) custom-call(f32[1280,128]{1,0:T(8,128)S(1)} %bitcast.39, bf16[192,128]{1,0:T(8,128)(2,1)S(1)} %copy-done.10, f32[512,128]{1,0:T(8,128)S(1)} %bitcast.37, f32[256,128]{1,0:T(8,128)S(1)} %bitcast.43, f32[768,128]{1,0:T(8,128)S(1)} %get-tuple-element.23.magnet_ref, ...), custom_call_target="tpu_custom_call" | custom-call | flops 60000000 | bytes 8000000 | tf_op jit(solution)/shard_map/pallas_call | solution.py:741
  (22 shorter events, 0.1 us)
Async XLA Ops:
  0.6 11.5 %copy-start = (f32[19,8,4096]{2,1,0:T(8,128)S(1)}, f32[19,8,4096]{2,1,0:T(8,128)}, u32[]{:S(2)}) copy-start(f32[19,8,4096]{2,1,0:T(8,128)} %param.14) | copy-start | bytes 7471108
  0.6 8.6 %copy-start.1 = (f32[2,8,4096]{2,1,0:T(8,128)S(1)}, f32[2,8,4096]{2,1,0:T(8,128)}, u32[]{:S(2)}) copy-start(f32[2,8,4096]{2,1,0:T(8,128)} %param.16) | copy-start | bytes 786436
  0.6 8.6 %copy-start.2 = (f32[8,4096]{1,0:T(8,128)S(1)}, f32[8,4096]{1,0:T(8,128)}, u32[]{:S(2)}) copy-start(f32[8,4096]{1,0:T(8,128)} %param.15) | copy-start | bytes 393220
  2.5 8.6 %collective-permute-start = (f32[96,128]{1,0:T(8,128)}, f32[96,128]{1,0:T(8,128)S(1)}, u32[]{:S(2)}, u32[]{:S(2)}) collective-permute-start(f32[96,128]{1,0:T(8,128)} %get-tuple-element.15), channel_id=1, source_target_pairs={{0,1},{1,2},{2,3},{3,4},{4,5},{5,6},{6,7},{7,0},{8,9},{9,10},{10,1... | collective-permute-start | bytes 147464 | tf_op jit(solution)/shard_map/ppermute | solution.py:650
  7.0 5.2 %collective-permute-start.1 = (f32[96,128]{1,0:T(8,128)}, f32[96,128]{1,0:T(8,128)S(1)}, u32[]{:S(2)}, u32[]{:S(2)}) collective-permute-start(f32[96,128]{1,0:T(8,128)} %get-tuple-element.16), channel_id=1, source_target_pairs={{0,7},{1,0},{2,1},{3,2},{4,3},{5,4},{6,5},{7,6},{8,15},{9,8},{10,9... | collective-permute-start | bytes 147464 | tf_op jit(solution)/shard_map/ppermute | solution.py:650
  9.3 0.8 %copy-start.11 = (bf16[64,384]{1,0:T(8,128)(2,1)S(1)}, bf16[64,384]{1,0:T(8,128)(2,1)}, u32[]{:S(2)}) copy-start(bf16[64,384]{1,0:T(8,128)(2,1)} %constant.22.clone.table_ref) | copy-start | bytes 147460
  11.0 25.6 %copy-start.3 = (bf16[768,384]{1,0:T(8,128)(2,1)S(1)}, bf16[768,384]{1,0:T(8,128)(2,1)}, u32[]{:S(2)}) copy-start(bf16[768,384]{1,0:T(8,128)(2,1)} %constant.28.clone.back_odd_ref) | copy-start | bytes 1769476
  11.0 25.6 %copy-start.4 = (bf16[768,384]{1,0:T(8,128)(2,1)S(1)}, bf16[768,384]{1,0:T(8,128)(2,1)}, u32[]{:S(2)}) copy-start(bf16[768,384]{1,0:T(8,128)(2,1)} %constant.27.clone.back_even_ref) | copy-start | bytes 1769476
  11.0 25.6 %copy-start.5 = (bf16[768,256]{1,0:T(8,128)(2,1)S(1)}, bf16[768,256]{1,0:T(8,128)(2,1)}, u32[]{:S(2)}) copy-start(bf16[768,256]{1,0:T(8,128)(2,1)} %constant.26.clone.odd_ref) | copy-start | bytes 1179652
  11.0 25.5 %copy-start.6 = (bf16[768,256]{1,0:T(8,128)(2,1)S(1)}, bf16[768,256]{1,0:T(8,128)(2,1)}, u32[]{:S(2)}) copy-start(bf16[768,256]{1,0:T(8,128)(2,1)} %constant.25.clone.even_ref) | copy-start | bytes 1179652
  11.0 25.5 %copy-start.7 = (bf16[2,128,384]{2,1,0:T(8,128)(2,1)S(1)}, bf16[2,128,384]{2,1,0:T(8,128)(2,1)}, u32[]{:S(2)}) copy-start(bf16[2,128,384]{2,1,0:T(8,128)(2,1)} %constant.23.clone.fwd_x_ref) | copy-start | bytes 589828
  11.1 25.5 %copy-start.8 = (bf16[2,96,384]{2,1,0:T(8,128)(2,1)S(1)}, bf16[2,96,384]{2,1,0:T(8,128)(2,1)}, u32[]{:S(2)}) copy-start(bf16[2,96,384]{2,1,0:T(8,128)(2,1)} %constant.24.clone.back_x_ref) | copy-start | bytes 442372
  11.1 25.5 %copy-start.9 = (f32[128,128]{1,0:T(8,128)S(1)}, f32[128,128]{1,0:T(8,128)}, u32[]{:S(2)}) copy-start(f32[128,128]{1,0:T(8,128)} %constant.29.clone.wave_x_ref) | copy-start | bytes 196612
  11.1 25.5 %copy-start.12 = (f32[64,128]{1,0:T(8,128)S(1)}, f32[64,128]{1,0:T(8,128)}, u32[]{:S(2)}) copy-start(f32[64,128]{1,0:T(8,128)} %constant.31.clone.wave_z_ref) | copy-start | bytes 98308
  11.1 25.5 %copy-start.13 = (f32[2,256]{1,0:T(2,128)S(1)}, f32[2,256]{1,0:T(2,128)}, u32[]{:S(2)}) copy-start(f32[2,256]{1,0:T(2,128)} %constant.30.clone.wave_y_ref) | copy-start | bytes 6148
  31.7 29.9 %copy-start.10 = (bf16[192,128]{1,0:T(8,128)(2,1)S(1)}, bf16[192,128]{1,0:T(8,128)(2,1)}, u32[]{:S(2)}) copy-start(bf16[192,128]{1,0:T(8,128)(2,1)} %constant.32.clone.table_ref) | copy-start | bytes 147460
  31.7 4.9 %collective-permute-start.2 = (f32[64,1536]{1,0:T(8,128)S(1)}, f32[64,1536]{1,0:T(8,128)S(1)}, u32[]{:S(2)}, u32[]{:S(2)}) collective-permute-start(f32[64,1536]{1,0:T(8,128)S(1)} %shard_map.152.own_ref), channel_id=1, source_target_pairs={{0,8},{8,0},{16,24},{24,16},{32,40},{40,32},{48,56},{56,48},{64,72... | collective-permute-start | bytes 1179656 | tf_op jit(solution)/shard_map/ppermute | solution.py:714
  35.2 3.3 %collective-permute-start.3 = (f32[528,128]{1,0:T(8,128)S(1)}, f32[528,128]{1,0:T(8,128)S(1)}, u32[]{:S(2)}, u32[]{:S(2)}) collective-permute-start(f32[528,128]{1,0:T(8,128)S(1)} %get-tuple-element.20), channel_id=1, source_target_pairs={{0,8},{8,0},{16,24},{24,16},{32,40},{40,32},{48,56},{56,48},{64,72... | collective-permute-start | bytes 811016 | tf_op jit(solution)/shard_map/ppermute | solution.py:715
  35.3 8.8 %collective-permute-start.4 = (f32[528,128]{1,0:T(8,128)S(1)}, f32[528,128]{1,0:T(8,128)S(1)}, u32[]{:S(2)}, u32[]{:S(2)}) collective-permute-start(f32[528,128]{1,0:T(8,128)S(1)} %get-tuple-element.21), channel_id=1, source_target_pairs={{0,120},{8,16},{16,8},{24,32},{32,24},{40,48},{48,40},{56,64},{64,... | collective-permute-start | bytes 811016 | tf_op jit(solution)/shard_map/ppermute | solution.py:716

commit v7 on v6

--- a/solution.py
+++ b/solution.py
@@ -44,7 +44,7 @@
 ROWS_FWD = 12
 ROWS_BACK = 20
 CORNER = 480
-FACE_ROWS = CORNER + 48
+FACE_ROWS = CORNER + 32
 PITCH = 69
 OWN_PITCH = 65
 
@@ -225,11 +225,10 @@
             lines += [line(ht_ref, x), line(ht_ref, 256 + x), line(ha_ref, x)]
         for k, value in enumerate(lines):
             out_ref[k * 32 : k * 32 + 32, :] = value
-        for ref, at in ((before_ref, CORNER), (after_ref, CORNER + 16)):
-            out_ref[at : at + 16, :] = jnp.zeros((16, 128), F32)
+        out_ref[CORNER + 24 : CORNER + 32, :] = jnp.zeros((8, 128), F32)
+        for ref, at in ((before_ref, CORNER), (after_ref, CORNER + 12)):
             out_ref[at : at + 12, :] = ref[pl.ds(face, 12, stride=8), :]
-        for ref, at in ((before_ref, CORNER + 32), (after_ref, CORNER + 40)):
-            out_ref[at : at + 8, :] = jnp.zeros((8, 128), F32)
+        for ref, at in ((before_ref, CORNER + 24), (after_ref, CORNER + 27)):
             out_ref[at : at + 3, :] = ref[pl.ds(72 + second, 3, stride=8), :]
 
 
@@ -427,10 +426,10 @@
             for odd, tile in enumerate(both(edge_ref[72 + c * 8 : 80 + c * 8, :])):
                 total_ref[pl.ds(base(c, 0) + y + odd, 8, stride=PITCH), :] = tile
         for which, near, far in ((0, -1, -2), (1, 8, 9)):
-            for x, k, corner in ((near, 9 + c, 9 + c), (far, 12 + c, 32 + c)):
+            for x, k, corner in ((near, 9 + c, 9 + c), (far, 12 + c, 24 + c)):
                 for odd, tile in enumerate(both(side(which, k * 32, 32))):
                     total_ref[pl.ds(base(c, x) + odd, 32, stride=2), :] = tile
-                after = 16 if x == near else 8
+                after = 12 if x == near else 3
                 for y, at in ((-2, CORNER + corner), (64, CORNER + corner + after)):
                     for odd, tile in enumerate(both(side(which, at, 1))):
                         at_row = base(c, x) + y + odd
@@ -496,7 +495,7 @@
         pair = []
         for which, k in ((0, k_low), (1, k_high)):
             value = jnp.where(
-                left[:1], side(which, CORNER + 16 + k, 1), side(which, CORNER + k, 1)
+                left[:1], side(which, CORNER + 12 + k, 1), side(which, CORNER + k, 1)
             )
             pair.append(jnp.broadcast_to(value, (8, 128)))
         return jnp.where(upper, pair[1], pair[0])

time: 67.4 us -> 67.2 us (level)
  no operation moved by 1% of the time
where the time goes in v7:
time: 67.2 us; the launch traced here: 66.3 us
  blocking collectives  36.4 us (54%)
  starting transfers between devices  10.8 us (16%)
  Pallas kernels  10 us (15%)
  waiting for transfers between devices  7.31 us (11%)
  local copies, waits for them, and re-layouts  0.88 us (1%)
  between operations  0.83 us (1%)
    all_to_all x2, blocking collectives, exchange(): lax.all_to_all(blocks, ('gx', 'gy'), 0, 0, axis_index_groups=GROUPS, tile...  36.4 us
    ppermute x2, starting transfers between devices, ring(): lax.ppermute(values, axis, [(i, (i + step) % size) for i in range(size)])  6.77 us
    ppermute x1, waiting for transfers between devices, on_device(): lax.ppermute(to_next, 'gx', [(i, (i + 1 ^ 1) - 1 & 15) for i in range(GX)])  5.41 us
    pallas_call x1, Pallas kernels, on_device(): call(cell_kernel, [VMEM] * 10, [((19, 256, 128), HBM), ((3 * 256, 128), H...  4.9 us
    ppermute x1, starting transfers between devices, on_device(): other = lax.ppermute(own, 'gx', [(i, i ^ 1) for i in range(GX)])  3.55 us
    pallas_call x1, Pallas kernels, on_device(): call(plane_kernel, [VMEM] * 11, [((64 * ROWS_BACK, 128), VMEM)], [], [],...  1.86 us
    pallas_call x1, Pallas kernels, on_device(): call(edge_kernel, [HBM] * 3, [((96, 128), VMEM), ((96, 128), VMEM)], [(2,...  1.81 us
  transfers between devices with their start and end apart: 5, of which 3 were waited for; matrix products, arithmetic and copies ran while one was open for 0% of the time, Pallas kernels for 4%

profile of v7, /device:TPU:1, one launch (start us, length us, event | category | flops | bytes accessed | tf_op | source)
XLA Modules:
  0.0 66.3 jit_solution(3460093954257362952)
XLA Ops:
  0.7 1.8 %shard_map.150 = (f32[96,128]{1,0:T(8,128)}, f32[96,128]{1,0:T(8,128)}) custom-call(f32[19,32,8,128]{3,2,1,0:T(8,128)} %bitcast.31, f32[512,128]{1,0:T(8,128)} %bitcast.34, f32[256,128]{1,0:T(8,128)} %bitcast.40), custom_call_target="tpu_custom_call" | custom-call | flops 100000 | bytes 300000 | tf_op jit(solution)/shard_map/pallas_call | solution.py:677
  2.5 4.5 %collective-permute-start = (f32[96,128]{1,0:T(8,128)}, f32[96,128]{1,0:T(8,128)S(1)}, u32[]{:S(2)}, u32[]{:S(2)}) collective-permute-start(f32[96,128]{1,0:T(8,128)} %get-tuple-element.15), channel_id=1, source_target_pairs={{0,1},{1,2},{2,3},{3,4},{4,5},{5,6},{6,7},{7,0},{8,9},{9,10},{10,1... | collective-permute-start | bytes 147464 | tf_op jit(solution)/shard_map/ppermute | solution.py:649
  7.0 2.3 %collective-permute-start.1 = (f32[96,128]{1,0:T(8,128)}, f32[96,128]{1,0:T(8,128)S(1)}, u32[]{:S(2)}, u32[]{:S(2)}) collective-permute-start(f32[96,128]{1,0:T(8,128)} %get-tuple-element.16), channel_id=1, source_target_pairs={{0,7},{1,0},{2,1},{3,2},{4,3},{5,4},{6,5},{7,6},{8,15},{9,8},{10,9... | collective-permute-start | bytes 147464 | tf_op jit(solution)/shard_map/ppermute | solution.py:649
  9.3 0.8 %copy-done.11 = bf16[64,384]{1,0:T(8,128)(2,1)S(1)} copy-done((bf16[64,384]{1,0:T(8,128)(2,1)S(1)}, bf16[64,384]{1,0:T(8,128)(2,1)}, u32[]{:S(2)}) %copy-start.11) | copy-done | bytes 49176
  10.1 0.9 %shard_map.149 = f32[768,128]{1,0:T(8,128)S(1)} custom-call(f32[512,128]{1,0:T(8,128)S(1)} %bitcast.35, f32[256,128]{1,0:T(8,128)S(1)} %bitcast.41, bf16[64,384]{1,0:T(8,128)(2,1)S(1)} %copy-done.11), custom_call_target="tpu_custom_call" | custom-call | flops 30000000 | bytes 1800000 | tf_op jit(solution)/shard_map/pallas_call | solution.py:688
  11.0 0.0 copy-start.3
  11.0 0.0 copy-start.5
  11.0 0.0 copy-start.6
  11.0 0.0 copy-start.7
  11.1 0.0 copy-start.8
  11.1 0.0 copy-start.12
  11.1 0.0 copy-start.13
  11.1 1.0 %collective-permute-done.1.after_ref = f32[96,128]{1,0:T(8,128)S(1)} collective-permute-done((f32[96,128]{1,0:T(8,128)}, f32[96,128]{1,0:T(8,128)S(1)}, u32[]{:S(2)}, u32[]{:S(2)}) %collective-permute-start.1) | collective-permute-done | bytes 49184 | tf_op jit(solution)/shard_map/ppermute | solution.py:649
  12.2 0.4 shard_map.151
  12.5 19.0 %all_to_all.10 = f32[64,1,1536]{2,1,0:T(1,128)S(1)} all-to-all(f32[64,1,1536]{2,1,0:T(1,128)S(1)} %bitcast.44), channel_id=1, replica_groups={{0,16,32,48,64,80,96,112,1,17,33,49,65,81,97,113,2,18,34,50,66,82,98,11..., dimensions={0} | all-to-all | bytes 786432 | tf_op jit(solution)/shard_map/all_to_all | solution.py:657
  31.5 0.2 shard_map.152.own_ref
  31.7 3.5 %collective-permute-start.2 = (f32[64,1536]{1,0:T(8,128)S(1)}, f32[64,1536]{1,0:T(8,128)S(1)}, u32[]{:S(2)}, u32[]{:S(2)}) collective-permute-start(f32[64,1536]{1,0:T(8,128)S(1)} %shard_map.152.own_ref), channel_id=1, source_target_pairs={{0,8},{8,0},{16,24},{24,16},{32,40},{40,32},{48,56},{56,48},{64,72... | collective-permute-start | bytes 1179656 | tf_op jit(solution)/shard_map/ppermute | solution.py:713
  35.2 0.1 collective-permute-start.3
  35.3 0.4 collective-permute-start.4
  35.7 0.9 %collective-permute-done.2.other_ref = f32[64,1536]{1,0:T(8,128)S(1)} collective-permute-done((f32[64,1536]{1,0:T(8,128)S(1)}, f32[64,1536]{1,0:T(8,128)S(1)}, u32[]{:S(2)}, u32[]{:S(2)}) %collective-permute-start.2) | collective-permute-done | bytes 393248 | tf_op jit(solution)/shard_map/ppermute | solution.py:713
  36.6 1.9 %shard_map.153 = f32[1280,128]{1,0:T(8,128)S(1)} custom-call(f32[64,1536]{1,0:T(8,128)S(1)} %shard_map.152.own_ref, f32[64,1536]{1,0:T(8,128)S(1)} %collective-permute-done.2.other_ref, bf16[2,128,384]{2,1,0:T(8,128)(2,1)S(1)} %copy-done.7, bf16[2,96,384]{2,1,0:T(8,128)(2,1)S(1)} %copy-done.8, bf16[768,256]{1,0:T(8,128)(2,1)S(1)} %copy-done.6, ...), custom_call_target="tpu_custom_call" | custom-call | flops 1000 | bytes 1000 | tf_op jit(solution)/shard_map/pallas_call | solution.py:716
  38.5 5.4 %collective-permute-done.4.next_ref = f32[512,128]{1,0:T(8,128)S(1)} collective-permute-done((f32[512,128]{1,0:T(8,128)S(1)}, f32[512,128]{1,0:T(8,128)S(1)}, u32[]{:S(2)}, u32[]{:S(2)}) %collective-permute-start.4) | collective-permute-done | bytes 262176 | tf_op jit(solution)/shard_map/ppermute | solution.py:715
  43.9 17.5 %all_to_all.11 = f32[64,1,2560]{2,1,0:T(1,128)S(1)} all-to-all(f32[64,1,2560]{2,1,0:T(1,128)S(1)} %bitcast.38), channel_id=1, replica_groups={{0,16,32,48,64,80,96,112,1,17,33,49,65,81,97,113,2,18,34,50,66,82,98,11..., dimensions={0} | all-to-all | bytes 1310720 | tf_op jit(solution)/shard_map/all_to_all | solution.py:657
  61.4 4.9 %shard_map.154 = (f32[19,256,128]{2,1,0:T(8,128)}, f32[768,128]{1,0:T(8,128)}) custom-call(f32[1280,128]{1,0:T(8,128)S(1)} %bitcast.39, bf16[192,128]{1,0:T(8,128)(2,1)S(1)} %copy-done.10, f32[512,128]{1,0:T(8,128)S(1)} %bitcast.37, f32[256,128]{1,0:T(8,128)S(1)} %bitcast.43, f32[768,128]{1,0:T(8,128)S(1)} %get-tuple-element.23.magnet_ref, ...), custom_call_target="tpu_custom_call" | custom-call | flops 60000000 | bytes 8000000 | tf_op jit(solution)/shard_map/pallas_call | solution.py:740
  (22 shorter events, 0.1 us)
Async XLA Ops:
  0.6 11.5 %copy-start = (f32[19,8,4096]{2,1,0:T(8,128)S(1)}, f32[19,8,4096]{2,1,0:T(8,128)}, u32[]{:S(2)}) copy-start(f32[19,8,4096]{2,1,0:T(8,128)} %param.14) | copy-start | bytes 7471108
  0.6 8.6 %copy-start.1 = (f32[2,8,4096]{2,1,0:T(8,128)S(1)}, f32[2,8,4096]{2,1,0:T(8,128)}, u32[]{:S(2)}) copy-start(f32[2,8,4096]{2,1,0:T(8,128)} %param.16) | copy-start | bytes 786436
  0.6 8.6 %copy-start.2 = (f32[8,4096]{1,0:T(8,128)S(1)}, f32[8,4096]{1,0:T(8,128)}, u32[]{:S(2)}) copy-start(f32[8,4096]{1,0:T(8,128)} %param.15) | copy-start | bytes 393220
  2.5 8.6 %collective-permute-start = (f32[96,128]{1,0:T(8,128)}, f32[96,128]{1,0:T(8,128)S(1)}, u32[]{:S(2)}, u32[]{:S(2)}) collective-permute-start(f32[96,128]{1,0:T(8,128)} %get-tuple-element.15), channel_id=1, source_target_pairs={{0,1},{1,2},{2,3},{3,4},{4,5},{5,6},{6,7},{7,0},{8,9},{9,10},{10,1... | collective-permute-start | bytes 147464 | tf_op jit(solution)/shard_map/ppermute | solution.py:649
  7.0 5.2 %collective-permute-start.1 = (f32[96,128]{1,0:T(8,128)}, f32[96,128]{1,0:T(8,128)S(1)}, u32[]{:S(2)}, u32[]{:S(2)}) collective-permute-start(f32[96,128]{1,0:T(8,128)} %get-tuple-element.16), channel_id=1, source_target_pairs={{0,7},{1,0},{2,1},{3,2},{4,3},{5,4},{6,5},{7,6},{8,15},{9,8},{10,9... | collective-permute-start | bytes 147464 | tf_op jit(solution)/shard_map/ppermute | solution.py:649
  9.3 0.8 %copy-start.11 = (bf16[64,384]{1,0:T(8,128)(2,1)S(1)}, bf16[64,384]{1,0:T(8,128)(2,1)}, u32[]{:S(2)}) copy-start(bf16[64,384]{1,0:T(8,128)(2,1)} %constant.22.clone.table_ref) | copy-start | bytes 147460
  11.0 25.6 %copy-start.3 = (bf16[768,384]{1,0:T(8,128)(2,1)S(1)}, bf16[768,384]{1,0:T(8,128)(2,1)}, u32[]{:S(2)}) copy-start(bf16[768,384]{1,0:T(8,128)(2,1)} %constant.28.clone.back_odd_ref) | copy-start | bytes 1769476
  11.0 25.6 %copy-start.4 = (bf16[768,384]{1,0:T(8,128)(2,1)S(1)}, bf16[768,384]{1,0:T(8,128)(2,1)}, u32[]{:S(2)}) copy-start(bf16[768,384]{1,0:T(8,128)(2,1)} %constant.27.clone.back_even_ref) | copy-start | bytes 1769476
  11.0 25.6 %copy-start.5 = (bf16[768,256]{1,0:T(8,128)(2,1)S(1)}, bf16[768,256]{1,0:T(8,128)(2,1)}, u32[]{:S(2)}) copy-start(bf16[768,256]{1,0:T(8,128)(2,1)} %constant.26.clone.odd_ref) | copy-start | bytes 1179652
  11.0 25.5 %copy-start.6 = (bf16[768,256]{1,0:T(8,128)(2,1)S(1)}, bf16[768,256]{1,0:T(8,128)(2,1)}, u32[]{:S(2)}) copy-start(bf16[768,256]{1,0:T(8,128)(2,1)} %constant.25.clone.even_ref) | copy-start | bytes 1179652
  11.0 25.5 %copy-start.7 = (bf16[2,128,384]{2,1,0:T(8,128)(2,1)S(1)}, bf16[2,128,384]{2,1,0:T(8,128)(2,1)}, u32[]{:S(2)}) copy-start(bf16[2,128,384]{2,1,0:T(8,128)(2,1)} %constant.23.clone.fwd_x_ref) | copy-start | bytes 589828
  11.1 25.5 %copy-start.8 = (bf16[2,96,384]{2,1,0:T(8,128)(2,1)S(1)}, bf16[2,96,384]{2,1,0:T(8,128)(2,1)}, u32[]{:S(2)}) copy-start(bf16[2,96,384]{2,1,0:T(8,128)(2,1)} %constant.24.clone.back_x_ref) | copy-start | bytes 442372
  11.1 25.5 %copy-start.9 = (f32[128,128]{1,0:T(8,128)S(1)}, f32[128,128]{1,0:T(8,128)}, u32[]{:S(2)}) copy-start(f32[128,128]{1,0:T(8,128)} %constant.29.clone.wave_x_ref) | copy-start | bytes 196612
  11.1 25.5 %copy-start.12 = (f32[64,128]{1,0:T(8,128)S(1)}, f32[64,128]{1,0:T(8,128)}, u32[]{:S(2)}) copy-start(f32[64,128]{1,0:T(8,128)} %constant.31.clone.wave_z_ref) | copy-start | bytes 98308
  11.1 25.5 %copy-start.13 = (f32[2,256]{1,0:T(2,128)S(1)}, f32[2,256]{1,0:T(2,128)}, u32[]{:S(2)}) copy-start(f32[2,256]{1,0:T(2,128)} %constant.30.clone.wave_y_ref) | copy-start | bytes 6148
  31.7 29.7 %copy-start.10 = (bf16[192,128]{1,0:T(8,128)(2,1)S(1)}, bf16[192,128]{1,0:T(8,128)(2,1)}, u32[]{:S(2)}) copy-start(bf16[192,128]{1,0:T(8,128)(2,1)} %constant.32.clone.table_ref) | copy-start | bytes 147460
  31.7 4.9 %collective-permute-start.2 = (f32[64,1536]{1,0:T(8,128)S(1)}, f32[64,1536]{1,0:T(8,128)S(1)}, u32[]{:S(2)}, u32[]{:S(2)}) collective-permute-start(f32[64,1536]{1,0:T(8,128)S(1)} %shard_map.152.own_ref), channel_id=1, source_target_pairs={{0,8},{8,0},{16,24},{24,16},{32,40},{40,32},{48,56},{56,48},{64,72... | collective-permute-start | bytes 1179656 | tf_op jit(solution)/shard_map/ppermute | solution.py:713
  35.2 3.3 %collective-permute-start.3 = (f32[512,128]{1,0:T(8,128)S(1)}, f32[512,128]{1,0:T(8,128)S(1)}, u32[]{:S(2)}, u32[]{:S(2)}) collective-permute-start(f32[512,128]{1,0:T(8,128)S(1)} %get-tuple-element.20), channel_id=1, source_target_pairs={{0,8},{8,0},{16,24},{24,16},{32,40},{40,32},{48,56},{56,48},{64,72... | collective-permute-start | bytes 786440 | tf_op jit(solution)/shard_map/ppermute | solution.py:714
  35.3 8.6 %collective-permute-start.4 = (f32[512,128]{1,0:T(8,128)S(1)}, f32[512,128]{1,0:T(8,128)S(1)}, u32[]{:S(2)}, u32[]{:S(2)}) collective-permute-start(f32[512,128]{1,0:T(8,128)S(1)} %get-tuple-element.21), channel_id=1, source_target_pairs={{0,120},{8,16},{16,8},{24,32},{32,24},{40,48},{48,40},{56,64},{64,... | collective-permute-start | bytes 786440 | tf_op jit(solution)/shard_map/ppermute | solution.py:715
